TPU v7x, 32 devices: a whole 2x2x4 slice. The times are simulated.
32 devices in a mesh: ctx: 16 (over z, y, core), seq: 2 (over x).
Axes of the slice: x: 2, y: 2, z: 4, core: 2. Of those that a mesh axis runs over, the one named last changes fastest.
Arguments:
- inputs: bfloat16 [4, 8192, 768], P('seq', 'ctx'), may hold values from -6 to 6
- out_grad: bfloat16 [4, 8192, 768], P('seq', 'ctx'), may hold values from -6 to 6
- segments: int32 [4, 8192], P('seq'), may hold values from 0 to 15, never falling along the last dimension, each value on 1 to 2048 neighbouring positions
- windows: int32 [12], replicated, may hold values from 256 to 1024, as said below
- owners: int32 [16], replicated, may hold values from 0 to 1, as said below
- weights: float32 [18, 768, 768], P('seq', 'ctx'), as said below
- first_moments: float32 [18, 768, 768], P('seq', 'ctx'), may hold values from -543.058 to 543.058
- second_moments: float32 [18, 768, 768], P('seq', 'ctx'), may hold values from 1966.08 to 32768
- norm_params: float32 [4, 768], replicated
- norm_first: float32 [4, 768], replicated, may hold values from -543.058 to 543.058
- norm_second: float32 [4, 768], replicated, may hold values from 1966.08 to 32768
Outputs:
- output: bfloat16 [4, 8192, 768], P('seq', 'ctx')
- input_grad: float32 [4, 8192, 768], P('seq', 'ctx')
- weight_grads: float32 [18, 768, 768], P('seq', 'ctx')
- norm_grads: float32 [4, 768], replicated
- new_weights: float32 [18, 768, 768], P('seq', 'ctx')
- new_first: float32 [18, 768, 768], P('seq', 'ctx')
- new_second: float32 [18, 768, 768], P('seq', 'ctx')
- weights_low: bfloat16 [18, 768, 768], P('seq', 'ctx')
- new_norms: float32 [4, 768], replicated
- new_norm_first: float32 [4, 768], replicated
- new_norm_second: float32 [4, 768], replicated
- factors: float32 [12], replicated
Inputs may be any that keep to these rules, and one draw needn't show every extreme that they name: `segments`: segment numbers never fall along a sequence; a document holds at most a quarter of 8192 tokens. `windows`: some head has a window of exactly 1024. `owners`: each index of seq owns 1 to 9 units, and some index owns exactly 9. `weights`: slots that no unit occupies hold values that no output reads.
All inputs are finite; a program needn't handle non-finite values.
Results may differ from a plain program's by a relative error of at most 0.024.
Values may be sent and summed in bfloat16 or wider, within the bound.
No kernel may reach another device: no remote copies, remote signals or barrier semaphores. Data moves between devices by JAX's collectives and lax.ppermute only.
A program may use at most 320 MiB of HBM per device.

v0:
```python
import jax
import jax.numpy as jnp
from jax import lax
from jax.sharding import PartitionSpec as P

D = 768
FF = 3072
WIN = 1024
STEP = 3


clip_level = 1.0
decay_rate = 0.1
norm_rate = 0.25


def shifted(value, axis, by):
    peers = lax.axis_size(axis)
    pairs = [(i, i + by) for i in range(peers) if 0 <= i + by < peers]
    return lax.ppermute(value, axis, pairs)


def layer_norm(rows_in, gain, bias):
    center = rows_in - jnp.mean(rows_in, axis=-1, keepdims=True)
    spread = jnp.mean(center * center, axis=-1, keepdims=True)
    return center * lax.rsqrt(spread + 1e-05) * gain + bias


def glu_product(gates, linear):
    return jax.nn.gelu(gates, approximate=False) * linear


def slot_maps(owners, slots, owner_count):
    unit_ids = jnp.arange(owners.shape[0], dtype=jnp.int32)
    same_owner = owners[None, :] == owners[:, None]
    earlier = unit_ids[None, :] < unit_ids[:, None]
    rank = jnp.sum((same_owner & earlier).astype(jnp.int32), axis=1)
    index = owners * slots + rank
    slot_ids = jnp.arange(owner_count * slots, dtype=jnp.int32)
    match = index[None, :] == slot_ids[:, None]
    inverse = jnp.sum(jnp.where(match, unit_ids[None, :], 0), axis=1)
    live = jnp.any(match, axis=1)
    return (index, inverse, live)


def contract_rows(left, right):
    return lax.dot_general(
        left, right, (((0,), (0,)), ((), ())), preferred_element_type=jnp.float32
    )


def times_transpose(left, right):
    return lax.dot_general(
        left, right, (((1,), (1,)), ((), ())), preferred_element_type=jnp.float32
    )


def join_columns(block):
    count, rows_in, cols = block.shape
    return jnp.transpose(block, (1, 0, 2)).reshape(rows_in, count * cols)


def split_columns(matrix, groups):
    rows_in, cols = matrix.shape
    return jnp.transpose(matrix.reshape(rows_in, groups, cols // groups), (1, 0, 2))


def to_pairs(array, pair_width):
    batch, length, width = array.shape
    return jnp.transpose(
        array.reshape(batch, length, width // pair_width, pair_width), (2, 0, 1, 3)
    )


def from_pairs(array):
    pair_count, batch, length, pair_width = array.shape
    return jnp.transpose(array, (1, 2, 0, 3)).reshape(batch, length, pair_count * pair_width)


def send_rim(piece, offset):
    return shifted(piece.astype(jnp.bfloat16), "ctx", offset).astype(piece.dtype)


def fetch_keys(piece, offset):
    return shifted(piece, "ctx", offset)


def adam_step(master, gradient, first, second, correction, learn_rate):
    new_first = 0.5 * first + 0.5 * gradient
    new_second = 0.5 * second + 0.5 * gradient * gradient
    normed = new_first / correction / (jnp.sqrt(new_second / correction) + 1e-08)
    return (master - learn_rate * (normed + decay_rate * master), new_first, new_second)


def on_device(
    inputs,
    out_grad,
    segments,
    windows,
    owners,
    weights,
    first_moments,
    second_moments,
    norm_params,
    norm_first,
    norm_second,
):
    seq_count, tokens_dev, width = inputs.shape
    rows = seq_count * tokens_dev
    heads = windows.shape[0]
    head_dim = width // heads
    pair_width = 2 * head_dim
    slots = weights.shape[0]
    owner_count = lax.axis_size("seq")
    groups = FF // D
    reach = WIN // 2
    seq_len = segments.shape[1]
    keys_len = tokens_dev + 2 * reach
    pieces = reach // tokens_dev
    index, inverse, live = slot_maps(owners, slots, owner_count)
    gathered = lax.all_gather(weights.astype(jnp.bfloat16), "ctx", axis=1, tiled=True)
    every_slot = lax.all_gather(gathered, "seq", axis=0, tiled=True)
    units = jnp.take(every_slot, index, axis=0)
    w_qkv = jnp.concatenate([units[0], units[1], units[2]], axis=1)
    w_out = units[3]
    w_gate_up = jnp.concatenate(
        [join_columns(units[4 : 4 + groups]), join_columns(units[4 + groups : 4 + 2 * groups])],
        axis=1,
    )
    w_down = units[4 + 2 * groups :].reshape(groups * width, width)
    hidden_width = groups * width
    start = lax.axis_index("ctx") * tokens_dev
    query_pos = start + jnp.arange(tokens_dev, dtype=jnp.int32)
    key_pos = start - reach + jnp.arange(keys_len, dtype=jnp.int32)
    key_valid = (key_pos >= 0) & (key_pos < seq_len)
    query_seg = lax.dynamic_slice_in_dim(segments, start, tokens_dev, 1)
    key_seg = jnp.take(segments, jnp.clip(key_pos, 0, seq_len - 1), axis=1)
    same_doc = (query_seg[:, :, None] == key_seg[:, None, :]) & key_valid[None, None, :]
    distance = jnp.abs(query_pos[:, None] - key_pos[None, :])
    dist_float = distance.astype(jnp.float32)
    slopes = jnp.power(2.0, -8.0 * (jnp.arange(heads, dtype=jnp.float32) + 1.0) / heads)
    pair_slopes = slopes.reshape(heads // 2, 2)
    pair_windows = windows.reshape(heads // 2, 2)

    def score_block(query_part, key_part, slope_pair, window_pair):
        query_four = query_part.reshape(seq_count, tokens_dev, 2, head_dim)
        key_four = key_part.reshape(seq_count, keys_len, 2, head_dim)
        raw = (
            jnp.einsum("stgd,skgd->sgtk", query_four, key_four, preferred_element_type=jnp.float32)
            * 0.125
        )
        allowed = same_doc[:, None] & (2 * distance[None, None] < window_pair[None, :, None, None])
        logits = jnp.where(
            allowed, raw - slope_pair[None, :, None, None] * dist_float[None, None], -1e30
        )
        return (raw, allowed, logits)

    tokens_flat = inputs.reshape(rows, width)
    projected = jnp.dot(tokens_flat, w_qkv, preferred_element_type=jnp.float32).astype(jnp.bfloat16)
    queries = projected[:, :width].reshape(seq_count, tokens_dev, width)
    kv_own = projected[:, width:].reshape(seq_count, tokens_dev, 2 * width)
    left_parts = [fetch_keys(kv_own, pieces - number) for number in range(pieces)]
    right_parts = [fetch_keys(kv_own, -(number + 1)) for number in range(pieces)]
    kv_ext = jnp.concatenate(left_parts + [kv_own] + right_parts, axis=1)
    query_pairs = to_pairs(queries, pair_width)
    key_pairs = to_pairs(kv_ext[:, :, :width], pair_width)
    value_pairs = to_pairs(kv_ext[:, :, width:], pair_width)

    def attend_pair(operands):
        query_part, key_part, value_part, slope_pair, window_pair = operands
        raw, allowed, logits = score_block(query_part, key_part, slope_pair, window_pair)
        top = jnp.max(logits, axis=-1, keepdims=True)
        lifted = jnp.exp(logits - top)
        total = jnp.sum(lifted, axis=-1, keepdims=True)
        attention = (lifted / total).astype(jnp.bfloat16)
        value_four = value_part.reshape(seq_count, keys_len, 2, head_dim)
        mixed_part = jnp.einsum(
            "sgtk,skgd->stgd", attention, value_four, preferred_element_type=jnp.float32
        )
        peak = jnp.max(jnp.where(allowed, raw, -1e30), axis=(0, 2, 3))
        return (
            mixed_part.reshape(seq_count, tokens_dev, pair_width),
            (top + jnp.log(total))[..., 0],
            peak,
        )

    mixed_pairs, log_totals, peaks = lax.map(
        attend_pair, (query_pairs, key_pairs, value_pairs, pair_slopes, pair_windows)
    )
    mixed = from_pairs(mixed_pairs).reshape(rows, width).astype(jnp.bfloat16)
    logit_peak = lax.pmax(peaks.reshape(heads), ("ctx", "seq"))
    tokens_wide = tokens_flat.astype(jnp.float32)
    first_sum = tokens_wide + jnp.dot(mixed, w_out, preferred_element_type=jnp.float32)
    normed_one, norm_one_back = jax.vjp(layer_norm, first_sum, norm_params[0], norm_params[1])
    normed_low = normed_one.astype(jnp.bfloat16)
    gate_up = jnp.dot(normed_low, w_gate_up, preferred_element_type=jnp.float32)
    hidden_wide, glu_back = jax.vjp(
        glu_product, gate_up[:, :hidden_width], gate_up[:, hidden_width:]
    )
    hidden = hidden_wide.astype(jnp.bfloat16)
    second_sum = normed_one + jnp.dot(hidden, w_down, preferred_element_type=jnp.float32)
    result, norm_two_back = jax.vjp(layer_norm, second_sum, norm_params[2], norm_params[3])
    output = result.astype(jnp.bfloat16).reshape(seq_count, tokens_dev, width)
    out_wide = out_grad.reshape(rows, width).astype(jnp.float32)
    second_grad, gain_two, bias_two = norm_two_back(out_wide)
    down_in = second_grad.astype(jnp.bfloat16)
    grad_down = contract_rows(hidden, down_in)
    hidden_grad = times_transpose(down_in, w_down)
    gate_grad, linear_grad = glu_back(hidden_grad)
    gate_up_grad = jnp.concatenate([gate_grad, linear_grad], axis=1).astype(jnp.bfloat16)
    grad_gate_up = contract_rows(normed_low, gate_up_grad)
    normed_grad = second_grad + times_transpose(gate_up_grad, w_gate_up)
    first_grad, gain_one, bias_one = norm_one_back(normed_grad)
    branch_grad = first_grad.astype(jnp.bfloat16)
    grad_out = contract_rows(mixed, branch_grad)
    mixed_grad = times_transpose(branch_grad, w_out).astype(jnp.bfloat16)
    mixed_grad_pairs = to_pairs(mixed_grad.reshape(seq_count, tokens_dev, width), pair_width)

    def attend_back(operands):
        query_part, key_part, value_part, upstream, log_total, slope_pair, window_pair = operands
        raw, allowed, logits = score_block(query_part, key_part, slope_pair, window_pair)
        attention = jnp.exp(logits - log_total[..., None])
        query_four = query_part.reshape(seq_count, tokens_dev, 2, head_dim)
        key_four = key_part.reshape(seq_count, keys_len, 2, head_dim)
        value_four = value_part.reshape(seq_count, keys_len, 2, head_dim)
        upstream_four = upstream.reshape(seq_count, tokens_dev, 2, head_dim)
        weight_grad = jnp.einsum(
            "stgd,skgd->sgtk", upstream_four, value_four, preferred_element_type=jnp.float32
        )
        inner = jnp.sum(attention * weight_grad, axis=-1, keepdims=True)
        score_grad = (attention * (weight_grad - inner)).astype(jnp.bfloat16)
        query_grad = (
            jnp.einsum("sgtk,skgd->stgd", score_grad, key_four, preferred_element_type=jnp.float32)
            * 0.125
        )
        key_grad = (
            jnp.einsum(
                "sgtk,stgd->skgd", score_grad, query_four, preferred_element_type=jnp.float32
            )
            * 0.125
        )
        value_grad = jnp.einsum(
            "sgtk,stgd->skgd",
            attention.astype(jnp.bfloat16),
            upstream_four,
            preferred_element_type=jnp.float32,
        )
        return (
            query_grad.reshape(seq_count, tokens_dev, pair_width),
            key_grad.reshape(seq_count, keys_len, pair_width),
            value_grad.reshape(seq_count, keys_len, pair_width),
        )

    query_grads, key_grads, value_grads = lax.map(
        attend_back,
        (
            query_pairs,
            key_pairs,
            value_pairs,
            mixed_grad_pairs,
            log_totals,
            pair_slopes,
            pair_windows,
        ),
    )
    kv_grad_ext = jnp.concatenate([from_pairs(key_grads), from_pairs(value_grads)], axis=2)
    kv_grad = kv_grad_ext[:, reach : reach + tokens_dev]
    for number in range(pieces):
        left_piece = kv_grad_ext[:, number * tokens_dev : (number + 1) * tokens_dev]
        right_piece = kv_grad_ext[
            :, reach + (number + 1) * tokens_dev : reach + (number + 2) * tokens_dev
        ]
        kv_grad = (
            kv_grad + send_rim(left_piece, number - pieces) + send_rim(right_piece, number + 1)
        )
    qkv_grad = jnp.concatenate(
        [from_pairs(query_grads).reshape(rows, width), kv_grad.reshape(rows, 2 * width)], axis=1
    ).astype(jnp.bfloat16)
    grad_qkv = contract_rows(tokens_flat, qkv_grad)
    input_grad = (first_grad + times_transpose(qkv_grad, w_qkv)).reshape(
        seq_count, tokens_dev, width
    )
    unit_grads = jnp.concatenate(
        [
            jnp.stack(
                [
                    grad_qkv[:, :width],
                    grad_qkv[:, width : 2 * width],
                    grad_qkv[:, 2 * width :],
                    grad_out,
                ]
            ),
            split_columns(grad_gate_up[:, :hidden_width], groups),
            split_columns(grad_gate_up[:, hidden_width:], groups),
            grad_down.reshape(groups, width, width),
        ],
        axis=0,
    )
    slot_grads = jnp.where(live[:, None, None], jnp.take(unit_grads, inverse, axis=0), 0.0)
    partial_sums = lax.psum_scatter(
        slot_grads.astype(jnp.bfloat16), "seq", scatter_dimension=0, tiled=True
    )
    owned_grads = lax.psum_scatter(partial_sums, "ctx", scatter_dimension=1, tiled=True).astype(
        jnp.float32
    )
    norm_terms = jnp.stack([gain_one, bias_one, gain_two, bias_two])
    norm_grads = lax.psum(norm_terms, ("ctx", "seq"))
    correction = jnp.float32(1.0 - 0.5**STEP)
    unit_rate = 0.5 / D**0.5
    moved, new_first, new_second = adam_step(
        weights, owned_grads, first_moments, second_moments, correction, unit_rate
    )
    factors = clip_level / jnp.maximum(logit_peak, clip_level)
    column_scale = jnp.repeat(jnp.sqrt(factors), head_dim)
    local_ids = lax.axis_index("seq") * slots + jnp.arange(slots, dtype=jnp.int32)
    local_live = jnp.any(index[None, :] == local_ids[:, None], axis=1)[:, None, None]
    clipped = ((local_ids == index[0]) | (local_ids == index[1]))[:, None, None]
    new_weights = jnp.where(clipped, moved * column_scale[None, None, :], moved)
    new_weights = jnp.where(local_live, new_weights, 0.0)
    new_first = jnp.where(local_live, new_first, 0.0)
    new_second = jnp.where(local_live, new_second, 0.0)
    weights_low = new_weights.astype(jnp.bfloat16)
    new_norms, new_norm_first, new_norm_second = adam_step(
        norm_params, norm_grads, norm_first, norm_second, correction, norm_rate
    )
    return (
        output,
        input_grad,
        owned_grads,
        norm_grads,
        new_weights,
        new_first,
        new_second,
        weights_low,
        new_norms,
        new_norm_first,
        new_norm_second,
        factors,
    )


def solution(mesh):
    return jax.shard_map(
        on_device,
        mesh=mesh,
        in_specs=(
            P("seq", "ctx", None),
            P("seq", "ctx", None),
            P("seq", None),
            P(),
            P(),
            P("seq", "ctx", None),
            P("seq", "ctx", None),
            P("seq", "ctx", None),
            P(),
            P(),
            P(),
        ),
        out_specs=(
            P("seq", "ctx", None),
            P("seq", "ctx", None),
            P("seq", "ctx", None),
            P(),
            P("seq", "ctx", None),
            P("seq", "ctx", None),
            P("seq", "ctx", None),
            P("seq", "ctx", None),
            P(),
            P(),
            P(),
            P(),
        ),
        check_vma=False,
    )
```

profile of v0, /device:TPU:0, one launch (start us, length us, event | category | flops | bytes accessed | tf_op | source)
XLA Modules:
  0.0 1617.0 jit_solution(7687415000253544719)
XLA Ops:
  9.5 92.8 %all-gather.3.cloned.1.call-done = bf16[9,768,768]{2,1,0:T(8,128)(2,1)} async-done(((bf16[9,48,768]{2,1,0:T(8,128)(2,1)}), bf16[9,768,768]{2,1,0:T(8,128)(2,1)}) %all-gather.3.cloned.1.call-update) | async-done | bytes 10616848 | tf_op jit(solution)/shard_map/all_gather | solution.py:121
  103.2 249.1 %all-gather.5.cloned.1.call-done = bf16[18,768,768]{2,1,0:T(8,128)(2,1)} async-done(((bf16[9,768,768]{2,1,0:T(8,128)(2,1)}), bf16[18,768,768]{2,1,0:T(8,128)(2,1)}) %all-gather.5.cloned.1.call-update) | async-done | bytes 21233680 | tf_op jit(solution)/shard_map/all_gather | solution.py:122
  352.3 15.0 gather_fusion
  367.3 9.9 broadcast_select_fusion
  428.6 11.0 fusion.85
  469.9 197.4 %while.32 = (s32[]{:T(128)}, bf16[6,2,512,128]{2,3,1,0:T(8,128)(2,1)S(1)}, f32[6,2,2,512]{3,2,1,0:T(2,128)S(1)}, f32[6,2]{1,0:T(8,128)}, bf16[6,2,1536,128]{2,3,...) while((s32[]{:T(128)}, ...), condition=%wide.region_5.6_spmd.clone.clone, body=%wide.region_1.5_spmd.clone.clone.sunk | while | flops 877656064 | bytes 94463720 | solution.py:187
  483.5 10.1 fusion.144
  493.7 8.2 fusion.145
  516.3 10.1 fusion.144
  526.5 8.2 fusion.145
  549.1 10.1 fusion.144
  559.2 8.2 fusion.145
  574.9 7.0 fusion.143
  581.9 10.1 fusion.144
  592.0 8.2 fusion.145
  614.7 10.1 fusion.144
  624.8 8.2 fusion.145
  647.4 10.1 fusion.144
  657.6 8.2 fusion.145
  673.4 19.3 %fusion.44 = f32[1024,6144]{1,0:T(8,128)} fusion(bf16[768,3072]{0,1:T(8,128)(2,1)} %bitcast.268, bf16[768,3072]{0,1:T(8,128)(2,1)} %bitcast.266, f32[1024,768]{1,0:T(8,128)S(1)} %get-tuple-element.596, f32[768]{0:T(1024)S(1)} %copy-done.38, f32[768]{0:T(1024)S(1)} %copy-done.28, f32[1024]{0:T(1024)S(1)} %fusion.65, f32[1024]{0:T(1024)S(1)} %broadcast_multiply_fusion.3), kind=kOutput, calls=%fused_computation.98 | convolution fusion | flops 9686482944 | bytes 37763072 | tf_op jit(solution)/shard_map/dot_general | solution.py:196
  692.7 29.9 %multiply_convert_fusion.2 = (bf16[1024,3072]{1,0:T(8,128)(2,1)S(1)}, f32[1024,3072]{1,0:T(8,128)}) fusion(f32[1024,6144]{1,0:T(8,128)} %fusion.44), kind=kLoop, calls=%fused_computation.70 | loop fusion | flops 207618048 | bytes 44040192 | tf_op jit(solution)/shard_map/convert_element_type | solution.py:200
  722.6 10.0 fusion.91
  738.0 23.3 %add_convert_fusion = (bf16[1024,3072]{1,0:T(8,128)(2,1)}, bf16[1024,3072]{1,0:T(8,128)(2,1)}) fusion(f32[1024,3072]{1,0:T(8,128)} %get-tuple-element.556, f32[1024,6144]{1,0:T(8,128)} %fusion.44, bf16[3072,768]{1,0:T(8,128)(2,1)} %bitcast.265, f32[1024,768]{1,0:T(8,128)} %get-tuple-element.554, f32[1024]{0:T(1024)S(1)} %negate_multiply_fusion.2), kind=kOutput, calls=%fused_computation.69 | convolution fusion | flops 4890034176 | bytes 58200064 | tf_op jit(solution)/shard_map/dot_general | solution.py:53
  761.4 21.1 %multiply_reduce_fusion.1 = (f32[768]{0:T(1024)}, f32[1024]{0:T(1024)S(1)}, f32[768]{0:T(1024)}, f32[1024,768]{1,0:T(8,128)}) fusion(f32[1024,768]{1,0:T(8,128)S(1)} %get-tuple-element.596, f32[1024]{0:T(1024)S(1)} %fusion.65, f32[1024]{0:T(1024)S(1)} %broadcast_multiply_fusion.3, f32[768]{0:T(1024)S(1)} %copy-done.28, bf16[768,3072]{0,1:T(8,128)(2,1)} %bitcast.269, ...), kind=kOutput, calls=%fused_computation.115 | convolution fusion | flops 9715577856 | bytes 31482880 | tf_op jit(solution)/shard_map/dot_general | solution.py:53
  793.0 273.7 %while.33 = (s32[]{:T(128)}, bf16[6,2,512,128]{2,3,1,0:T(8,128)(2,1)}, f32[6,2,1536,128]{2,3,0,1:T(8,128)}, f32[6,2,1536,128]{2,3,0,1:T(8,128)}, bf16[6,2,1536,1...) while((s32[]{:T(128)}, ...), condition=%wide.region_16.17_spmd.clone.clone, body=%wide.region_14.16_spmd.clone.clone.sunk | while | flops 2057959424 | bytes 194579312 | solution.py:254
  809.2 11.8 multiply_reduce_fusion.6
  821.0 9.1 multiply_convert_fusion.4
  854.8 11.8 multiply_reduce_fusion.6
  866.7 9.1 multiply_convert_fusion.4
  900.4 11.8 multiply_reduce_fusion.6
  912.3 9.1 multiply_convert_fusion.4
  946.0 11.8 multiply_reduce_fusion.6
  957.9 9.1 multiply_convert_fusion.4
  991.6 11.8 multiply_reduce_fusion.6
  1003.4 9.1 multiply_convert_fusion.4
  1037.1 11.8 multiply_reduce_fusion.6
  1049.0 9.1 multiply_convert_fusion.4
  1078.2 19.9 %collective-permute-start.3 = (bf16[2,512,1536]{1,2,0:T(8,128)(2,1)}, bf16[2,512,1536]{1,2,0:T(8,128)(2,1)}, u32[]{:S(2)}, u32[]{:S(2)}) collective-permute-start(bf16[2,512,1536]{1,2,0:T(8,128)(2,1)} %get-tuple-element.584), channel_id=1, source_target_pairs={{0,2},{2,4},{4,6},{6,8},{8,10},{10,12},{12,14},{14,16},{16,18},{18... | collective-permute-start | bytes 9437192 | tf_op jit(solution)/shard_map/ppermute | solution.py:20
  1098.2 16.5 %fusion.38 = bf16[768,6144]{1,0:T(8,128)(2,1)} fusion(bf16[1024,3072]{1,0:T(8,128)(2,1)} %get-tuple-element.574, bf16[1024,3072]{1,0:T(8,128)(2,1)} %get-tuple-element.573, f32[1024,768]{1,0:T(8,128)S(1)} %copy-done.6, f32[768]{0:T(1024)S(1)} %copy-done.39, f32[768]{0:T(1024)S(1)} %copy-done.29, f32[1024]{0:T(1024)S(1)} %copy-done.32, f32[1024]{0:T(1024)S(1)} %copy-done.26), kind=kOutput, calls=%fused_computation.92 | convolution fusion | flops 9692774400 | bytes 25180160 | tf_op jit(solution)/shard_map/dot_general | solution.py:47
  1119.2 8.4 fusion.86
  1127.6 10.5 fusion.74
  1175.0 15.1 gather_fusion.2
  1190.1 22.1 %select_convert_fusion = bf16[18,768,768]{2,1,0:T(8,128)(2,1)} fusion(bf16[18,768,768]{2,1,0:T(8,128)(2,1)} %gather_fusion.2, pred[18]{0:T(512)(128)(4,1)S(1)} %copy-done.48, pred[18]{0:T(512)(128)(4,1)S(1)} %copy-done.47), kind=kLoop, calls=%fused_computation.59 | loop fusion | flops 21233664 | bytes 42467364 | tf_op jit(solution)/shard_map/convert_element_type | solution.py:301
  1212.3 264.5 %reduce-scatter.3.cloned.1.call-done = bf16[9,768,768]{2,1,0:T(8,128)(2,1)} async-done(((bf16[18,768,768]{2,1,0:T(8,128)(2,1)}), bf16[9,768,768]{2,1,0:T(8,128)(2,1)}) %reduce-scatter.3.cloned.1.call-update) | async-done | bytes 10616848 | tf_op jit(solution)/shard_map/reduce_scatter | solution.py:300
  1480.0 39.4 %pmax.7 = f32[12]{0:T(128)S(1)} all-reduce(f32[12]{0:T(128)S(1)} %reshape.371), channel_id=1, replica_groups=mesh['ctx'=16,'seq'=2] {'ctx','seq'}, use_global_device_ids=true, to_apply=%region_27.28 | all-reduce | flops 12 | bytes 96 | tf_op jit(solution)/shard_map/pmax | solution.py:191
  1520.0 45.9 %psum.7 = f32[4,768]{1,0:T(4,128)S(1)} all-reduce(f32[4,768]{1,0:T(4,128)S(1)} %pad_maximum_fusion.20), channel_id=1, replica_groups=mesh['ctx'=16,'seq'=2] {'ctx','seq'}, use_global_device_ids=true, to_apply=%region_25.26 | all-reduce | flops 3072 | bytes 24576 | tf_op jit(solution)/shard_map/psum | solution.py:307
  1566.6 10.0 add_add_fusion.2
  1576.7 27.6 %reduce-scatter.5.cloned.1.call-done = bf16[9,48,768]{2,1,0:T(8,128)(2,1)} async-done(((bf16[9,768,768]{2,1,0:T(8,128)(2,1)}), bf16[9,48,768]{2,1,0:T(8,128)(2,1)}) %reduce-scatter.5.cloned.1.call-update) | async-done | bytes 663568 | tf_op jit(solution)/shard_map/reduce_scatter | solution.py:303
  (475 shorter events, 396.4 us)
Async XLA Ops:
  7.2 95.1 %all-gather.3.cloned.1.call-start = ((), (), s32[]{:S(2)}) async-start(), calls=%async_computation.2 | async-start | bytes 11280384 | tf_op jit(solution)/shard_map/all_gather | solution.py:121
  9.5 342.8 %all-gather.5.cloned.1.call-start = ((), (), s32[]{:S(2)}) async-start(), calls=%async_computation.3 | async-start | bytes 31850496 | tf_op jit(solution)/shard_map/all_gather | solution.py:122
  102.3 1374.5 %reduce-scatter.3.cloned.1.call-start = ((), (), s32[]{:S(2)}) async-start(), calls=%async_computation.4 | async-start | bytes 31850496 | tf_op jit(solution)/shard_map/reduce_scatter | solution.py:300
  103.2 311.6 %copy-start.36 = (s32[16]{0:T(128)}, s32[16]{0:T(128)S(1)}, u32[]{:S(2)}) copy-start(s32[16]{0:T(128)S(1)} %get-tuple-element.558) | copy-start | bytes 196
  396.8 22.5 %copy-start.4 = (bf16[2,512,1536]{1,2,0:T(8,128)(2,1)}, bf16[2,512,1536]{1,2,0:T(8,128)(2,1)S(1)}, u32[]{:S(2)}) copy-start(bf16[2,512,1536]{1,2,0:T(8,128)(2,1)S(1)} %copy.114) | copy-start | bytes 9437188
  396.9 17.1 %copy-start.49 = (s32[12]{0:T(128)S(1)}, s32[12]{0:T(128)}, u32[]{:S(2)}) copy-start(s32[12]{0:T(128)} %param.18) | copy-start | bytes 148
  396.9 18.6 %copy-start.22 = (f32[4,768]{1,0:T(4,128)S(1)}, f32[4,768]{1,0:T(4,128)}, u32[]{:S(2)}) copy-start(f32[4,768]{1,0:T(4,128)} %param.23) | copy-start | bytes 36868
  396.9 56.0 %collective-permute-start = (bf16[2,512,1536]{1,2,0:T(8,128)(2,1)S(1)}, bf16[2,512,1536]{1,2,0:T(8,128)(2,1)}, u32[]{:S(2)}, u32[]{:S(2)}) collective-permute-start(bf16[2,512,1536]{1,2,0:T(8,128)(2,1)S(1)} %copy.114), channel_id=1, source_target_pairs={{0,2},{2,4},{4,6},{6,8},{8,10},{10,12},{12,14},{14,16},{16,18},{18... | collective-permute-start | bytes 9437192 | tf_op jit(solution)/shard_map/ppermute | solution.py:20
  400.4 52.5 %collective-permute-start.1 = (bf16[2,512,1536]{1,2,0:T(8,128)(2,1)S(1)}, bf16[2,512,1536]{1,2,0:T(8,128)(2,1)}, u32[]{:S(2)}, u32[]{:S(2)}) collective-permute-start(bf16[2,512,1536]{1,2,0:T(8,128)(2,1)S(1)} %copy.114), channel_id=1, source_target_pairs={{2,0},{4,2},{6,4},{8,6},{10,8},{12,10},{14,12},{16,14},{18,16},{20... | collective-permute-start | bytes 9437192 | tf_op jit(solution)/shard_map/ppermute | solution.py:20
  672.8 109.7 %copy-start.5 = (f32[1024,768]{1,0:T(8,128)}, f32[1024,768]{1,0:T(8,128)S(1)}, u32[]{:S(2)}) copy-start(f32[1024,768]{1,0:T(8,128)S(1)} %get-tuple-element.596) | copy-start | bytes 9437188
  672.8 109.7 %copy-start.25 = (f32[1024]{0:T(1024)}, f32[1024]{0:T(1024)S(1)}, u32[]{:S(2)}) copy-start(f32[1024]{0:T(1024)S(1)} %broadcast_multiply_fusion.3) | copy-start | bytes 12292
  673.3 109.2 %copy-start.31 = (f32[1024]{0:T(1024)}, f32[1024]{0:T(1024)S(1)}, u32[]{:S(2)}) copy-start(f32[1024]{0:T(1024)S(1)} %fusion.65) | copy-start | bytes 12292
  722.6 10.6 copy-start.2
  722.6 10.6 copy-start.27
  738.0 23.4 %copy-start.45 = (f32[1024]{0:T(1024)}, f32[1024]{0:T(1024)S(1)}, u32[]{:S(2)}) copy-start(f32[1024]{0:T(1024)S(1)} %negate_multiply_fusion.2) | copy-start | bytes 12292
  821.0 10.7 slice-start.1
  821.0 11.9 slice-start.2
  866.7 10.7 slice-start.1
  866.7 11.9 slice-start.2
  912.2 10.7 slice-start.1
  912.3 11.9 slice-start.2
  957.9 10.7 slice-start.1
  957.9 11.9 slice-start.2
  1003.4 10.7 slice-start.1
  1003.4 11.9 slice-start.2
  1049.0 10.7 slice-start.1
  1049.0 11.9 slice-start.2
  1073.6 24.5 %copy-start.6 = (f32[1024,768]{1,0:T(8,128)S(1)}, f32[1024,768]{1,0:T(8,128)}, u32[]{:S(2)}) copy-start(f32[1024,768]{1,0:T(8,128)} %copy-done.5) | copy-start | bytes 9437188
  1073.6 24.5 %copy-start.26 = (f32[1024]{0:T(1024)S(1)}, f32[1024]{0:T(1024)}, u32[]{:S(2)}) copy-start(f32[1024]{0:T(1024)} %copy-done.25) | copy-start | bytes 12292
  1073.6 24.5 %copy-start.29 = (f32[768]{0:T(1024)S(1)}, f32[768]{0:T(1024)}, u32[]{:S(2)}) copy-start(f32[768]{0:T(1024)} %get-tuple-element.481) | copy-start | bytes 9220
  1073.7 24.5 %copy-start.32 = (f32[1024]{0:T(1024)S(1)}, f32[1024]{0:T(1024)}, u32[]{:S(2)}) copy-start(f32[1024]{0:T(1024)} %copy-done.31) | copy-start | bytes 12292
  1073.7 24.5 %copy-start.39 = (f32[768]{0:T(1024)S(1)}, f32[768]{0:T(1024)}, u32[]{:S(2)}) copy-start(f32[768]{0:T(1024)} %get-tuple-element.480) | copy-start | bytes 9220
  1076.9 61.2 %collective-permute-start.2 = (bf16[2,512,1536]{1,2,0:T(8,128)(2,1)}, bf16[2,512,1536]{1,2,0:T(8,128)(2,1)}, u32[]{:S(2)}, u32[]{:S(2)}) collective-permute-start(bf16[2,512,1536]{1,2,0:T(8,128)(2,1)} %get-tuple-element.583), channel_id=1, source_target_pairs={{2,0},{4,2},{6,4},{8,6},{10,8},{12,10},{14,12},{16,14},{18,16},{20... | collective-permute-start | bytes 9437192 | tf_op jit(solution)/shard_map/ppermute | solution.py:20
  1078.2 59.9 %collective-permute-start.3 = (bf16[2,512,1536]{1,2,0:T(8,128)(2,1)}, bf16[2,512,1536]{1,2,0:T(8,128)(2,1)}, u32[]{:S(2)}, u32[]{:S(2)}) collective-permute-start(bf16[2,512,1536]{1,2,0:T(8,128)(2,1)} %get-tuple-element.584), channel_id=1, source_target_pairs={{0,2},{2,4},{4,6},{6,8},{8,10},{10,12},{12,14},{14,16},{16,18},{18... | collective-permute-start | bytes 9437192 | tf_op jit(solution)/shard_map/ppermute | solution.py:20
  1119.2 19.0 %slice-start.3 = ((s8[9437184]{0:T(1024)(128)(4,1)}), s8[1048576]{0:T(1024)(128)(4,1)S(1)}, s32[]{:S(2)}) async-start(s8[9437184]{0:T(1024)(128)(4,1)} %bitcast.240), calls=%async_computation.9 | async-start | bytes 2097152
  1119.2 19.0 %slice-start.4 = ((s8[9437184]{0:T(1024)(128)(4,1)}), s8[4194304]{0:T(1024)(128)(4,1)S(1)}, s32[]{:S(2)}) async-start(s8[9437184]{0:T(1024)(128)(4,1)} %bitcast.240), calls=%async_computation.10 | async-start | bytes 8388608
  1175.0 15.1 copy-start.47
  1175.0 15.1 copy-start.48
  1212.2 392.0 %reduce-scatter.5.cloned.1.call-start = ((), (), s32[]{:S(2)}) async-start(), calls=%async_computation.5 | async-start | bytes 11280384 | tf_op jit(solution)/shard_map/reduce_scatter | solution.py:303
  1476.8 43.1 %copy-start.41 = (f32[768]{0:T(1024)S(1)}, f32[768]{0:T(1024)}, u32[]{:S(2)}) copy-start(f32[768]{0:T(1024)} %get-tuple-element.474) | copy-start | bytes 9220
  1476.8 43.1 %copy-start.40 = (f32[768]{0:T(1024)S(1)}, f32[768]{0:T(1024)}, u32[]{:S(2)}) copy-start(f32[768]{0:T(1024)} %get-tuple-element.478) | copy-start | bytes 9220
  1476.9 43.1 %copy-start.33 = (f32[768]{0:T(1024)S(1)}, f32[768]{0:T(1024)}, u32[]{:S(2)}) copy-start(f32[768]{0:T(1024)} %get-tuple-element.476) | copy-start | bytes 9220
  1476.9 89.1 %copy-start.23 = (f32[4,768]{1,0:T(4,128)S(1)}, f32[4,768]{1,0:T(4,128)}, u32[]{:S(2)}) copy-start(f32[4,768]{1,0:T(4,128)} %param.23) | copy-start | bytes 36868
  1476.9 89.1 %copy-start.34 = (f32[4,768]{1,0:T(4,128)S(1)}, f32[4,768]{1,0:T(4,128)}, u32[]{:S(2)}) copy-start(f32[4,768]{1,0:T(4,128)} %param.24) | copy-start | bytes 36868
  1476.9 89.1 %copy-start.35 = (f32[4,768]{1,0:T(4,128)S(1)}, f32[4,768]{1,0:T(4,128)}, u32[]{:S(2)}) copy-start(f32[4,768]{1,0:T(4,128)} %param.25) | copy-start | bytes 36868
  1566.0 10.7 copy-start.24
  1566.6 37.6 %copy-start.8 = (f32[9,48,768]{2,1,0:T(8,128)S(1)}, f32[9,48,768]{2,1,0:T(8,128)}, u32[]{:S(2)}) copy-start(f32[9,48,768]{2,1,0:T(8,128)} %param.20) | copy-start | bytes 3981316
  1566.6 37.6 %copy-start.9 = (f32[9,48,768]{2,1,0:T(8,128)S(1)}, f32[9,48,768]{2,1,0:T(8,128)}, u32[]{:S(2)}) copy-start(f32[9,48,768]{2,1,0:T(8,128)} %param.22) | copy-start | bytes 3981316
  (50 other events, 246.1 us)
Sparse Core Ops, SparseCore 0:
  10.9 91.4 all-gather.2
  103.9 248.3 all-gather.4
  1212.4 264.4 reduce-scatter.2
  1481.3 122.9 reduce-scatter.4
where the time goes:
time: 1630 us; the launch traced here: 1620 us
  waiting for transfers between devices  634 us (39%)
  matrix products  360 us (22%)
  other arithmetic  269 us (17%)
  local copies, waits for them, and re-layouts  225 us (14%)
  blocking collectives  85.3 us (5%)
  starting transfers between devices  26.2 us (2%)
    reduce_scatter x1, waiting for transfers between devices, on_device(): lax.psum_scatter(slot_grads.astype(jnp.bfloat16), 'seq', scatter_dimensio...  265 us
    all_gather x1, waiting for transfers between devices, on_device(): every_slot = lax.all_gather(gathered, 'seq', axis=0, tiled=True)  249 us
    dot_general x12, matrix products, score_block(): jnp.einsum('stgd,skgd->sgtk', query_four, key_four, preferred_element_typ...  113 us
    all_gather x1, waiting for transfers between devices, on_device(): lax.all_gather(weights.astype(jnp.bfloat16), 'ctx', axis=1, tiled=True)  92.8 us
    reduce_max x6, other arithmetic, attend_pair(): peak = jnp.max(jnp.where(allowed, raw, -1e+30), axis=(0, 2, 3))  60.7 us
    dot_general x4, matrix products, times_transpose(): lax.dot_general(left, right, (((1,), (1,)), ((), ())), preferred_element_...  57.2 us
    convert_element_type x6, other arithmetic, attend_back(): score_grad = (attention * (weight_grad - inner)).astype(jnp.bfloat16)  54.7 us
    dot_general x6, matrix products, attend_pair(): jnp.einsum('sgtk,skgd->stgd', attention, value_four, preferred_element_ty...  49.1 us
  transfers between devices with their start and end apart: 8, of which 4 were waited for; matrix products, arithmetic and copies ran while one was open for 6% of the time, Pallas kernels for 0%

commit v1 on v0

v1 whole, which is shorter than its diff:
```python
import jax
import jax.numpy as jnp
from jax import lax
from jax.experimental import pallas as pl
from jax.experimental.pallas import tpu as pltpu
from jax.sharding import PartitionSpec as P

D = 768
FF = 3072
STEP = 3
clip_level = 1.0
decay_rate = 0.1
norm_rate = 0.25
LOG2E = 1.4426950408889634
NEG = -1e30
REACH = 512
QB = 256
bf16 = jnp.bfloat16
f32 = jnp.float32

def dot_nt(a, b):
    return lax.dot_general(a, b, (((1,), (1,)), ((), ())), preferred_element_type=f32)

def dot_nn(a, b):
    return lax.dot_general(a, b, (((1,), (0,)), ((), ())), preferred_element_type=f32)

def fill_bias(bias_ref, slope2):
    rows = bias_ref.shape[0]
    k = lax.broadcasted_iota(jnp.int32, (rows, QB), 0)
    q = lax.broadcasted_iota(jnp.int32, (rows, QB), 1)
    bias_ref[...] = jnp.abs(k - q - REACH).astype(f32) * (-slope2)

def fold8(x, op):
    y = x.reshape(x.shape[0] // 8, 8, x.shape[1])
    return op(y, axis=0)

def head_window(win_ref, lo_ref, hi_ref, head, qb):
    reach = (win_ref[head] - 1) >> 1
    cls = jnp.clip((reach + 127) >> 7, 2, 4)
    qpos = lax.broadcasted_iota(jnp.int32, (1, QB), 1) + (qb * QB + REACH)
    lo = jnp.maximum(lo_ref[0, :, pl.ds(qb * QB, QB)], qpos - reach)
    hi = jnp.minimum(hi_ref[0, :, pl.ds(qb * QB, QB)], qpos + reach)
    return cls, lo, hi

def fwd_kernel(win_ref, slope_ref, q_ref, k_ref, v_ref, lo_ref, hi_ref, o_ref, lse_ref, peak_ref,
               vt_ref, ot_ref, z_ref, bias_ref):
    pair = pl.program_id(0)
    seq = pl.program_id(1)
    tokens = q_ref.shape[1]
    vt_ref[...] = v_ref[0].T

    @pl.when(seq == 0)
    def _():
        peak_ref[...] = jnp.full(peak_ref.shape, NEG, f32)

    rows = lax.broadcasted_iota(jnp.int32, (QB, QB), 0)
    lane = lax.broadcasted_iota(jnp.int32, (1, 128), 1)
    for h in range(2):
        head = pair * 2 + h
        @pl.when(seq == 0)
        def _():
            fill_bias(bias_ref.at[h], slope_ref[head])
        hmask = jnp.where((lane >= h * 64) & (lane < h * 64 + 64), 0.125, 0.0)
        for qb in range(tokens // QB):
            cls, lo, hi = head_window(win_ref, lo_ref, hi_ref, head, qb)
            q = (q_ref[0, pl.ds(qb * QB, QB), :].astype(f32) * hmask).astype(bf16)

            def branch(c):
                reach = c * 128
                first = REACH - reach
                n = 1 + c
                pk = mx = None
                for t in range(n):
                    b = first + t * QB
                    s = dot_nt(k_ref[0, pl.ds(qb * QB + b, QB), :], q)
                    kk = rows + (qb * QB + b)
                    s = jnp.where((kk >= lo) & (kk <= hi), s, NEG)
                    z = s * LOG2E + bias_ref[h, pl.ds(b, QB), :]
                    a, d = fold8(s, jnp.max), fold8(z, jnp.max)
                    pk = a if t == 0 else jnp.maximum(pk, a)
                    mx = d if t == 0 else jnp.maximum(mx, d)
                    z_ref[pl.ds(t * QB, QB), :] = z
                peak_ref[h] = jnp.maximum(peak_ref[h], pk)
                m = jnp.max(mx, axis=0, keepdims=True)
                acc = total = None
                for t in range(n):
                    p = jnp.exp2(z_ref[pl.ds(t * QB, QB), :] - m)
                    e = fold8(p, jnp.sum)
                    total = e if t == 0 else total + e
                    b = first + t * QB
                    part = dot_nn(vt_ref[pl.ds(h * 64, 64), pl.ds(qb * QB + b, QB)], p.astype(bf16))
                    acc = part if t == 0 else acc + part
                total = jnp.sum(total, axis=0, keepdims=True)
                ot_ref[pl.ds(h * 64, 64), pl.ds(qb * QB, QB)] = acc * (1.0 / total)
                lse_ref[0, 0, pl.ds(h, 1), pl.ds(qb * QB, QB)] = m + jnp.log2(total)

            for c in (2, 3, 4):
                pl.when(cls == c)(lambda c=c: branch(c))
    o_ref[0] = ot_ref[...].T.astype(bf16)

def attend_fwd(windows, slopes2, q, kv, lo, hi):
    seqs, tokens, width = q.shape
    keys = kv.shape[1]
    pairs = width // 128
    smem = pl.BlockSpec(memory_space=pltpu.SMEM)
    return pl.pallas_call(
        fwd_kernel,
        grid=(pairs, seqs),
        in_specs=[
            smem, smem,
            pl.BlockSpec((1, tokens, 128), lambda p, s: (s, 0, p)),
            pl.BlockSpec((1, keys, 128), lambda p, s: (s, 0, p)),
            pl.BlockSpec((1, keys, 128), lambda p, s: (s, 0, p + pairs)),
            pl.BlockSpec((1, 1, tokens), lambda p, s: (s, 0, 0)),
            pl.BlockSpec((1, 1, tokens), lambda p, s: (s, 0, 0)),
        ],
        out_specs=[
            pl.BlockSpec((1, tokens, 128), lambda p, s: (s, 0, p)),
            pl.BlockSpec((1, 1, 2, tokens), lambda p, s: (s, p, 0, 0)),
            pl.BlockSpec((2, 8, QB), lambda p, s: (p, 0, 0)),
        ],
        out_shape=[
            jax.ShapeDtypeStruct((seqs, tokens, width), bf16),
            jax.ShapeDtypeStruct((seqs, pairs, 2, tokens), f32),
            jax.ShapeDtypeStruct((2 * pairs, 8, QB), f32),
        ],
        scratch_shapes=[
            pltpu.VMEM((128, keys), bf16),
            pltpu.VMEM((128, tokens), f32),
            pltpu.VMEM((QB + 2 * REACH, QB), f32),
            pltpu.VMEM((2, QB + 2 * REACH, QB), f32),
        ],
        compiler_params=pltpu.CompilerParams(vmem_limit_bytes=40 * 2**20),
        cost_estimate=pl.CostEstimate(flops=2 * 10**10, bytes_accessed=10**7, transcendentals=10**7),
        name="attend_fwd",
    )(windows, slopes2, q, kv, kv, lo, hi)

def bwd_kernel(win_ref, slope_ref, q_ref, k_ref, v_ref, do_ref, lo_ref, hi_ref, lse_ref, dsum_ref,
               dq_ref, dk_ref, dv_ref, kt_ref, dqt_ref, dka_ref, dva_ref, bias_ref):
    pair = pl.program_id(0)
    seq = pl.program_id(1)
    tokens = q_ref.shape[1]
    kt_ref[...] = k_ref[0].T
    dka_ref[...] = jnp.zeros(dka_ref.shape, f32)
    dva_ref[...] = jnp.zeros(dva_ref.shape, f32)
    rows = lax.broadcasted_iota(jnp.int32, (QB, QB), 0)
    lane = lax.broadcasted_iota(jnp.int32, (1, 128), 1)
    for h in range(2):
        head = pair * 2 + h
        @pl.when(seq == 0)
        def _():
            fill_bias(bias_ref.at[h], slope_ref[head])
        inside = (lane >= h * 64) & (lane < h * 64 + 64)
        qmask = jnp.where(inside, 0.125, 0.0)
        dmask = jnp.where(inside, 1.0, 0.0)
        for qb in range(tokens // QB):
            cls, lo, hi = head_window(win_ref, lo_ref, hi_ref, head, qb)
            q = (q_ref[0, pl.ds(qb * QB, QB), :].astype(f32) * qmask).astype(bf16)
            do = (do_ref[0, pl.ds(qb * QB, QB), :].astype(f32) * dmask).astype(bf16)
            lse = lse_ref[0, 0, pl.ds(h, 1), pl.ds(qb * QB, QB)]
            dsum = dsum_ref[0, 0, pl.ds(h, 1), pl.ds(qb * QB, QB)]

            def branch(c):
                first = REACH - c * 128
                dqt = None
                for t in range(1 + c):
                    b = first + t * QB
                    at = pl.ds(qb * QB + b, QB)
                    s = dot_nt(k_ref[0, at, :], q)
                    dp = dot_nt(v_ref[0, at, :], do)
                    kk = rows + (qb * QB + b)
                    z = s * LOG2E + (bias_ref[h, pl.ds(b, QB), :] - lse)
                    p = jnp.exp2(jnp.where((kk >= lo) & (kk <= hi), z, NEG))
                    ds = (p * (dp - dsum)).astype(bf16)
                    dva_ref[at, :] += dot_nn(p.astype(bf16), do)
                    dka_ref[at, :] += dot_nn(ds, q)
                    part = dot_nn(kt_ref[pl.ds(h * 64, 64), at], ds)
                    dqt = part if t == 0 else dqt + part
                dqt_ref[pl.ds(h * 64, 64), pl.ds(qb * QB, QB)] = dqt * 0.125

            for c in (2, 3, 4):
                pl.when(cls == c)(lambda c=c: branch(c))
    dq_ref[0] = dqt_ref[...].T.astype(bf16)
    dk_ref[0] = dka_ref[...].astype(bf16)
    dv_ref[0] = dva_ref[...].astype(bf16)

def attend_bwd(windows, slopes2, q, kv, do, lo, hi, lse, dsum):
    seqs, tokens, width = q.shape
    keys = kv.shape[1]
    pairs = width // 128
    smem = pl.BlockSpec(memory_space=pltpu.SMEM)
    tok = pl.BlockSpec((1, tokens, 128), lambda p, s: (s, 0, p))
    key = pl.BlockSpec((1, keys, 128), lambda p, s: (s, 0, p))
    row = pl.BlockSpec((1, 1, tokens), lambda p, s: (s, 0, 0))
    stat = pl.BlockSpec((1, 1, 2, tokens), lambda p, s: (s, p, 0, 0))
    return pl.pallas_call(
        bwd_kernel,
        grid=(pairs, seqs),
        in_specs=[smem, smem, tok, key, pl.BlockSpec((1, keys, 128), lambda p, s: (s, 0, p + pairs)), tok, row, row, stat, stat],
        out_specs=[tok, key, key],
        out_shape=[
            jax.ShapeDtypeStruct((seqs, tokens, width), bf16),
            jax.ShapeDtypeStruct((seqs, keys, width), bf16),
            jax.ShapeDtypeStruct((seqs, keys, width), bf16),
        ],
        scratch_shapes=[
            pltpu.VMEM((128, keys), bf16),
            pltpu.VMEM((128, tokens), f32),
            pltpu.VMEM((keys, 128), f32),
            pltpu.VMEM((keys, 128), f32),
            pltpu.VMEM((2, QB + 2 * REACH, QB), f32),
        ],
        compiler_params=pltpu.CompilerParams(vmem_limit_bytes=40 * 2**20),
        cost_estimate=pl.CostEstimate(flops=5 * 10**10, bytes_accessed=2 * 10**7, transcendentals=10**7),
        name="attend_bwd",
    )(windows, slopes2, q, kv, kv, do, lo, hi, lse, dsum)

def shifted(value, axis, by):
    peers = lax.axis_size(axis)
    pairs = [(i, i + by) for i in range(peers) if 0 <= i + by < peers]
    return lax.ppermute(value, axis, pairs)


def swapped(value, axis, bit):
    peers = lax.axis_size(axis)
    return lax.ppermute(value, axis, [(i, i ^ bit) for i in range(peers)])


def layer_norm(rows_in):
    center = rows_in - jnp.mean(rows_in, axis=-1, keepdims=True)
    spread = jnp.mean(center * center, axis=-1, keepdims=True)
    scale = lax.rsqrt(spread + 1e-05)
    return center * scale, scale


def layer_norm_back(grad, hat, scale, gain):
    inner = grad * gain
    mean_one = jnp.mean(inner, axis=-1, keepdims=True)
    mean_two = jnp.mean(inner * hat, axis=-1, keepdims=True)
    back = scale * (inner - mean_one - hat * mean_two)
    return back, jnp.sum(grad * hat, axis=0), jnp.sum(grad, axis=0)


def pick_units(slot_of, sources, count):
    slots, rows, width = sources[0].shape

    def kernel(slot_ref, *refs):
        out_ref = refs[-1]
        for u in range(count):
            at = pl.ds(u * width, width)
            for number, ref in enumerate(refs[:-1]):

                @pl.when(slot_ref[0, u] == number)
                def _(ref=ref, u=u, at=at):
                    out_ref[:, at] = ref[slot_ref[1, u]]

    vmem = pl.BlockSpec(memory_space=pltpu.VMEM)
    return pl.pallas_call(
        kernel,
        in_specs=[pl.BlockSpec(memory_space=pltpu.SMEM)] + [vmem] * len(sources),
        out_specs=vmem,
        out_shape=jax.ShapeDtypeStruct((rows, count * width), sources[0].dtype),
        compiler_params=pltpu.CompilerParams(vmem_limit_bytes=24 * 2**20),
        name="pick_units",
    )(slot_of, *sources)


def to_slots(unit_of, columns, slots, width):
    rows = columns.shape[0]

    def kernel(unit_ref, col_ref, out_ref):
        for s in range(slots):
            unit = unit_ref[s]

            @pl.when(unit >= 0)
            def _(s=s, unit=unit):
                out_ref[s] = col_ref[:, pl.ds(pl.multiple_of(unit * width, 128), width)]

            @pl.when(unit < 0)
            def _(s=s):
                out_ref[s] = jnp.zeros((rows, width), out_ref.dtype)

    vmem = pl.BlockSpec(memory_space=pltpu.VMEM)
    return pl.pallas_call(
        kernel,
        in_specs=[pl.BlockSpec(memory_space=pltpu.SMEM), vmem],
        out_specs=vmem,
        out_shape=jax.ShapeDtypeStruct((slots, rows, width), columns.dtype),
        compiler_params=pltpu.CompilerParams(vmem_limit_bytes=24 * 2**20),
        name="to_slots",
    )(unit_of, columns)


def adam_slots(unit_of, weights, first, second, grads, scale, correction, rate):
    slots, rows, width = weights.shape

    def kernel(unit_ref, w_ref, m_ref, v_ref, scale_ref, *refs):
        grad_refs, (g_out, w_out, m_out, v_out, low_out) = refs[:-5], refs[-5:]
        unit = unit_ref[pl.program_id(0)]
        live = unit >= 0
        g = grad_refs[0][0].astype(f32)
        for ref in grad_refs[1:]:
            g = g + ref[0].astype(f32)
        g = jnp.where(live, g, 0.0)
        w = w_ref[0]
        m = 0.5 * m_ref[0] + 0.5 * g
        v = 0.5 * v_ref[0] + 0.5 * g * g
        step = m * (1.0 / correction) / (jnp.sqrt(v * (1.0 / correction)) + 1e-08)
        moved = w - rate * (step + decay_rate * w)
        moved = jnp.where((unit == 0) | (unit == 1), moved * scale_ref[...], moved)
        moved = jnp.where(live, moved, 0.0)
        g_out[0] = g
        w_out[0] = moved
        m_out[0] = jnp.where(live, m, 0.0)
        v_out[0] = jnp.where(live, v, 0.0)
        low_out[0] = moved.astype(bf16)

    block = pl.BlockSpec((1, rows, width), lambda s: (s, 0, 0))
    wide = jax.ShapeDtypeStruct(weights.shape, f32)
    return pl.pallas_call(
        kernel,
        grid=(slots,),
        in_specs=[pl.BlockSpec(memory_space=pltpu.SMEM), block, block, block,
                  pl.BlockSpec((1, width), lambda s: (0, 0))] + [block] * len(grads),
        out_specs=[block] * 5,
        out_shape=[wide] * 4 + [jax.ShapeDtypeStruct(weights.shape, bf16)],
        compiler_params=pltpu.CompilerParams(vmem_limit_bytes=24 * 2**20),
        name="adam_slots",
    )(unit_of, weights, first, second, scale, *grads)


def adam_step(master, gradient, first, second, correction, learn_rate):
    new_first = 0.5 * first + 0.5 * gradient
    new_second = 0.5 * second + 0.5 * gradient * gradient
    normed = new_first / correction / (jnp.sqrt(new_second / correction) + 1e-08)
    return (master - learn_rate * (normed + decay_rate * master), new_first, new_second)


def dot_tn(a, b):
    return lax.dot_general(a, b, (((0,), (0,)), ((), ())), preferred_element_type=f32)


def gelu_parts(gate):
    cdf = 0.5 * (1.0 + lax.erf(gate * 0.7071067811865476))
    density = 0.3989422804014327 * jnp.exp(-0.5 * gate * gate)
    return cdf, density


def on_device(inputs, out_grad, segments, windows, owners, weights, first_moments, second_moments,
              norm_params, norm_first, norm_second):
    seqs, tokens, width = inputs.shape
    rows = seqs * tokens
    heads = windows.shape[0]
    slots = weights.shape[0]
    owner_count = lax.axis_size("seq")
    me = lax.axis_index("seq")
    seq_len = segments.shape[1]
    keys = tokens + 2 * REACH
    pieces = REACH // tokens
    groups = FF // width
    units = owners.shape[0]
    rest = units - 3

    ids = jnp.arange(units, dtype=jnp.int32)
    before = (owners[None, :] == owners[:, None]) & (ids[None, :] < ids[:, None])
    rank = jnp.sum(before.astype(jnp.int32), axis=1)
    slot_ids = jnp.arange(owner_count * slots, dtype=jnp.int32)
    match = (owners * slots + rank)[None, :] == slot_ids[:, None]
    unit_of = jnp.max(jnp.where(match, ids[None, :], -1), axis=1)
    my_units = lax.dynamic_slice_in_dim(unit_of, me * slots, slots, 0)

    low = weights.astype(bf16)
    if owner_count == 2:
        place = jnp.stack([jnp.where(owners == me, 0, 1), rank])
        own_first = pick_units(place[:, :3] * jnp.array([[0], [1]], jnp.int32), [low], 3)
        got_first = swapped(own_first, "seq", 1)
        mine = jnp.repeat(owners[:3] == me, width)[None, :]
        picked_first = jnp.where(mine, own_first, got_first)
        sources = [low, swapped(low, "seq", 1)]
    else:
        every = lax.all_gather(low, "seq", axis=0, tiled=True)
        place = jnp.stack([jnp.zeros_like(owners), owners * slots + rank])
        sources = [every]
        picked_first = pick_units(place[:, :3], sources, 3)
    w_first = lax.all_gather(picked_first, "ctx", axis=0, tiled=True)
    picked_rest = pick_units(place[:, 3:], sources, rest)
    picked_rest, w_first = lax.optimization_barrier((picked_rest, w_first))
    w_rest = lax.all_gather(picked_rest, "ctx", axis=0, tiled=True)

    left = [shifted(inputs, "ctx", pieces - n) for n in range(pieces)]
    right = [shifted(inputs, "ctx", -(n + 1)) for n in range(pieces)]
    x_ext = jnp.concatenate(left + [inputs] + right, axis=1)

    start = lax.axis_index("ctx") * tokens
    padded = jnp.pad(segments, ((0, 0), (REACH, 0)), constant_values=-1)
    padded = jnp.pad(padded, ((0, 0), (0, REACH)), constant_values=1 << 20)
    key_seg = lax.dynamic_slice_in_dim(padded, start, keys, 1)
    query_seg = key_seg[:, REACH : REACH + tokens]
    lo = jnp.sum((key_seg[:, :, None] < query_seg[:, None, :]).astype(jnp.int32), axis=1)[:, None]
    hi = jnp.sum((key_seg[:, :, None] <= query_seg[:, None, :]).astype(jnp.int32), axis=1)[:, None] - 1
    slopes2 = jnp.power(2.0, -8.0 * (jnp.arange(heads, dtype=f32) + 1.0) / heads) * LOG2E

    w_q, w_kv = w_first[:, :width], w_first[:, width:]
    x = inputs.reshape(rows, width)
    q = dot_nn(x, w_q).astype(bf16).reshape(seqs, tokens, width)
    kv = dot_nn(x_ext.reshape(seqs * keys, width), w_kv).astype(bf16).reshape(seqs, keys, 2 * width)
    mixed, lse, peaks = attend_fwd(windows, slopes2, q, kv, lo, hi)
    peak = jnp.max(peaks, axis=(1, 2))
    o = mixed.reshape(rows, width)

    w_out = w_rest[:, :width]
    w_gate = w_rest[:, width : width + FF]
    w_up = w_rest[:, width + FF : width + 2 * FF]
    w_down = jnp.concatenate(
        [w_rest[:, width + 2 * FF + g * width : width + 2 * FF + (g + 1) * width] for g in range(groups)], axis=0
    )
    first_sum = x.astype(f32) + dot_nn(o, w_out)
    hat_one, scale_one = layer_norm(first_sum)
    y1 = hat_one * norm_params[0] + norm_params[1]
    y_low = y1.astype(bf16)
    gate = dot_nn(y_low, w_gate)
    up = dot_nn(y_low, w_up)
    cdf, density = gelu_parts(gate)
    hidden = (gate * cdf * up).astype(bf16)
    second_sum = y1 + dot_nn(hidden, w_down)
    hat_two, scale_two = layer_norm(second_sum)
    output = (hat_two * norm_params[2] + norm_params[3]).astype(bf16).reshape(seqs, tokens, width)

    out_wide = out_grad.reshape(rows, width).astype(f32)
    second_grad, gain_two, bias_two = layer_norm_back(out_wide, hat_two, scale_two, norm_params[2])
    f_grad = second_grad.astype(bf16)
    hidden_grad = dot_nt(f_grad, w_down)
    gate_grad = (hidden_grad * up * (cdf + gate * density)).astype(bf16)
    up_grad = (hidden_grad * (gate * cdf)).astype(bf16)
    y1_grad = second_grad + dot_nt(gate_grad, w_gate) + dot_nt(up_grad, w_up)
    first_grad, gain_one, bias_one = layer_norm_back(y1_grad, hat_one, scale_one, norm_params[0])
    a_grad = first_grad.astype(bf16)
    rest_grads = jnp.concatenate(
        [dot_tn(o, a_grad).astype(bf16), dot_tn(y_low, gate_grad).astype(bf16), dot_tn(y_low, up_grad).astype(bf16)]
        + [dot_tn(hidden[:, g * width : (g + 1) * width], f_grad).astype(bf16) for g in range(groups)],
        axis=1,
    )
    rest_sums = lax.psum_scatter(rest_grads, "ctx", scatter_dimension=0, tiled=True)

    o_grad = dot_nt(a_grad, w_out).astype(bf16)
    dsum = jnp.sum((o.astype(f32) * o_grad.astype(f32)).reshape(seqs, tokens, heads // 2, 2, width // heads), axis=-1)
    dsum = jnp.transpose(dsum, (0, 2, 3, 1))
    dq, dk, dv = attend_bwd(windows, slopes2, q, kv, o_grad.reshape(seqs, tokens, width), lo, hi, lse, dsum)

    xe = x_ext.reshape(seqs * keys, width)
    dk_flat, dv_flat = dk.reshape(seqs * keys, width), dv.reshape(seqs * keys, width)
    first_grads = jnp.concatenate(
        [dot_tn(x, dq.reshape(rows, width)).astype(bf16), dot_tn(xe, dk_flat).astype(bf16), dot_tn(xe, dv_flat).astype(bf16)],
        axis=1,
    )
    first_sums = lax.psum_scatter(first_grads, "ctx", scatter_dimension=0, tiled=True)

    key_part = (dot_nt(dk_flat, w_kv[:, :width]) + dot_nt(dv_flat, w_kv[:, width:])).reshape(seqs, keys, width)
    input_grad = first_grad.reshape(seqs, tokens, width) + dot_nt(dq.reshape(rows, width), w_q).reshape(seqs, tokens, width)
    input_grad = input_grad + key_part[:, REACH : REACH + tokens]
    for n in range(pieces):
        to_left = key_part[:, n * tokens : (n + 1) * tokens].astype(bf16)
        to_right = key_part[:, REACH + (n + 1) * tokens : REACH + (n + 2) * tokens].astype(bf16)
        input_grad = input_grad + shifted(to_left, "ctx", n - pieces).astype(f32)
        input_grad = input_grad + shifted(to_right, "ctx", n + 1).astype(f32)

    small = jnp.concatenate(
        [jnp.stack([gain_one, bias_one, gain_two, bias_two]), jnp.pad(peak, (0, width - heads))[None], jnp.zeros((3, width), f32)]
    )
    is_peak = (jnp.arange(8) == 4)[:, None]
    for axis in ("ctx", "seq"):
        bit = 1
        while bit < lax.axis_size(axis):
            other = swapped(small, axis, bit)
            small = jnp.where(is_peak, jnp.maximum(small, other), small + other)
            bit *= 2
    norm_grads = small[:4]
    factors = clip_level / jnp.maximum(small[4, :heads], clip_level)
    column_scale = jnp.repeat(jnp.sqrt(factors), width // heads)[None, :]
    correction = 1.0 - 0.5**STEP

    def owned(columns, lowest):
        count = columns.shape[1] // width
        local = unit_of - lowest
        local = jnp.where((local >= 0) & (local < count), local, -1)
        if owner_count == 2:
            keep = to_slots(lax.dynamic_slice_in_dim(local, me * slots, slots, 0), columns, slots, width)
            give = to_slots(lax.dynamic_slice_in_dim(local, (1 - me) * slots, slots, 0), columns, slots, width)
            return [keep, swapped(give, "seq", 1)]
        every = to_slots(local, columns, owner_count * slots, width)
        return [lax.psum_scatter(every, "seq", scatter_dimension=0, tiled=True)]

    parts = owned(rest_sums, 3) + owned(first_sums, 0)
    weight_grads, new_weights, new_first, new_second, weights_low = adam_slots(
        my_units, weights, first_moments, second_moments, parts, column_scale, correction, 0.5 / D**0.5
    )
    new_norms, new_norm_first, new_norm_second = adam_step(
        norm_params, norm_grads, norm_first, norm_second, correction, norm_rate
    )
    return (output, input_grad, weight_grads, norm_grads, new_weights, new_first, new_second, weights_low,
            new_norms, new_norm_first, new_norm_second, factors)


def solution(mesh):
    block = P("seq", "ctx", None)
    return jax.shard_map(
        on_device,
        mesh=mesh,
        in_specs=(block, block, P("seq", None), P(), P(), block, block, block, P(), P(), P()),
        out_specs=(block, block, block, P(), block, block, block, block, P(), P(), P(), P()),
        check_vma=False,
    )
```

time: 1630 us -> 667 us (0.41)
  waiting for transfers between devices: 634 us -> 262 us
  other arithmetic: 269 us -> 22.3 us
  matrix products: 360 us -> 169 us
  local copies, waits for them, and re-layouts: 225 us -> 39.8 us
  Pallas kernels: 0 us -> 130 us
  blocking collectives: 85.3 us -> 0 us
    all_gather x2, waiting for transfers between devices: 342 us -> 80 us  [the longest x1 49.2 us: on_device(): w_rest = lax.all_gather(picked_rest, 'ctx', axis=0, tiled=True)]
    dot_general x54 -> x23, matrix products: 360 us -> 169 us  [the longest x7 69.2 us: dot_nt(): lax.dot_general(a, b, (((1,), (1,)), ((), ())), preferred_element_type=f32)]
    reduce_scatter x2, waiting for transfers between devices: 292 us -> 130 us  [the longest x1 130 us: on_device(): lax.psum_scatter(rest_grads, 'ctx', scatter_dimension=0, tiled=True)]
    pallas_call x0 -> x9, Pallas kernels: none -> 130 us  [the longest x1 70.6 us: attend_bwd(): pl.pallas_call(bwd_kernel, grid=(pairs, seqs), in_specs=[smem, smem, tok,...]
    convert_element_type x16 -> x3, other arithmetic: 117 us -> 5.41 us  [the longest x1 3.35 us: on_device(): f_grad = second_grad.astype(bf16)]
    reduce_max x6 -> x2, other arithmetic: 60.7 us -> 0.26 us  [the longest x1 0.17 us: on_device(): peak = jnp.max(peaks, axis=(1, 2))]
    ppermute x0 -> x9, waiting for transfers between devices: none -> 51.6 us  [swapped(): return lax.ppermute(value, axis, [(i, i ^ bit) for i in range(peers)])]
    psum x1 -> x0, blocking collectives: 45.9 us -> none  [on_device(): norm_grads = lax.psum(norm_terms, ('ctx', 'seq'))]
  transfers between devices with their start and end apart: 8 -> 17, of which waited for: 4 -> 9; matrix products, arithmetic and copies ran while one was open for 6% -> 12% of each run, Pallas kernels for 0% -> 8%
where the time goes in v1:
time: 667 us; the launch traced here: 661 us
  waiting for transfers between devices  262 us (39%)
  matrix products  169 us (25%)
  Pallas kernels  130 us (19%)
  local copies, waits for them, and re-layouts  39.8 us (6%)
  starting transfers between devices  23.2 us (3%)
  other arithmetic  22.3 us (3%)
  between operations  14.8 us (2%)
    reduce_scatter x1, waiting for transfers between devices, on_device(): lax.psum_scatter(rest_grads, 'ctx', scatter_dimension=0, tiled=True)  130 us
    pallas_call x1, Pallas kernels, attend_bwd(): pl.pallas_call(bwd_kernel, grid=(pairs, seqs), in_specs=[smem, smem, tok,...  70.6 us
    dot_general x7, matrix products, dot_nt(): lax.dot_general(a, b, (((1,), (1,)), ((), ())), preferred_element_type=f32)  69.2 us
    dot_general x6, matrix products, dot_nn(): lax.dot_general(a, b, (((1,), (0,)), ((), ())), preferred_element_type=f32)  53.5 us
    ppermute x9, waiting for transfers between devices, swapped(): return lax.ppermute(value, axis, [(i, i ^ bit) for i in range(peers)])  51.6 us
    all_gather x1, waiting for transfers between devices, on_device(): w_rest = lax.all_gather(picked_rest, 'ctx', axis=0, tiled=True)  49.2 us
    pallas_call x1, Pallas kernels, attend_fwd(): pl.pallas_call(fwd_kernel, grid=(pairs, seqs), in_specs=[smem, smem, pl.B...  48.8 us
    dot_general x10, matrix products, dot_tn(): lax.dot_general(a, b, (((0,), (0,)), ((), ())), preferred_element_type=f32)  46.7 us
  transfers between devices with their start and end apart: 17, of which 9 were waited for; matrix products, arithmetic and copies ran while one was open for 12% of the time, Pallas kernels for 8%

profile of v1, /device:TPU:0, one launch (start us, length us, event | category | flops | bytes accessed | tf_op | source)
XLA Modules:
  0.0 661.3 jit_solution(9718328956059145389)
XLA Ops:
  11.5 3.0 collective-permute-start.1
  15.2 4.7 collective-permute-done.1
  22.6 14.3 %collective-permute-done.refs_1_ = bf16[9,48,768]{2,1,0:T(8,128)(2,1)S(1)} collective-permute-done((bf16[9,48,768]{2,1,0:T(8,128)(2,1)S(1)}, bf16[9,48,768]{2,1,0:T(8,128)(2,1)S(1)}, u32[]{:S(2)}, u32[]{:S(2)}) %collective-permute-start) | collective-permute-done | bytes 663584 | tf_op jit(solution)/shard_map/ppermute | solution.py:226
  38.6 30.9 %all-gather.3.cloned.1.call-done = bf16[768,2304]{1,0:T(8,128)(2,1)} async-done(((bf16[48,2304]{1,0:T(8,128)(2,1)}), bf16[768,2304]{1,0:T(8,128)(2,1)}) %all-gather.3.cloned.1.call-update) | async-done | bytes 3538960 | tf_op jit(solution)/shard_map/all_gather | solution.py:385
  69.6 3.4 collective-permute-start.2
  77.1 2.7 constant_dynamic-update-slice_fusion.2
  81.1 3.2 constant_dynamic-update-slice_fusion
  84.3 2.6 fusion.63
  88.6 10.5 %convolution_convert_fusion = bf16[3072,1536]{1,0:T(8,128)(2,1)S(1)} fusion(bf16[3072,768]{1,0:T(8,128)(2,1)} %bitcast.5, bf16[768,2304]{1,0:T(8,128)(2,1)} %all-gather.3.cloned.1.call-done), kind=kOutput, calls=%fused_computation.10 | convolution fusion | flops 7252475904 | bytes 16515072 | tf_op jit(solution)/shard_map/dot_general | solution.py:25
  99.1 48.8 %attend_fwd.1 = (bf16[2,512,768]{2,1,0:T(8,128)(2,1)S(1)}, f32[2,6,2,512]{3,2,1,0:T(2,128)S(1)}, f32[12,8,256]{2,1,0:T(8,128)S(1)}) custom-call(s32[12]{0:T(128)S(1)} %copy-done.10, f32[12]{0:T(128)S(1)} %power_multiply_fusion.slope_ref, bf16[2,512,768]{2,1,0:T(8,128)(2,1)S(1)} %bitcast.84, bf16[2,1536,1536]{2,1,0:T(8,128)(2,1)S(1)} %bitcast.90, ...), custom_call_target="tpu_custom_call" | custom-call | flops 20000000000 | bytes 10000000 | tf_op jit(solution)/shard_map/attend_fwd/pallas_call | solution.py:106
  147.9 3.5 copy-done.11
  151.4 49.2 %all-gather.5.cloned.1.call-done = bf16[768,9984]{1,0:T(8,128)(2,1)} async-done(((bf16[48,9984]{1,0:T(8,128)(2,1)}), bf16[768,9984]{1,0:T(8,128)(2,1)}) %all-gather.5.cloned.1.call-update) | async-done | bytes 15335440 | tf_op jit(solution)/shard_map/all_gather | solution.py:388
  200.6 3.4 fusion.94
  208.0 2.3 fusion.90
  210.6 8.3 %fusion.14 = f32[1024,3072]{1,0:T(8,128)} fusion(bf16[1024,768]{1,0:T(8,128)(2,1)S(1)} %fusion.26, bf16[768,9984]{1,0:T(8,128)(2,1)S(1)} %copy-done.22), kind=kOutput, calls=%fused_computation.25 | convolution fusion | flops 4831838208 | bytes 18874368 | tf_op jit(solution)/shard_map/dot_general | solution.py:25
  218.9 17.0 %multiply_convert_fusion.1 = (bf16[1024,3072]{1,0:T(8,128)(2,1)}, f32[1024,3072]{1,0:T(8,128)}, f32[1024,3072]{1,0:T(8,128)}) fusion(f32[1024,3072]{1,0:T(8,128)} %fusion.14, bf16[1024,768]{1,0:T(8,128)(2,1)} %copy-done.20, bf16[768,9984]{1,0:T(8,128)(2,1)} %all-gather.5.cloned.1.call-done), kind=kOutput, calls=%fused_computation.8 | convolution fusion | flops 4850712576 | bytes 50331648 | tf_op jit(solution)/shard_map/dot_general | solution.py:25
  235.9 11.6 %fusion.95 = (f32[1024]{0:T(1024)S(1)}, f32[1024,768]{1,0:T(8,128)S(1)}) fusion(bf16[1024,3072]{1,0:T(8,128)(2,1)} %get-tuple-element.60, bf16[768,768]{1,0:T(8,128)(2,1)} %get-tuple-element.63, bf16[768,768]{1,0:T(8,128)(2,1)} %get-tuple-element.64, bf16[768,768]{1,0:T(8,128)(2,1)} %get-tuple-element.65, bf16[768,768]{1,0:T(8,128)(2,1)} %get-tuple-element.62, ...), kind=kOutput, calls=%fused_computation.151 | convolution fusion | flops 4855430144 | bytes 17319936 | tf_op jit(solution)/shard_map/dot_general | solution.py:25
  250.7 3.4 fusion.87
  254.0 23.6 %fusion.5 = (bf16[1024,3072]{1,0:T(8,128)(2,1)}, bf16[1024,3072]{1,0:T(8,128)(2,1)}) fusion(f32[1024,3072]{1,0:T(8,128)} %fusion.14, f32[1024,3072]{1,0:T(8,128)} %get-tuple-element.81, f32[1024,3072]{1,0:T(8,128)} %get-tuple-element.61, bf16[1024,768]{1,0:T(8,128)(2,1)} %get-tuple-element.58, bf16[768,768]{1,0:T(8,128)(2,1)} %get-tuple-element.63, ...), kind=kOutput, calls=%fused_computation.6 | convolution fusion | flops 4891607040 | bytes 56623104 | tf_op jit(solution)/shard_map/dot_general | solution.py:22
  277.7 9.9 %fusion.8 = f32[1024,768]{1,0:T(8,128)} fusion(bf16[1024,3072]{1,0:T(8,128)(2,1)} %get-tuple-element.67, bf16[768,9984]{1,0:T(8,128)(2,1)} %all-gather.5.cloned.1.call-done), kind=kOutput, calls=%fused_computation.19 | convolution fusion | flops 4831838208 | bytes 14155776 | tf_op jit(solution)/shard_map/dot_general | solution.py:22
  287.6 9.6 %multiply_reduce_fusion = (f32[768]{0:T(1024)S(1)}, f32[1024]{0:T(1024)S(1)}, f32[1024]{0:T(1024)S(1)}, f32[768]{0:T(1024)S(1)}, f32[1024,768]{1,0:T(8,128)S(1)}) fusion(f32[1024,768]{1,0:T(8,128)S(1)} %copy-done.15, f32[1024]{0:T(1024)S(1)} %add_rsqrt_fusion.1, f32[1024]{0:T(1024)S(1)} %broadcast_multiply_fusion.4, f32[768]{0:T(1024)S(1)} %get-tuple-element.50, ...), kind=kOutput, calls=%fused_computation.42 | convolution fusion | flops 4840484864 | bytes 23618560 | tf_op jit(solution)/shard_map/dot_general | solution.py:22
  298.2 5.8 convert_multiply_fusion.1
  304.1 3.5 copy.64
  307.6 5.6 reshape.152
  313.2 2.7 reduce_sum.155
  317.4 70.6 %attend_bwd.1 = (bf16[2,512,768]{2,1,0:T(8,128)(2,1)S(1)}, bf16[2,1536,768]{2,1,0:T(8,128)(2,1)S(1)}, bf16[2,1536,768]{2,1,0:T(8,128)(2,1)S(1)}) custom-call(s32[12]{0:T(128)S(1)} %copy-done.10, f32[12]{0:T(128)S(1)} %power_multiply_fusion.slope_ref, bf16[2,512,768]{2,1,0:T(8,128)(2,1)S(1)} %bitcast.85, bf16[2,1536,1536]{2,1,0:T(8,128)(2,1)} %bitcast.92, ...), custom_call_target="tpu_custom_call" | custom-call | flops 49999998976 | bytes 20000000 | tf_op jit(solution)/shard_map/attend_bwd/pallas_call | solution.py:196
  390.1 7.2 %bitcast_convert_fusion.1 = bf16[768,768]{1,0:T(8,128)(2,1)S(1)} fusion(bf16[2,1536,768]{2,1,0:T(8,128)(2,1)} %constant_dynamic-update-slice_fusion, bf16[2,1536,768]{2,1,0:T(8,128)(2,1)S(1)} %get-tuple-element.30), kind=kOutput, calls=%fused_computation.58 | convolution fusion | flops 3624468480 | bytes 10616832 | tf_op jit(solution)/shard_map/dot_general | solution.py:340
  397.3 6.2 bitcast_convert_fusion
  403.5 1.9 pad_maximum_fusion.1
  406.9 4.6 fusion.62
  411.5 10.3 %fusion.7 = bf16[768,9984]{1,0:T(8,128)(2,1)} fusion(bf16[768,9984]{1,0:T(8,128)(2,1)} %fusion.62, bf16[1024,768]{1,0:T(8,128)(2,1)S(1)} %copy-done.21, bf16[1024,3072]{1,0:T(8,128)(2,1)} %get-tuple-element.66), kind=kOutput, calls=%fused_computation.17 | convolution fusion | flops 4834197504 | bytes 12582912 | tf_op jit(solution)/shard_map/dot_general | solution.py:340
  421.8 6.9 %fusion.6 = bf16[768,9984]{1,0:T(8,128)(2,1)} fusion(bf16[768,9984]{1,0:T(8,128)(2,1)} %fusion.7, bf16[1024,768]{1,0:T(8,128)(2,1)S(1)} %copy-done.21, bf16[1024,3072]{1,0:T(8,128)(2,1)S(1)} %bitcast.107), kind=kOutput, calls=%fused_computation.15 | convolution fusion | flops 4834197504 | bytes 12582912 | tf_op jit(solution)/shard_map/dot_general | solution.py:340
  428.7 2.6 fusion.41
  431.2 2.5 fusion.47
  433.7 2.5 fusion.53
  436.3 2.5 fusion.59
  440.1 6.4 fusion.67
  446.6 6.4 convolution_add_fusion
  453.5 3.0 copy-done.17
  457.3 1.9 fusion.91
  460.5 4.2 collective-permute-start.5
  465.5 21.3 %collective-permute-done.8 = f32[8,768]{1,0:T(8,128)S(1)} collective-permute-done((f32[8,768]{1,0:T(8,128)S(1)}, f32[8,768]{1,0:T(8,128)S(1)}, u32[]{:S(2)}, u32[]{:S(2)}) %collective-permute-start.8) | collective-permute-done | bytes 24608 | tf_op jit(solution)/shard_map/ppermute | solution.py:226
  488.7 2.9 collective-permute-done.9
  493.3 2.2 collective-permute-done.10
  500.2 130.0 %reduce-scatter.3.cloned.1.call-done.col_ref = bf16[48,9984]{1,0:T(8,128)(2,1)} async-done(((bf16[768,9984]{1,0:T(8,128)(2,1)}), bf16[48,9984]{1,0:T(8,128)(2,1)}) %reduce-scatter.3.cloned.1.call-update) | async-done | bytes 958480 | tf_op jit(solution)/shard_map/reduce_scatter | solution.py:443
  633.7 7.5 %fusion.17 = f32[2,512,768]{2,1,0:T(8,128)} fusion(f32[2,1536,768]{2,1,0:T(8,128)} %bitcast.100, bf16[2,512,768]{2,1,0:T(8,128)(2,1)} %collective-permute-done.5, bf16[2,512,768]{2,1,0:T(8,128)(2,1)} %collective-permute-done.4, f32[2,512,768]{2,1,0:T(8,128)} %bitcast.96, bf16[2,512,768]{2,1,0:T(8,128)(2,1)S(1)} %get-tuple-element.29, ...), kind=kOutput, calls=%fused_computation.30 | convolution fusion | flops 1212678144 | bytes 15335424 | tf_op jit(solution)/shard_map/dot_general | solution.py:22
  642.6 6.2 collective-permute-done.11.refs_1_
  648.8 5.5 adam_slots.1
  (175 shorter events, 47.5 us)
Async XLA Ops:
  7.2 62.3 %all-gather.3.cloned.1.call-start = ((), (), s32[]{:S(2)}) async-start(), calls=%async_computation.2 | async-start | bytes 3760128 | tf_op jit(solution)/shard_map/all_gather | solution.py:385
  9.3 64.9 %copy-start.28 = (s32[2,8192]{1,0:T(2,128)S(1)}, s32[2,8192]{1,0:T(2,128)}, u32[]{:S(2)}) copy-start(s32[2,8192]{1,0:T(2,128)} %param.14) | copy-start | bytes 196612
  9.3 66.4 %copy-start.29 = (f32[4,768]{1,0:T(4,128)S(1)}, f32[4,768]{1,0:T(4,128)}, u32[]{:S(2)}) copy-start(f32[4,768]{1,0:T(4,128)} %param.20) | copy-start | bytes 36868
  9.4 66.4 %copy-start.18 = (bf16[2,512,768]{2,1,0:T(8,128)(2,1)S(1)}, bf16[2,512,768]{2,1,0:T(8,128)(2,1)}, u32[]{:S(2)}) copy-start(bf16[2,512,768]{2,1,0:T(8,128)(2,1)} %param.13) | copy-start | bytes 4718596
  11.5 8.4 %collective-permute-start.1 = (bf16[48,2304]{1,0:T(8,128)(2,1)S(1)}, bf16[48,2304]{1,0:T(8,128)(2,1)S(1)}, u32[]{:S(2)}, u32[]{:S(2)}) collective-permute-start(bf16[48,2304]{1,0:T(8,128)(2,1)S(1)} %pick_units.3), channel_id=1, source_target_pairs={{0,1},{1,0},{2,3},{3,2},{4,5},{5,4},{6,7},{7,6},{8,9},{9,8},{10,11... | collective-permute-start | bytes 663560 | tf_op jit(solution)/shard_map/ppermute | solution.py:226
  20.7 180.0 %all-gather.5.cloned.1.call-start = ((), (), s32[]{:S(2)}) async-start(), calls=%async_computation.3 | async-start | bytes 16293888 | tf_op jit(solution)/shard_map/all_gather | solution.py:388
  20.7 16.2 %collective-permute-start = (bf16[9,48,768]{2,1,0:T(8,128)(2,1)S(1)}, bf16[9,48,768]{2,1,0:T(8,128)(2,1)S(1)}, u32[]{:S(2)}, u32[]{:S(2)}) collective-permute-start(bf16[9,48,768]{2,1,0:T(8,128)(2,1)S(1)} %convert_element_type.109.refs_0_), channel_id=1, source_target_pairs={{0,1},{1,0},{2,3},{3,2},{4,5},{5,4},{6,7},{7,6},{8,9},{9,8},{10,11... | collective-permute-start | bytes 1990664 | tf_op jit(solution)/shard_map/ppermute | solution.py:226
  38.6 41.2 %copy-start.25 = (bf16[2,512,768]{2,1,0:T(8,128)(2,1)S(1)}, bf16[2,512,768]{2,1,0:T(8,128)(2,1)}, u32[]{:S(2)}) copy-start(bf16[2,512,768]{2,1,0:T(8,128)(2,1)} %param.12) | copy-start | bytes 4718596
  69.5 427.4 %reduce-scatter.5.cloned.1.call-start = ((), (), s32[]{:S(2)}) async-start(), calls=%async_computation.5 | async-start | bytes 3760128 | tf_op jit(solution)/shard_map/reduce_scatter | solution.py:456
  69.6 7.5 %collective-permute-start.2 = (bf16[2,512,768]{2,1,0:T(8,128)(2,1)}, bf16[2,512,768]{2,1,0:T(8,128)(2,1)}, u32[]{:S(2)}, u32[]{:S(2)}) collective-permute-start(bf16[2,512,768]{2,1,0:T(8,128)(2,1)} %param.12), channel_id=1, source_target_pairs={{0,2},{2,4},{4,6},{6,8},{8,10},{10,12},{12,14},{14,16},{16,18},{18... | collective-permute-start | bytes 4718600 | tf_op jit(solution)/shard_map/ppermute | solution.py:221
  72.9 8.1 %collective-permute-start.3 = (bf16[2,512,768]{2,1,0:T(8,128)(2,1)}, bf16[2,512,768]{2,1,0:T(8,128)(2,1)}, u32[]{:S(2)}, u32[]{:S(2)}) collective-permute-start(bf16[2,512,768]{2,1,0:T(8,128)(2,1)} %param.12), channel_id=1, source_target_pairs={{2,0},{4,2},{6,4},{8,6},{10,8},{12,10},{14,12},{16,14},{18,16},{20... | collective-permute-start | bytes 4718600 | tf_op jit(solution)/shard_map/ppermute | solution.py:221
  79.8 4.5 copy-start.27
  88.6 10.5 %copy-start.10 = (s32[12]{0:T(128)S(1)}, s32[12]{0:T(128)}, u32[]{:S(2)}) copy-start(s32[12]{0:T(128)} %win_ref.3) | copy-start | bytes 148
  147.9 3.5 copy-start.11
  151.4 146.8 %copy-start.3 = (bf16[2,512,768]{2,1,0:T(8,128)(2,1)}, bf16[2,512,768]{2,1,0:T(8,128)(2,1)S(1)}, u32[]{:S(2)}) copy-start(bf16[2,512,768]{2,1,0:T(8,128)(2,1)S(1)} %get-tuple-element.26) | copy-start | bytes 4718596
  200.6 7.3 %copy-start.22 = (bf16[768,9984]{1,0:T(8,128)(2,1)S(1)}, bf16[768,9984]{1,0:T(8,128)(2,1)}, u32[]{:S(2)}) copy-start(bf16[768,9984]{1,0:T(8,128)(2,1)} %all-gather.5.cloned.1.call-done) | copy-start | bytes 46006276
  208.0 2.6 copy-start.20
  277.7 10.0 %copy-start.15 = (f32[1024,768]{1,0:T(8,128)S(1)}, f32[1024,768]{1,0:T(8,128)}, u32[]{:S(2)}) copy-start(f32[1024,768]{1,0:T(8,128)} %copy-done.14) | copy-start | bytes 9437188
  277.7 9.9 %copy-start.23 = (f32[1024,768]{1,0:T(8,128)S(1)}, f32[1024,768]{1,0:T(8,128)}, u32[]{:S(2)}) copy-start(f32[1024,768]{1,0:T(8,128)} %get-tuple-element.59) | copy-start | bytes 9437188
  277.7 9.9 %copy-start.36 = (bf16[1024,3072]{1,0:T(8,128)(2,1)S(1)}, bf16[1024,3072]{1,0:T(8,128)(2,1)}, u32[]{:S(2)}) copy-start(bf16[1024,3072]{1,0:T(8,128)(2,1)} %get-tuple-element.66) | copy-start | bytes 18874372
  298.2 5.8 copy-start.16
  317.4 70.6 %copy-start.26 = (bf16[2,512,768]{2,1,0:T(8,128)(2,1)S(1)}, bf16[2,512,768]{2,1,0:T(8,128)(2,1)}, u32[]{:S(2)}) copy-start(bf16[2,512,768]{2,1,0:T(8,128)(2,1)} %param.12) | copy-start | bytes 4718596
  388.0 9.3 %copy-start.12 = (bf16[2,1536,768]{2,1,0:T(8,128)(2,1)}, bf16[2,1536,768]{2,1,0:T(8,128)(2,1)S(1)}, u32[]{:S(2)}) copy-start(bf16[2,1536,768]{2,1,0:T(8,128)(2,1)S(1)} %get-tuple-element.31) | copy-start | bytes 14155780
  405.5 224.7 %reduce-scatter.3.cloned.1.call-start = ((), (), s32[]{:S(2)}) async-start(), calls=%async_computation.4 | async-start | bytes 16293888 | tf_op jit(solution)/shard_map/reduce_scatter | solution.py:443
  406.9 4.6 copy-start.21
  406.9 14.9 %slice-start.2 = ((s8[6291456]{0:T(1024)(128)(4,1)}), s8[4194304]{0:T(1024)(128)(4,1)S(1)}, s32[]{:S(2)}) async-start(s8[6291456]{0:T(1024)(128)(4,1)} %bitcast.106), calls=%async_computation.8 | async-start | bytes 8388608
  411.5 10.3 %slice-start.3 = ((s8[6291456]{0:T(1024)(128)(4,1)}), s8[2097152]{0:T(1024)(128)(4,1)S(1)}, s32[]{:S(2)}) async-start(s8[6291456]{0:T(1024)(128)(4,1)} %bitcast.106), calls=%async_computation.9 | async-start | bytes 4194304
  411.5 17.2 %slice-start = ((s8[6291456]{0:T(1024)(128)(4,1)}), s8[4194304]{0:T(1024)(128)(4,1)S(1)}, s32[]{:S(2)}) async-start(s8[6291456]{0:T(1024)(128)(4,1)} %bitcast.97), calls=%async_computation.6 | async-start | bytes 8388608
  421.7 6.9 %slice-start.1 = ((s8[6291456]{0:T(1024)(128)(4,1)}), s8[2097152]{0:T(1024)(128)(4,1)S(1)}, s32[]{:S(2)}) async-start(s8[6291456]{0:T(1024)(128)(4,1)} %bitcast.97), calls=%async_computation.7 | async-start | bytes 4194304
  421.7 6.9 %copy-start.24 = (bf16[1024,768]{1,0:T(8,128)(2,1)S(1)}, bf16[1024,768]{1,0:T(8,128)(2,1)}, u32[]{:S(2)}) copy-start(bf16[1024,768]{1,0:T(8,128)(2,1)} %get-tuple-element.58) | copy-start | bytes 4718596
  439.8 16.7 %collective-permute-start.6 = (f32[8,768]{1,0:T(8,128)S(1)}, f32[8,768]{1,0:T(8,128)S(1)}, u32[]{:S(2)}, u32[]{:S(2)}) collective-permute-start(f32[8,768]{1,0:T(8,128)S(1)} %concatenate.17), channel_id=1, source_target_pairs={{0,2},{2,0},{4,6},{6,4},{8,10},{10,8},{12,14},{14,12},{16,18},{18,... | collective-permute-start | bytes 73736 | tf_op jit(solution)/shard_map/ppermute | solution.py:226
  453.0 3.5 copy-start.17
  456.6 39.7 %copy-start.30 = (f32[4,768]{1,0:T(4,128)S(1)}, f32[4,768]{1,0:T(4,128)}, u32[]{:S(2)}) copy-start(f32[4,768]{1,0:T(4,128)} %param.20) | copy-start | bytes 36868
  456.6 39.7 %copy-start.33 = (f32[4,768]{1,0:T(4,128)S(1)}, f32[4,768]{1,0:T(4,128)}, u32[]{:S(2)}) copy-start(f32[4,768]{1,0:T(4,128)} %param.21) | copy-start | bytes 36868
  456.6 39.7 %copy-start.34 = (f32[4,768]{1,0:T(4,128)S(1)}, f32[4,768]{1,0:T(4,128)}, u32[]{:S(2)}) copy-start(f32[4,768]{1,0:T(4,128)} %param.22) | copy-start | bytes 36868
  456.6 8.1 %collective-permute-start.7 = (f32[8,768]{1,0:T(8,128)S(1)}, f32[8,768]{1,0:T(8,128)S(1)}, u32[]{:S(2)}, u32[]{:S(2)}) collective-permute-start(f32[8,768]{1,0:T(8,128)S(1)} %add_select_fusion.4), channel_id=1, source_target_pairs={{0,4},{2,6},{4,0},{6,2},{8,12},{10,14},{12,8},{14,10},{16,20},{18,... | collective-permute-start | bytes 73736 | tf_op jit(solution)/shard_map/ppermute | solution.py:226
  459.2 174.4 %collective-permute-start.4 = (bf16[2,512,768]{2,1,0:T(8,128)(2,1)}, bf16[2,512,768]{2,1,0:T(8,128)(2,1)}, u32[]{:S(2)}, u32[]{:S(2)}) collective-permute-start(bf16[2,512,768]{2,1,0:T(8,128)(2,1)} %get-tuple-element.68), channel_id=1, source_target_pairs={{2,0},{4,2},{6,4},{8,6},{10,8},{12,10},{14,12},{16,14},{18,16},{20... | collective-permute-start | bytes 4718600 | tf_op jit(solution)/shard_map/ppermute | solution.py:221
  460.5 173.2 %collective-permute-start.5 = (bf16[2,512,768]{2,1,0:T(8,128)(2,1)}, bf16[2,512,768]{2,1,0:T(8,128)(2,1)}, u32[]{:S(2)}, u32[]{:S(2)}) collective-permute-start(bf16[2,512,768]{2,1,0:T(8,128)(2,1)} %get-tuple-element.69), channel_id=1, source_target_pairs={{0,2},{2,4},{4,6},{6,8},{8,10},{10,12},{12,14},{14,16},{16,18},{18... | collective-permute-start | bytes 4718600 | tf_op jit(solution)/shard_map/ppermute | solution.py:221
  464.8 22.0 %collective-permute-start.8 = (f32[8,768]{1,0:T(8,128)S(1)}, f32[8,768]{1,0:T(8,128)S(1)}, u32[]{:S(2)}, u32[]{:S(2)}) collective-permute-start(f32[8,768]{1,0:T(8,128)S(1)} %add_select_fusion.3), channel_id=1, source_target_pairs={{0,8},{2,10},{4,12},{6,14},{8,0},{10,2},{12,4},{14,6},{16,24},{18,... | collective-permute-start | bytes 73736 | tf_op jit(solution)/shard_map/ppermute | solution.py:226
  486.9 4.7 collective-permute-start.9
  491.7 3.8 collective-permute-start.10
  498.6 144.0 %collective-permute-start.12 = (bf16[9,48,768]{2,1,0:T(8,128)(2,1)S(1)}, bf16[9,48,768]{2,1,0:T(8,128)(2,1)S(1)}, u32[]{:S(2)}, u32[]{:S(2)}) collective-permute-start(bf16[9,48,768]{2,1,0:T(8,128)(2,1)S(1)} %to_slots.7), channel_id=1, source_target_pairs={{0,1},{1,0},{2,3},{3,2},{4,5},{5,4},{6,7},{7,6},{8,9},{9,8},{10,11... | collective-permute-start | bytes 1990664 | tf_op jit(solution)/shard_map/ppermute | solution.py:226
  632.1 16.7 %collective-permute-start.11 = (bf16[9,48,768]{2,1,0:T(8,128)(2,1)S(1)}, bf16[9,48,768]{2,1,0:T(8,128)(2,1)S(1)}, u32[]{:S(2)}, u32[]{:S(2)}) collective-permute-start(bf16[9,48,768]{2,1,0:T(8,128)(2,1)S(1)} %to_slots.5), channel_id=1, source_target_pairs={{0,1},{1,0},{2,3},{3,2},{4,5},{5,4},{6,7},{7,6},{8,9},{9,8},{10,11... | collective-permute-start | bytes 1990664 | tf_op jit(solution)/shard_map/ppermute | solution.py:226
  633.6 7.5 %copy-start.9 = (bf16[48,2304]{1,0:T(8,128)(2,1)S(1)}, bf16[48,2304]{1,0:T(8,128)(2,1)}, u32[]{:S(2)}) copy-start(bf16[48,2304]{1,0:T(8,128)(2,1)} %reduce-scatter.5.cloned.1.call-done.col_ref) | copy-start | bytes 663556
  633.6 8.2 %copy-start.2 = (bf16[48,9984]{1,0:T(8,128)(2,1)S(1)}, bf16[48,9984]{1,0:T(8,128)(2,1)}, u32[]{:S(2)}) copy-start(bf16[48,9984]{1,0:T(8,128)(2,1)} %reduce-scatter.3.cloned.1.call-done.col_ref) | copy-start | bytes 2875396
  633.7 15.1 %copy-start.6 = (f32[9,48,768]{2,1,0:T(8,128)S(1)}, f32[9,48,768]{2,1,0:T(8,128)}, u32[]{:S(2)}) copy-start(f32[9,48,768]{2,1,0:T(8,128)} %m_ref.1) | copy-start | bytes 3981316
  633.7 15.1 %copy-start.7 = (f32[9,48,768]{2,1,0:T(8,128)S(1)}, f32[9,48,768]{2,1,0:T(8,128)}, u32[]{:S(2)}) copy-start(f32[9,48,768]{2,1,0:T(8,128)} %v_ref.1) | copy-start | bytes 3981316
  641.2 7.6 %copy-start = (f32[9,48,768]{2,1,0:T(8,128)S(1)}, f32[9,48,768]{2,1,0:T(8,128)}, u32[]{:S(2)}) copy-start(f32[9,48,768]{2,1,0:T(8,128)} %w_ref.1) | copy-start | bytes 3981316
  (10 other events, 12.5 us)
Sparse Core Ops, SparseCore 0:
  20.8 48.6 all-gather.2
  72.4 128.2 all-gather.4
  405.6 68.1 reduce-scatter.4
  477.7 152.4 reduce-scatter.2

commit v2 on v1

--- a/solution.py
+++ b/solution.py
@@ -135,7 +135,7 @@
         name="attend_fwd",
     )(windows, slopes2, q, kv, kv, lo, hi)
 
-def bwd_kernel(win_ref, slope_ref, q_ref, k_ref, v_ref, do_ref, lo_ref, hi_ref, lse_ref, dsum_ref,
+def bwd_kernel(win_ref, slope_ref, q_ref, k_ref, v_ref, do_ref, o_ref, lo_ref, hi_ref, lse_ref,
                dq_ref, dk_ref, dv_ref, kt_ref, dqt_ref, dka_ref, dva_ref, bias_ref):
     pair = pl.program_id(0)
     seq = pl.program_id(1)
@@ -145,6 +145,7 @@
     dva_ref[...] = jnp.zeros(dva_ref.shape, f32)
     rows = lax.broadcasted_iota(jnp.int32, (QB, QB), 0)
     lane = lax.broadcasted_iota(jnp.int32, (1, 128), 1)
+    ones = jnp.ones((16, 128), bf16)
     for h in range(2):
         head = pair * 2 + h
         @pl.when(seq == 0)
@@ -158,7 +159,10 @@
             q = (q_ref[0, pl.ds(qb * QB, QB), :].astype(f32) * qmask).astype(bf16)
             do = (do_ref[0, pl.ds(qb * QB, QB), :].astype(f32) * dmask).astype(bf16)
             lse = lse_ref[0, 0, pl.ds(h, 1), pl.ds(qb * QB, QB)]
-            dsum = dsum_ref[0, 0, pl.ds(h, 1), pl.ds(qb * QB, QB)]
+            prod = do.astype(f32) * o_ref[0, pl.ds(qb * QB, QB), :].astype(f32)
+            prod_hi = prod.astype(bf16)
+            prod_lo = (prod - prod_hi.astype(f32)).astype(bf16)
+            dsum = (dot_nt(ones, prod_hi) + dot_nt(ones, prod_lo))[:1]
 
             def branch(c):
                 first = REACH - c * 128
@@ -184,7 +188,7 @@
     dk_ref[0] = dka_ref[...].astype(bf16)
     dv_ref[0] = dva_ref[...].astype(bf16)
 
-def attend_bwd(windows, slopes2, q, kv, do, lo, hi, lse, dsum):
+def attend_bwd(windows, slopes2, q, kv, do, o, lo, hi, lse):
     seqs, tokens, width = q.shape
     keys = kv.shape[1]
     pairs = width // 128
@@ -196,7 +200,7 @@
     return pl.pallas_call(
         bwd_kernel,
         grid=(pairs, seqs),
-        in_specs=[smem, smem, tok, key, pl.BlockSpec((1, keys, 128), lambda p, s: (s, 0, p + pairs)), tok, row, row, stat, stat],
+        in_specs=[smem, smem, tok, key, pl.BlockSpec((1, keys, 128), lambda p, s: (s, 0, p + pairs)), tok, tok, row, row, stat],
         out_specs=[tok, key, key],
         out_shape=[
             jax.ShapeDtypeStruct((seqs, tokens, width), bf16),
@@ -213,7 +217,7 @@
         compiler_params=pltpu.CompilerParams(vmem_limit_bytes=40 * 2**20),
         cost_estimate=pl.CostEstimate(flops=5 * 10**10, bytes_accessed=2 * 10**7, transcendentals=10**7),
         name="attend_bwd",
-    )(windows, slopes2, q, kv, kv, do, lo, hi, lse, dsum)
+    )(windows, slopes2, q, kv, kv, do, o, lo, hi, lse)
 
 def shifted(value, axis, by):
     peers = lax.axis_size(axis)
@@ -238,7 +242,25 @@
     mean_one = jnp.mean(inner, axis=-1, keepdims=True)
     mean_two = jnp.mean(inner * hat, axis=-1, keepdims=True)
     back = scale * (inner - mean_one - hat * mean_two)
-    return back, jnp.sum(grad * hat, axis=0), jnp.sum(grad, axis=0)
+    return back, jnp.sum(grad * hat, axis=0, keepdims=True), jnp.sum(grad, axis=0, keepdims=True)
+
+
+def exchange_scatter(value, axis):
+    peers = lax.axis_size(axis)
+    me = lax.axis_index(axis)
+    rows = value.shape[0] // peers
+    bit = 1
+    value = value.reshape((peers, rows) + value.shape[1:])
+    while bit < peers:
+        count = value.shape[0]
+        split = value.reshape((count // 2, 2) + value.shape[1:])
+        side = (me // bit) % 2
+        keep = lax.dynamic_index_in_dim(split, side, 1, False)
+        give = lax.dynamic_index_in_dim(split, 1 - side, 1, False)
+        got = swapped(give, axis, bit)
+        value = (keep.astype(f32) + got.astype(f32)).astype(value.dtype)
+        bit *= 2
+    return value[0]
 
 
 def pick_units(slot_of, sources, count):
@@ -346,6 +368,178 @@
     return cdf, density
 
 
+RB = 256
+CHUNK = 256
+
+
+def ffn_kernel(o_ref, x_ref, og_ref, wo_ref, wg_ref, wu_ref, wd_ref, norm_ref,
+               out_ref, first_ref, ograd_ref, small_ref, grads_ref,
+               hat_ref, scale_ref, acc_ref, a_ref, b_ref, h_ref, ylow_ref, ylowt_ref, fgrad_ref,
+               gg_ref, ug_ref, stage_g, stage_u, stage_d, stage_o, sems):
+    step = pl.program_id(0)
+    rows, width = x_ref.shape
+    chunk = wg_ref.shape[1]
+    chunks = FF // chunk
+    blocks = rows // RB
+
+    def at(i):
+        return pl.ds(i * RB, RB)
+
+    def copies(j):
+        slot = lax.rem(j, 2)
+        column = pl.multiple_of(width + j * chunk, 128)
+        per = width // chunk
+        return (
+            pltpu.make_async_copy(stage_g.at[slot], grads_ref.at[:, pl.ds(column, chunk)], sems.at[slot, 0]),
+            pltpu.make_async_copy(stage_u.at[slot], grads_ref.at[:, pl.ds(column + FF, chunk)], sems.at[slot, 1]),
+            pltpu.make_async_copy(
+                stage_d.at[slot],
+                grads_ref.at[pl.ds(pl.multiple_of(lax.rem(j, per) * chunk, 128), chunk),
+                             pl.ds(pl.multiple_of(width + 2 * FF + lax.div(j, per) * width, 128), width)],
+                sems.at[slot, 2],
+            ),
+        )
+
+    @pl.when(step == 0)
+    def _():
+        for i in range(blocks):
+            total = x_ref[at(i), :].astype(f32) + dot_nn(o_ref[at(i), :], wo_ref[...])
+            hat, scale = layer_norm(total)
+            y1 = hat * norm_ref[0:1, :] + norm_ref[1:2, :]
+            hat_ref[at(i), :] = hat
+            scale_ref[at(i), :] = scale
+            acc_ref[at(i), :] = y1
+            ylow_ref[at(i), :] = y1.astype(bf16)
+            ylowt_ref[:, at(i)] = y1.T.astype(bf16)
+
+    @pl.when(step < chunks)
+    def _():
+        for i in range(blocks):
+            y = ylow_ref[at(i), :]
+            gate = dot_nn(y, wg_ref[...])
+            up = dot_nn(y, wu_ref[...])
+            cdf, density = gelu_parts(gate)
+            a = gate * cdf
+            hidden = (a * up).astype(bf16)
+            a_ref[step, at(i), :] = a.astype(bf16)
+            b_ref[step, at(i), :] = (up * (cdf + gate * density)).astype(bf16)
+            h_ref[step, at(i), :] = hidden
+            acc_ref[at(i), :] += dot_nn(hidden, wd_ref[...])
+
+    @pl.when(step == chunks)
+    def _():
+        gain = bias = None
+        for i in range(blocks):
+            hat, scale = layer_norm(acc_ref[at(i), :])
+            out_ref[at(i), :] = (hat * norm_ref[2:3, :] + norm_ref[3:4, :]).astype(bf16)
+            grad = og_ref[at(i), :].astype(f32)
+            back, g, b = layer_norm_back(grad, hat, scale, norm_ref[2:3, :])
+            gain = g if i == 0 else gain + g
+            bias = b if i == 0 else bias + b
+            acc_ref[at(i), :] = back
+            fgrad_ref[at(i), :] = back.astype(bf16)
+        small_ref[2:3, :] = gain
+        small_ref[3:4, :] = bias
+
+    @pl.when(step >= chunks)
+    def _():
+        j = step - chunks
+        slot = lax.rem(j, 2)
+
+        @pl.when(j >= 2)
+        def _():
+            for copy in copies(j - 2):
+                copy.wait()
+
+        for i in range(blocks):
+            hidden_grad = dot_nt(fgrad_ref[at(i), :], wd_ref[...])
+            gg = (hidden_grad * b_ref[j, at(i), :].astype(f32)).astype(bf16)
+            ug = (hidden_grad * a_ref[j, at(i), :].astype(f32)).astype(bf16)
+            gg_ref[at(i), :] = gg
+            ug_ref[at(i), :] = ug
+            acc_ref[at(i), :] += dot_nt(gg, wg_ref[...]) + dot_nt(ug, wu_ref[...])
+        stage_g[slot] = dot_nn(ylowt_ref[...], gg_ref[...]).astype(bf16)
+        stage_u[slot] = dot_nn(ylowt_ref[...], ug_ref[...]).astype(bf16)
+        stage_d[slot] = dot_tn(h_ref[j], fgrad_ref[...]).astype(bf16)
+        for copy in copies(j):
+            copy.start()
+
+    @pl.when(step == 2 * chunks - 1)
+    def _():
+        gain = bias = None
+        for i in range(blocks):
+            back, g, b = layer_norm_back(acc_ref[at(i), :], hat_ref[at(i), :], scale_ref[at(i), :], norm_ref[0:1, :])
+            gain = g if i == 0 else gain + g
+            bias = b if i == 0 else bias + b
+            first_ref[at(i), :] = back
+            low = back.astype(bf16)
+            fgrad_ref[at(i), :] = low
+            ograd_ref[at(i), :] = dot_nt(low, wo_ref[...]).astype(bf16)
+        small_ref[0:1, :] = gain
+        small_ref[1:2, :] = bias
+        small_ref[4:8, :] = jnp.zeros((4, width), f32)
+        stage_o[...] = dot_tn(o_ref[...], fgrad_ref[...]).astype(bf16)
+        last = pltpu.make_async_copy(stage_o, grads_ref.at[:, pl.ds(0, width)], sems.at[2, 0])
+        last.start()
+        for j in (chunks - 2, chunks - 1):
+            for copy in copies(j):
+                copy.wait()
+        last.wait()
+
+
+def feed_forward(o, x, out_grad, w_rest, norms):
+    rows, width = x.shape
+    chunks = FF // CHUNK
+    lead = width // CHUNK
+    per = width // CHUNK
+
+    def whole(shape):
+        return pl.BlockSpec(shape, lambda s: (0,) * len(shape), pipeline_mode=pl.Buffered(1))
+
+    full = whole((rows, width))
+    return pl.pallas_call(
+        ffn_kernel,
+        grid=(2 * chunks,),
+        in_specs=[
+            full, full, full,
+            whole((width, width)),
+            pl.BlockSpec((width, CHUNK), lambda s: (0, lead + lax.rem(s, chunks))),
+            pl.BlockSpec((width, CHUNK), lambda s: (0, lead + chunks + lax.rem(s, chunks))),
+            pl.BlockSpec((CHUNK, width), lambda s: (lax.rem(lax.rem(s, chunks), per), 1 + 2 * FF // width + lax.div(lax.rem(s, chunks), per))),
+            whole(norms.shape),
+        ],
+        out_specs=[full, full, full, whole((8, width)), pl.BlockSpec(memory_space=pl.ANY)],
+        out_shape=[
+            jax.ShapeDtypeStruct((rows, width), bf16),
+            jax.ShapeDtypeStruct((rows, width), f32),
+            jax.ShapeDtypeStruct((rows, width), bf16),
+            jax.ShapeDtypeStruct((8, width), f32),
+            jax.ShapeDtypeStruct((width, w_rest.shape[1]), bf16),
+        ],
+        scratch_shapes=[
+            pltpu.VMEM((rows, width), f32),
+            pltpu.VMEM((rows, 1), f32),
+            pltpu.VMEM((rows, width), f32),
+            pltpu.VMEM((chunks, rows, CHUNK), bf16),
+            pltpu.VMEM((chunks, rows, CHUNK), bf16),
+            pltpu.VMEM((chunks, rows, CHUNK), bf16),
+            pltpu.VMEM((rows, width), bf16),
+            pltpu.VMEM((width, rows), bf16),
+            pltpu.VMEM((rows, width), bf16),
+            pltpu.VMEM((rows, CHUNK), bf16),
+            pltpu.VMEM((rows, CHUNK), bf16),
+            pltpu.VMEM((2, width, CHUNK), bf16),
+            pltpu.VMEM((2, width, CHUNK), bf16),
+            pltpu.VMEM((2, CHUNK, width), bf16),
+            pltpu.VMEM((width, width), bf16),
+            pltpu.SemaphoreType.DMA((3, 3)),
+        ],
+        compiler_params=pltpu.CompilerParams(vmem_limit_bytes=58 * 2**20),
+        cost_estimate=pl.CostEstimate(flops=46 * 10**9, bytes_accessed=6 * 10**7, transcendentals=6 * 10**6),
+        name="feed_forward",
+    )(o, x, out_grad, w_rest, w_rest, w_rest, w_rest, norms)
+
+
 def on_device(inputs, out_grad, segments, windows, owners, weights, first_moments, second_moments,
               norm_params, norm_first, norm_second):
     seqs, tokens, width = inputs.shape
@@ -368,6 +562,9 @@
     match = (owners * slots + rank)[None, :] == slot_ids[:, None]
     unit_of = jnp.max(jnp.where(match, ids[None, :], -1), axis=1)
     my_units = lax.dynamic_slice_in_dim(unit_of, me * slots, slots, 0)
+
+    left = [shifted(inputs, "ctx", pieces - n) for n in range(pieces)]
+    right = [shifted(inputs, "ctx", -(n + 1)) for n in range(pieces)]
 
     low = weights.astype(bf16)
     if owner_count == 2:
@@ -384,12 +581,8 @@
         picked_first = pick_units(place[:, :3], sources, 3)
     w_first = lax.all_gather(picked_first, "ctx", axis=0, tiled=True)
     picked_rest = pick_units(place[:, 3:], sources, rest)
-    picked_rest, w_first = lax.optimization_barrier((picked_rest, w_first))
+    picked_rest, w_first, left, right = lax.optimization_barrier((picked_rest, w_first, left, right))
     w_rest = lax.all_gather(picked_rest, "ctx", axis=0, tiled=True)
-
-    left = [shifted(inputs, "ctx", pieces - n) for n in range(pieces)]
-    right = [shifted(inputs, "ctx", -(n + 1)) for n in range(pieces)]
-    x_ext = jnp.concatenate(left + [inputs] + right, axis=1)
 
     start = lax.axis_index("ctx") * tokens
     padded = jnp.pad(segments, ((0, 0), (REACH, 0)), constant_values=-1)
@@ -400,6 +593,7 @@
     hi = jnp.sum((key_seg[:, :, None] <= query_seg[:, None, :]).astype(jnp.int32), axis=1)[:, None] - 1
     slopes2 = jnp.power(2.0, -8.0 * (jnp.arange(heads, dtype=f32) + 1.0) / heads) * LOG2E
 
+    x_ext = jnp.concatenate(left + [inputs] + right, axis=1)
     w_q, w_kv = w_first[:, :width], w_first[:, width:]
     x = inputs.reshape(rows, width)
     q = dot_nn(x, w_q).astype(bf16).reshape(seqs, tokens, width)
@@ -408,44 +602,12 @@
     peak = jnp.max(peaks, axis=(1, 2))
     o = mixed.reshape(rows, width)
 
-    w_out = w_rest[:, :width]
-    w_gate = w_rest[:, width : width + FF]
-    w_up = w_rest[:, width + FF : width + 2 * FF]
-    w_down = jnp.concatenate(
-        [w_rest[:, width + 2 * FF + g * width : width + 2 * FF + (g + 1) * width] for g in range(groups)], axis=0
+    result, first_grad, o_grad, small, rest_grads = feed_forward(
+        o, x, out_grad.reshape(rows, width), w_rest, norm_params
     )
-    first_sum = x.astype(f32) + dot_nn(o, w_out)
-    hat_one, scale_one = layer_norm(first_sum)
-    y1 = hat_one * norm_params[0] + norm_params[1]
-    y_low = y1.astype(bf16)
-    gate = dot_nn(y_low, w_gate)
-    up = dot_nn(y_low, w_up)
-    cdf, density = gelu_parts(gate)
-    hidden = (gate * cdf * up).astype(bf16)
-    second_sum = y1 + dot_nn(hidden, w_down)
-    hat_two, scale_two = layer_norm(second_sum)
-    output = (hat_two * norm_params[2] + norm_params[3]).astype(bf16).reshape(seqs, tokens, width)
-
-    out_wide = out_grad.reshape(rows, width).astype(f32)
-    second_grad, gain_two, bias_two = layer_norm_back(out_wide, hat_two, scale_two, norm_params[2])
-    f_grad = second_grad.astype(bf16)
-    hidden_grad = dot_nt(f_grad, w_down)
-    gate_grad = (hidden_grad * up * (cdf + gate * density)).astype(bf16)
-    up_grad = (hidden_grad * (gate * cdf)).astype(bf16)
-    y1_grad = second_grad + dot_nt(gate_grad, w_gate) + dot_nt(up_grad, w_up)
-    first_grad, gain_one, bias_one = layer_norm_back(y1_grad, hat_one, scale_one, norm_params[0])
-    a_grad = first_grad.astype(bf16)
-    rest_grads = jnp.concatenate(
-        [dot_tn(o, a_grad).astype(bf16), dot_tn(y_low, gate_grad).astype(bf16), dot_tn(y_low, up_grad).astype(bf16)]
-        + [dot_tn(hidden[:, g * width : (g + 1) * width], f_grad).astype(bf16) for g in range(groups)],
-        axis=1,
-    )
+    output = result.reshape(seqs, tokens, width)
     rest_sums = lax.psum_scatter(rest_grads, "ctx", scatter_dimension=0, tiled=True)
-
-    o_grad = dot_nt(a_grad, w_out).astype(bf16)
-    dsum = jnp.sum((o.astype(f32) * o_grad.astype(f32)).reshape(seqs, tokens, heads // 2, 2, width // heads), axis=-1)
-    dsum = jnp.transpose(dsum, (0, 2, 3, 1))
-    dq, dk, dv = attend_bwd(windows, slopes2, q, kv, o_grad.reshape(seqs, tokens, width), lo, hi, lse, dsum)
+    dq, dk, dv = attend_bwd(windows, slopes2, q, kv, o_grad.reshape(seqs, tokens, width), mixed, lo, hi, lse)
 
     xe = x_ext.reshape(seqs * keys, width)
     dk_flat, dv_flat = dk.reshape(seqs * keys, width), dv.reshape(seqs * keys, width)
@@ -453,7 +615,7 @@
         [dot_tn(x, dq.reshape(rows, width)).astype(bf16), dot_tn(xe, dk_flat).astype(bf16), dot_tn(xe, dv_flat).astype(bf16)],
         axis=1,
     )
-    first_sums = lax.psum_scatter(first_grads, "ctx", scatter_dimension=0, tiled=True)
+    first_sums = exchange_scatter(first_grads, "ctx")
 
     key_part = (dot_nt(dk_flat, w_kv[:, :width]) + dot_nt(dv_flat, w_kv[:, width:])).reshape(seqs, keys, width)
     input_grad = first_grad.reshape(seqs, tokens, width) + dot_nt(dq.reshape(rows, width), w_q).reshape(seqs, tokens, width)
@@ -464,15 +626,13 @@
         input_grad = input_grad + shifted(to_left, "ctx", n - pieces).astype(f32)
         input_grad = input_grad + shifted(to_right, "ctx", n + 1).astype(f32)
 
-    small = jnp.concatenate(
-        [jnp.stack([gain_one, bias_one, gain_two, bias_two]), jnp.pad(peak, (0, width - heads))[None], jnp.zeros((3, width), f32)]
-    )
-    is_peak = (jnp.arange(8) == 4)[:, None]
+    is_peak_row = (jnp.arange(8) == 4)[:, None]
+    small = jnp.where(is_peak_row, jnp.pad(peak, (0, width - heads))[None], small)
     for axis in ("ctx", "seq"):
         bit = 1
         while bit < lax.axis_size(axis):
             other = swapped(small, axis, bit)
-            small = jnp.where(is_peak, jnp.maximum(small, other), small + other)
+            small = jnp.where(is_peak_row, jnp.maximum(small, other), small + other)
             bit *= 2
     norm_grads = small[:4]
     factors = clip_level / jnp.maximum(small[4, :heads], clip_level)

time: 667 us -> 506 us (0.76)
  matrix products: 169 us -> 44.6 us
  waiting for transfers between devices: 262 us -> 155 us
  Pallas kernels: 130 us -> 216 us
  local copies, waits for them, and re-layouts: 39.8 us -> 29.2 us
  other arithmetic: 22.3 us -> 12.6 us
    reduce_scatter x1, waiting for transfers between devices: 130 us -> 0.01 us  [on_device(): lax.psum_scatter(rest_grads, 'ctx', scatter_dimension=0, tiled=True)]
    pallas_call x0 -> x1, Pallas kernels: none -> 79.8 us  [feed_forward(): pl.pallas_call(ffn_kernel, grid=(2 * chunks,), in_specs=[full, full, full...]
    dot_general x7 -> x3, matrix products: 69.2 us -> 19.8 us  [dot_nt(): lax.dot_general(a, b, (((1,), (1,)), ((), ())), preferred_element_type=f32)]
    dot_general x6 -> x2, matrix products: 53.5 us -> 12.2 us  [dot_nn(): lax.dot_general(a, b, (((1,), (0,)), ((), ())), preferred_element_type=f32)]
    dot_general x10 -> x3, matrix products: 46.7 us -> 12.6 us  [dot_tn(): lax.dot_general(a, b, (((0,), (0,)), ((), ())), preferred_element_type=f32)]
    ppermute x9 -> x13, waiting for transfers between devices: 51.6 us -> 73.4 us  [swapped(): return lax.ppermute(value, axis, [(i, i ^ bit) for i in range(peers)])]
    unnamed x85 -> x64, local copies, waits for them, and re-layouts: 20.9 us -> 13.2 us
    reduce_sum x5 -> x0, other arithmetic: 6.75 us -> none  [the longest x2 3.01 us: layer_norm_back(): return (back, jnp.sum(grad * hat, axis=0), jnp.sum(grad, axis=0))]
  transfers between devices with their start and end apart: 17 -> 20, of which waited for: 9 -> 10; matrix products, arithmetic and copies ran while one was open for 12% -> 14% of each run, Pallas kernels for 8% -> 26%
where the time goes in v2:
time: 506 us; the launch traced here: 501 us
  Pallas kernels  216 us (43%)
  waiting for transfers between devices  155 us (31%)
  matrix products  44.6 us (9%)
  starting transfers between devices  29.5 us (6%)
  local copies, waits for them, and re-layouts  29.2 us (6%)
  between operations  14.8 us (3%)
  other arithmetic  12.6 us (2%)
    pallas_call x1, Pallas kernels, feed_forward(): pl.pallas_call(ffn_kernel, grid=(2 * chunks,), in_specs=[full, full, full...  79.8 us
    pallas_call x1, Pallas kernels, attend_bwd(): pl.pallas_call(bwd_kernel, grid=(pairs, seqs), in_specs=[smem, smem, tok,...  76.9 us
    ppermute x13, waiting for transfers between devices, swapped(): return lax.ppermute(value, axis, [(i, i ^ bit) for i in range(peers)])  73.4 us
    pallas_call x1, Pallas kernels, attend_fwd(): pl.pallas_call(fwd_kernel, grid=(pairs, seqs), in_specs=[smem, smem, pl.B...  48.3 us
    all_gather x1, waiting for transfers between devices, on_device(): w_rest = lax.all_gather(picked_rest, 'ctx', axis=0, tiled=True)  46.5 us
    all_gather x1, waiting for transfers between devices, on_device(): w_first = lax.all_gather(picked_first, 'ctx', axis=0, tiled=True)  34.5 us
    dot_general x3, matrix products, dot_nt(): lax.dot_general(a, b, (((1,), (1,)), ((), ())), preferred_element_type=f32)  19.8 us
    ppermute x13, starting transfers between devices, swapped(): return lax.ppermute(value, axis, [(i, i ^ bit) for i in range(peers)])  18.3 us
  transfers between devices with their start and end apart: 20, of which 10 were waited for; matrix products, arithmetic and copies ran while one was open for 14% of the time, Pallas kernels for 26%

profile of v2, /device:TPU:0, one launch (start us, length us, event | category | flops | bytes accessed | tf_op | source)
XLA Modules:
  0.0 501.0 jit_solution(5000817960983310350)
XLA Ops:
  8.9 1.4 convert_element_type.91.refs_0_
  10.9 3.0 collective-permute-start.1
  14.7 4.7 collective-permute-done.1
  20.2 1.3 collective-permute-start.3
  21.5 4.2 collective-permute-start.2
  25.6 1.7 collective-permute-start
  27.5 15.3 %collective-permute-done.refs_1_ = bf16[9,48,768]{2,1,0:T(8,128)(2,1)S(1)} collective-permute-done((bf16[9,48,768]{2,1,0:T(8,128)(2,1)S(1)}, bf16[9,48,768]{2,1,0:T(8,128)(2,1)S(1)}, u32[]{:S(2)}, u32[]{:S(2)}) %collective-permute-start) | collective-permute-done | bytes 663584 | tf_op jit(solution)/shard_map/ppermute | solution.py:230
  42.8 1.8 pick_units.2
  44.6 34.5 %all-gather.3.cloned.1.call-done = bf16[768,2304]{1,0:T(8,128)(2,1)} async-done(((bf16[48,2304]{1,0:T(8,128)(2,1)}), bf16[768,2304]{1,0:T(8,128)(2,1)}) %all-gather.3.cloned.1.call-update) | async-done | bytes 3538960 | tf_op jit(solution)/shard_map/all_gather | solution.py:582
  79.2 1.4 convert_reduce_fusion
  80.7 3.9 fusion.5
  84.5 1.8 copy.36
  86.4 1.5 constant_dynamic-update-slice_fusion.2
  88.0 1.9 constant_dynamic-update-slice_fusion
  90.8 8.3 %convolution_convert_fusion = bf16[3072,1536]{1,0:T(8,128)(2,1)S(1)} fusion(bf16[3072,768]{1,0:T(8,128)(2,1)S(1)} %bitcast.92, bf16[768,2304]{1,0:T(8,128)(2,1)S(1)} %copy-done.19), kind=kOutput, calls=%fused_computation | convolution fusion | flops 7252475904 | bytes 16515072 | tf_op jit(solution)/shard_map/dot_general | solution.py:25
  99.2 48.3 %attend_fwd.1 = (bf16[2,512,768]{2,1,0:T(8,128)(2,1)S(1)}, f32[2,6,2,512]{3,2,1,0:T(2,128)S(1)}, f32[12,8,256]{2,1,0:T(8,128)S(1)}) custom-call(s32[12]{0:T(128)S(1)} %copy-done.5, f32[12]{0:T(128)S(1)} %power_multiply_fusion.slope_ref, bf16[2,512,768]{2,1,0:T(8,128)(2,1)S(1)} %bitcast.70, bf16[2,1536,1536]{2,1,0:T(8,128)(2,1)S(1)} %bitcast.72, ...), custom_call_target="tpu_custom_call" | custom-call | flops 20000000000 | bytes 10000000 | tf_op jit(solution)/shard_map/attend_fwd/pallas_call | solution.py:106
  147.5 3.5 copy-done.6
  152.2 46.5 %all-gather.5.cloned.1.call-done.wo_ref.wg_ref.wu_ref.wd_ref = bf16[768,9984]{1,0:T(8,128)(2,1)} async-done(((bf16[48,9984]{1,0:T(8,128)(2,1)}), bf16[768,9984]{1,0:T(8,128)(2,1)}) %all-gather.5.cloned.1.call-update) | async-done | bytes 15335440 | tf_op jit(solution)/shard_map/all_gather | solution.py:585
  198.7 79.8 %feed_forward.1 = (bf16[1024,768]{1,0:T(8,128)(2,1)}, f32[1024,768]{1,0:T(8,128)}, bf16[1024,768]{1,0:T(8,128)(2,1)}, f32[8,768]{1,0:T(8,128)}, bf16[768,9984]{1,0:T(8,128)(2,1)}) custom-call(bf16[1024,768]{1,0:T(8,128)(2,1)} %bitcast.79, bf16[1024,768]{1,0:T(8,128)(2,1)} %bitcast.90, bf16[1024,768]{1,0:T(8,128)(2,1)} %bitcast.96, ...), custom_call_target="tpu_custom_call" | custom-call | flops 46000001024 | bytes 60000000 | tf_op jit(solution)/shard_map/feed_forward/pallas_call | solution.py:500
  278.7 1.4 copy-done.9
  280.1 1.4 copy-done.10
  281.5 76.9 %attend_bwd.1 = (bf16[2,512,768]{2,1,0:T(8,128)(2,1)S(1)}, bf16[2,1536,768]{2,1,0:T(8,128)(2,1)S(1)}, bf16[2,1536,768]{2,1,0:T(8,128)(2,1)}) custom-call(s32[12]{0:T(128)S(1)} %copy-done.5, f32[12]{0:T(128)S(1)} %power_multiply_fusion.slope_ref, bf16[2,512,768]{2,1,0:T(8,128)(2,1)S(1)} %bitcast.71, bf16[2,1536,1536]{2,1,0:T(8,128)(2,1)} %bitcast.74, ...), custom_call_target="tpu_custom_call" | custom-call | flops 49999998976 | bytes 20000000 | tf_op jit(solution)/shard_map/attend_bwd/pallas_call | solution.py:200
  358.5 1.5 fusion.6
  360.9 7.1 %bitcast_convert_fusion.1 = bf16[768,768]{0,1:T(8,128)(2,1)S(1)} fusion(bf16[2,1536,768]{2,1,0:T(8,128)(2,1)} %copy-done.18, bf16[2,1536,768]{2,1,0:T(8,128)(2,1)S(1)} %get-tuple-element.42), kind=kOutput, calls=%fused_computation.11 | convolution fusion | flops 3624468480 | bytes 10616832 | tf_op jit(solution)/shard_map/dot_general | solution.py:362
  368.0 4.1 bitcast_convert_fusion
  372.1 2.1 pad_maximum_fusion
  374.2 5.9 %copy.40 = bf16[768,2304]{1,0:T(8,128)(2,1)} copy(bf16[768,2304]{0,1:T(8,128)(2,1)} %pad_maximum_fusion) | data formatting | bytes 7077888 | tf_op jit(solution)/shard_map/concatenate | solution.py:614
  380.1 2.9 dynamic-slice_bitcast_fusion
  384.0 2.7 collective-permute-done.6
  387.0 6.8 %fusion.8 = f32[3072,768]{1,0:T(8,128)S(1)} fusion(bf16[3072,768]{1,0:T(8,128)(2,1)} %bitcast.97, bf16[768,2304]{1,0:T(8,128)(2,1)} %all-gather.3.cloned.1.call-done), kind=kOutput, calls=%fused_computation.21 | convolution fusion | flops 3623878656 | bytes 15335424 | tf_op jit(solution)/shard_map/dot_general | solution.py:22
  393.9 2.0 fusion
  397.0 1.9 collective-permute-start.13
  398.9 5.5 %convolution_add_fusion = f32[3072,768]{1,0:T(8,128)S(1)} fusion(f32[3072,768]{1,0:T(8,128)S(1)} %fusion.8, bf16[3072,768]{1,0:T(8,128)(2,1)S(1)} %bitcast.78, bf16[768,2304]{1,0:T(8,128)(2,1)} %all-gather.3.cloned.1.call-done), kind=kOutput, calls=%fused_computation.3 | convolution fusion | flops 3626237952 | bytes 24772608 | tf_op jit(solution)/shard_map/dot_general | solution.py:22
  405.0 1.5 collective-permute-start.9
  406.5 1.8 fusion.23
  409.2 1.4 collective-permute-start.4
  410.6 4.2 collective-permute-start.5
  414.9 1.4 collective-permute-start.10
  416.3 13.2 %collective-permute-done.13 = bf16[4,48,2304]{2,1,0:T(8,128)(2,1)S(1)} collective-permute-done((bf16[4,48,2304]{2,1,0:T(8,128)(2,1)}, bf16[4,48,2304]{2,1,0:T(8,128)(2,1)S(1)}, u32[]{:S(2)}, u32[]{:S(2)}) %collective-permute-start.13) | collective-permute-done | bytes 884768 | tf_op jit(solution)/shard_map/ppermute | solution.py:230
  429.7 4.3 collective-permute-start.14
  434.8 24.3 %collective-permute-done.14 = bf16[2,48,2304]{2,1,0:T(8,128)(2,1)S(1)} collective-permute-done((bf16[2,48,2304]{2,1,0:T(8,128)(2,1)S(1)}, bf16[2,48,2304]{2,1,0:T(8,128)(2,1)S(1)}, u32[]{:S(2)}, u32[]{:S(2)}) %collective-permute-start.14) | collective-permute-done | bytes 442400 | tf_op jit(solution)/shard_map/ppermute | solution.py:230
  459.2 1.7 collective-permute-start.15
  461.6 5.9 %collective-permute-done.15 = bf16[1,48,2304]{2,1,0:T(8,128)(2,1)S(1)} collective-permute-done((bf16[1,48,2304]{2,1,0:T(8,128)(2,1)S(1)}, bf16[1,48,2304]{2,1,0:T(8,128)(2,1)S(1)}, u32[]{:S(2)}, u32[]{:S(2)}) %collective-permute-start.15) | collective-permute-done | bytes 221216 | tf_op jit(solution)/shard_map/ppermute | solution.py:230
  468.2 1.5 collective-permute-start.16
  469.8 1.2 copy-done.1
  472.3 7.5 %fusion.2 = f32[2,512,768]{2,1,0:T(8,128)} fusion(f32[2,1536,768]{2,1,0:T(8,128)} %bitcast.82, bf16[2,512,768]{2,1,0:T(8,128)(2,1)} %collective-permute-done.5, bf16[2,512,768]{2,1,0:T(8,128)(2,1)} %collective-permute-done.4, f32[2,512,768]{2,1,0:T(8,128)} %bitcast.89, bf16[2,512,768]{2,1,0:T(8,128)(2,1)S(1)} %get-tuple-element.41, ...), kind=kOutput, calls=%fused_computation.9 | convolution fusion | flops 1212678144 | bytes 15335424 | tf_op jit(solution)/shard_map/dot_general | solution.py:22
  481.4 7.1 %collective-permute-done.11.refs_1_ = bf16[9,48,768]{2,1,0:T(8,128)(2,1)S(1)} collective-permute-done((bf16[9,48,768]{2,1,0:T(8,128)(2,1)S(1)}, bf16[9,48,768]{2,1,0:T(8,128)(2,1)S(1)}, u32[]{:S(2)}, u32[]{:S(2)}) %collective-permute-start.11) | collective-permute-done | bytes 663584 | tf_op jit(solution)/shard_map/ppermute | solution.py:230
  488.5 5.6 %adam_slots.1 = (f32[9,48,768]{2,1,0:T(8,128)}, f32[9,48,768]{2,1,0:T(8,128)}, f32[9,48,768]{2,1,0:T(8,128)}, f32[9,48,768]{2,1,0:T(8,128)}, bf16[9,48,768]{2,1,0:T(8,128)(2,1)}) custom-call(s32[9]{0:T(128)S(1)} %dynamic_slice.43.unit_ref, f32[9,48,768]{2,1,0:T(8,128)S(1)} %copy-done, f32[9,48,768]{2,1,0:T(8,128)S(1)} %copy-done.3, ...), custom_call_target="tpu_custom_call" | custom-call | tf_op jit(solution)/shard_map/adam_slots/pallas_call | solution.py:342
  (129 shorter events, 16.7 us)
Async XLA Ops:
  7.2 13.0 %copy-start.15 = (bf16[2,512,768]{2,1,0:T(8,128)(2,1)S(1)}, bf16[2,512,768]{2,1,0:T(8,128)(2,1)}, u32[]{:S(2)}) copy-start(bf16[2,512,768]{2,1,0:T(8,128)(2,1)} %param.12) | copy-start | bytes 4718596
  7.2 71.9 %all-gather.3.cloned.1.call-start = ((), (), s32[]{:S(2)}) async-start(), calls=%async_computation.1 | async-start | bytes 3760128 | tf_op jit(solution)/shard_map/all_gather | solution.py:582
  8.9 70.3 %copy-start.21 = (s32[2,8192]{1,0:T(2,128)S(1)}, s32[2,8192]{1,0:T(2,128)}, u32[]{:S(2)}) copy-start(s32[2,8192]{1,0:T(2,128)} %param.14) | copy-start | bytes 196612
  10.9 8.4 %collective-permute-start.1 = (bf16[48,2304]{1,0:T(8,128)(2,1)S(1)}, bf16[48,2304]{1,0:T(8,128)(2,1)S(1)}, u32[]{:S(2)}, u32[]{:S(2)}) collective-permute-start(bf16[48,2304]{1,0:T(8,128)(2,1)S(1)} %pick_units.3), channel_id=1, source_target_pairs={{0,1},{1,0},{2,3},{3,2},{4,5},{5,4},{6,7},{7,6},{8,9},{9,8},{10,11... | collective-permute-start | bytes 663560 | tf_op jit(solution)/shard_map/ppermute | solution.py:230
  20.1 178.6 %all-gather.5.cloned.1.call-start = ((), (), s32[]{:S(2)}) async-start(), calls=%async_computation.2 | async-start | bytes 16293888 | tf_op jit(solution)/shard_map/all_gather | solution.py:585
  20.2 24.4 %collective-permute-start.3 = (bf16[2,512,768]{2,1,0:T(8,128)(2,1)S(1)}, bf16[2,512,768]{2,1,0:T(8,128)(2,1)}, u32[]{:S(2)}, u32[]{:S(2)}) collective-permute-start(bf16[2,512,768]{2,1,0:T(8,128)(2,1)S(1)} %copy-done.15), channel_id=1, source_target_pairs={{2,0},{4,2},{6,4},{8,6},{10,8},{12,10},{14,12},{16,14},{18,16},{20... | collective-permute-start | bytes 4718600 | tf_op jit(solution)/shard_map/ppermute | solution.py:225
  21.5 23.1 %collective-permute-start.2 = (bf16[2,512,768]{2,1,0:T(8,128)(2,1)S(1)}, bf16[2,512,768]{2,1,0:T(8,128)(2,1)}, u32[]{:S(2)}, u32[]{:S(2)}) collective-permute-start(bf16[2,512,768]{2,1,0:T(8,128)(2,1)S(1)} %copy-done.15), channel_id=1, source_target_pairs={{0,2},{2,4},{4,6},{6,8},{8,10},{10,12},{12,14},{14,16},{16,18},{18... | collective-permute-start | bytes 4718600 | tf_op jit(solution)/shard_map/ppermute | solution.py:225
  25.6 17.1 %collective-permute-start = (bf16[9,48,768]{2,1,0:T(8,128)(2,1)S(1)}, bf16[9,48,768]{2,1,0:T(8,128)(2,1)S(1)}, u32[]{:S(2)}, u32[]{:S(2)}) collective-permute-start(bf16[9,48,768]{2,1,0:T(8,128)(2,1)S(1)} %convert_element_type.91.refs_0_), channel_id=1, source_target_pairs={{0,1},{1,0},{2,3},{3,2},{4,5},{5,4},{6,7},{7,6},{8,9},{9,8},{10,11... | collective-permute-start | bytes 1990664 | tf_op jit(solution)/shard_map/ppermute | solution.py:230
  79.1 390.7 %reduce-scatter.2.cloned.1.call-start = ((), (), s32[]{:S(2)}) async-start(), calls=%async_computation.3 | async-start | bytes 16293888 | tf_op jit(solution)/shard_map/reduce_scatter | solution.py:609
  84.5 3.4 copy-start.16
  87.9 2.9 copy-start.19
  89.9 9.3 %copy-start.18 = (bf16[2,1536,768]{2,1,0:T(8,128)(2,1)}, bf16[2,1536,768]{2,1,0:T(8,128)(2,1)S(1)}, u32[]{:S(2)}) copy-start(bf16[2,1536,768]{2,1,0:T(8,128)(2,1)S(1)} %constant_dynamic-update-slice_fusion) | copy-start | bytes 14155780
  90.8 8.3 %copy-start.5 = (s32[12]{0:T(128)S(1)}, s32[12]{0:T(128)}, u32[]{:S(2)}) copy-start(s32[12]{0:T(128)} %win_ref.3) | copy-start | bytes 148
  147.5 3.5 copy-start.6
  278.7 1.4 copy-start.9
  281.5 77.0 %copy-start.17 = (bf16[2,512,768]{2,1,0:T(8,128)(2,1)S(1)}, bf16[2,512,768]{2,1,0:T(8,128)(2,1)}, u32[]{:S(2)}) copy-start(bf16[2,512,768]{2,1,0:T(8,128)(2,1)} %param.12) | copy-start | bytes 4718596
  358.5 2.4 copy-start.7
  358.5 9.5 %slice-start.2 = ((s8[4718592]{0:T(1024)(128)(4,1)}), s8[4194304]{0:T(1024)(128)(4,1)S(1)}, s32[]{:S(2)}) async-start(s8[4718592]{0:T(1024)(128)(4,1)} %bitcast.93), calls=%async_computation.6 | async-start | bytes 8388608
  358.5 9.5 %slice-start.4 = ((s8[4718592]{0:T(1024)(128)(4,1)}), s8[524288]{0:T(1024)(128)(4,1)S(1)}, s32[]{:S(2)}) async-start(s8[4718592]{0:T(1024)(128)(4,1)} %bitcast.98), calls=%async_computation.8 | async-start | bytes 1048576
  360.9 7.1 %slice-start.3 = ((s8[4718592]{0:T(1024)(128)(4,1)}), s8[524288]{0:T(1024)(128)(4,1)S(1)}, s32[]{:S(2)}) async-start(s8[4718592]{0:T(1024)(128)(4,1)} %bitcast.93), calls=%async_computation.7 | async-start | bytes 1048576
  360.9 7.1 %slice-start.5 = ((s8[4718592]{0:T(1024)(128)(4,1)}), s8[4194304]{0:T(1024)(128)(4,1)S(1)}, s32[]{:S(2)}) async-start(s8[4718592]{0:T(1024)(128)(4,1)} %bitcast.98), calls=%async_computation.9 | async-start | bytes 8388608
  380.1 3.5 copy-start.20
  380.1 18.8 %slice-start = ((s8[4718592]{0:T(1024)(128)(4,1)}), s8[524288]{0:T(1024)(128)(4,1)S(1)}, s32[]{:S(2)}) async-start(s8[4718592]{0:T(1024)(128)(4,1)} %bitcast.76), calls=%async_computation.4 | async-start | bytes 1048576
  383.0 10.9 %collective-permute-start.12 = (bf16[8,48,2304]{2,1,0:T(8,128)(2,1)}, bf16[8,48,2304]{2,1,0:T(8,128)(2,1)}, u32[]{:S(2)}, u32[]{:S(2)}) collective-permute-start(bf16[8,48,2304]{2,1,0:T(8,128)(2,1)} %dynamic-slice_bitcast_fusion), channel_id=1, source_target_pairs={{0,2},{2,0},{4,6},{6,4},{8,10},{10,8},{12,14},{14,12},{16,18},{18,... | collective-permute-start | bytes 5308424 | tf_op jit(solution)/shard_map/ppermute | solution.py:230
  383.7 3.0 collective-permute-start.6
  386.8 7.0 %collective-permute-start.7 = (f32[8,768]{1,0:T(8,128)S(1)}, f32[8,768]{1,0:T(8,128)S(1)}, u32[]{:S(2)}, u32[]{:S(2)}) collective-permute-start(f32[8,768]{1,0:T(8,128)S(1)} %add_select_fusion.4), channel_id=1, source_target_pairs={{0,4},{2,6},{4,0},{6,2},{8,12},{10,14},{12,8},{14,10},{16,20},{18,... | collective-permute-start | bytes 73736 | tf_op jit(solution)/shard_map/ppermute | solution.py:230
  387.0 7.0 %copy-start.12 = (bf16[768,2304]{1,0:T(8,128)(2,1)S(1)}, bf16[768,2304]{1,0:T(8,128)(2,1)}, u32[]{:S(2)}) copy-start(bf16[768,2304]{1,0:T(8,128)(2,1)} %copy.40) | copy-start | bytes 10616836
  387.0 11.9 %slice-start.1 = ((s8[4718592]{0:T(1024)(128)(4,1)}), s8[4194304]{0:T(1024)(128)(4,1)S(1)}, s32[]{:S(2)}) async-start(s8[4718592]{0:T(1024)(128)(4,1)} %bitcast.76), calls=%async_computation.5 | async-start | bytes 8388608
  393.9 11.0 %collective-permute-start.8 = (f32[8,768]{1,0:T(8,128)S(1)}, f32[8,768]{1,0:T(8,128)S(1)}, u32[]{:S(2)}, u32[]{:S(2)}) collective-permute-start(f32[8,768]{1,0:T(8,128)S(1)} %add_select_fusion.3), channel_id=1, source_target_pairs={{0,8},{2,10},{4,12},{6,14},{8,0},{10,2},{12,4},{14,6},{16,24},{18,... | collective-permute-start | bytes 73736 | tf_op jit(solution)/shard_map/ppermute | solution.py:230
  395.9 3.0 copy-start.13
  397.0 32.4 %collective-permute-start.13 = (bf16[4,48,2304]{2,1,0:T(8,128)(2,1)}, bf16[4,48,2304]{2,1,0:T(8,128)(2,1)S(1)}, u32[]{:S(2)}, u32[]{:S(2)}) collective-permute-start(bf16[4,48,2304]{2,1,0:T(8,128)(2,1)} %dynamic-slice_bitcast_fusion.1), channel_id=1, source_target_pairs={{0,4},{2,6},{4,0},{6,2},{8,12},{10,14},{12,8},{14,10},{16,20},{18,... | collective-permute-start | bytes 2654216 | tf_op jit(solution)/shard_map/ppermute | solution.py:230
  404.4 4.8 copy-start.11
  405.0 24.5 %copy-start.14 = (bf16[8,48,2304]{2,1,0:T(8,128)(2,1)S(1)}, bf16[8,48,2304]{2,1,0:T(8,128)(2,1)}, u32[]{:S(2)}) copy-start(bf16[8,48,2304]{2,1,0:T(8,128)(2,1)} %copy-done.13) | copy-start | bytes 5308420
  405.0 9.8 %collective-permute-start.9 = (f32[8,768]{1,0:T(8,128)S(1)}, f32[8,768]{1,0:T(8,128)S(1)}, u32[]{:S(2)}, u32[]{:S(2)}) collective-permute-start(f32[8,768]{1,0:T(8,128)S(1)} %add_select_fusion.2), channel_id=1, source_target_pairs={{0,16},{2,18},{4,20},{6,22},{8,24},{10,26},{12,28},{14,30},{16,0},... | collective-permute-start | bytes 73736 | tf_op jit(solution)/shard_map/ppermute | solution.py:230
  409.2 51.8 %copy-start.22 = (f32[4,768]{1,0:T(4,128)S(1)}, f32[4,768]{1,0:T(4,128)}, u32[]{:S(2)}) copy-start(f32[4,768]{1,0:T(4,128)} %norm_ref.1) | copy-start | bytes 36868
  409.2 51.8 %copy-start.23 = (f32[4,768]{1,0:T(4,128)S(1)}, f32[4,768]{1,0:T(4,128)}, u32[]{:S(2)}) copy-start(f32[4,768]{1,0:T(4,128)} %param.21) | copy-start | bytes 36868
  409.2 51.8 %copy-start.24 = (f32[4,768]{1,0:T(4,128)S(1)}, f32[4,768]{1,0:T(4,128)}, u32[]{:S(2)}) copy-start(f32[4,768]{1,0:T(4,128)} %param.22) | copy-start | bytes 36868
  409.2 63.1 %collective-permute-start.4 = (bf16[2,512,768]{2,1,0:T(8,128)(2,1)}, bf16[2,512,768]{2,1,0:T(8,128)(2,1)}, u32[]{:S(2)}, u32[]{:S(2)}) collective-permute-start(bf16[2,512,768]{2,1,0:T(8,128)(2,1)} %get-tuple-element.60), channel_id=1, source_target_pairs={{2,0},{4,2},{6,4},{8,6},{10,8},{12,10},{14,12},{16,14},{18,16},{20... | collective-permute-start | bytes 4718600 | tf_op jit(solution)/shard_map/ppermute | solution.py:225
  410.6 61.7 %collective-permute-start.5 = (bf16[2,512,768]{2,1,0:T(8,128)(2,1)}, bf16[2,512,768]{2,1,0:T(8,128)(2,1)}, u32[]{:S(2)}, u32[]{:S(2)}) collective-permute-start(bf16[2,512,768]{2,1,0:T(8,128)(2,1)} %get-tuple-element.61), channel_id=1, source_target_pairs={{0,2},{2,4},{4,6},{6,8},{8,10},{10,12},{12,14},{14,16},{16,18},{18... | collective-permute-start | bytes 4718600 | tf_op jit(solution)/shard_map/ppermute | solution.py:225
  414.9 19.1 %collective-permute-start.10 = (f32[8,768]{1,0:T(8,128)S(1)}, f32[8,768]{1,0:T(8,128)S(1)}, u32[]{:S(2)}, u32[]{:S(2)}) collective-permute-start(f32[8,768]{1,0:T(8,128)S(1)} %add_select_fusion.1), channel_id=1, source_target_pairs={{0,1},{1,0},{2,3},{3,2},{4,5},{5,4},{6,7},{7,6},{8,9},{9,8},{10,11... | collective-permute-start | bytes 73736 | tf_op jit(solution)/shard_map/ppermute | solution.py:230
  429.7 29.3 %collective-permute-start.14 = (bf16[2,48,2304]{2,1,0:T(8,128)(2,1)S(1)}, bf16[2,48,2304]{2,1,0:T(8,128)(2,1)S(1)}, u32[]{:S(2)}, u32[]{:S(2)}) collective-permute-start(bf16[2,48,2304]{2,1,0:T(8,128)(2,1)S(1)} %dynamic-slice_bitcast_fusion.2), channel_id=1, source_target_pairs={{0,8},{2,10},{4,12},{6,14},{8,0},{10,2},{12,4},{14,6},{16,24},{18,... | collective-permute-start | bytes 1327112 | tf_op jit(solution)/shard_map/ppermute | solution.py:230
  459.2 8.3 %collective-permute-start.15 = (bf16[1,48,2304]{2,1,0:T(8,128)(2,1)S(1)}, bf16[1,48,2304]{2,1,0:T(8,128)(2,1)S(1)}, u32[]{:S(2)}, u32[]{:S(2)}) collective-permute-start(bf16[1,48,2304]{2,1,0:T(8,128)(2,1)S(1)} %constant_dynamic-slice_fusion), channel_id=1, source_target_pairs={{0,16},{2,18},{4,20},{6,22},{8,24},{10,26},{12,28},{14,30},{16,0},... | collective-permute-start | bytes 663560 | tf_op jit(solution)/shard_map/ppermute | solution.py:230
  468.2 13.1 %collective-permute-start.16 = (bf16[9,48,768]{2,1,0:T(8,128)(2,1)S(1)}, bf16[9,48,768]{2,1,0:T(8,128)(2,1)S(1)}, u32[]{:S(2)}, u32[]{:S(2)}) collective-permute-start(bf16[9,48,768]{2,1,0:T(8,128)(2,1)S(1)} %to_slots.7), channel_id=1, source_target_pairs={{0,1},{1,0},{2,3},{3,2},{4,5},{5,4},{6,7},{7,6},{8,9},{9,8},{10,11... | collective-permute-start | bytes 1990664 | tf_op jit(solution)/shard_map/ppermute | solution.py:230
  471.7 16.8 %collective-permute-start.11 = (bf16[9,48,768]{2,1,0:T(8,128)(2,1)S(1)}, bf16[9,48,768]{2,1,0:T(8,128)(2,1)S(1)}, u32[]{:S(2)}, u32[]{:S(2)}) collective-permute-start(bf16[9,48,768]{2,1,0:T(8,128)(2,1)S(1)} %to_slots.5), channel_id=1, source_target_pairs={{0,1},{1,0},{2,3},{3,2},{4,5},{5,4},{6,7},{7,6},{8,9},{9,8},{10,11... | collective-permute-start | bytes 1990664 | tf_op jit(solution)/shard_map/ppermute | solution.py:230
  472.3 8.2 %copy-start.2 = (bf16[48,9984]{1,0:T(8,128)(2,1)S(1)}, bf16[48,9984]{1,0:T(8,128)(2,1)}, u32[]{:S(2)}) copy-start(bf16[48,9984]{1,0:T(8,128)(2,1)} %reduce-scatter.2.cloned.1.call-done.col_ref) | copy-start | bytes 2875396
  472.3 16.2 %copy-start.3 = (f32[9,48,768]{2,1,0:T(8,128)S(1)}, f32[9,48,768]{2,1,0:T(8,128)}, u32[]{:S(2)}) copy-start(f32[9,48,768]{2,1,0:T(8,128)} %m_ref.1) | copy-start | bytes 3981316
  472.3 16.2 %copy-start.4 = (f32[9,48,768]{2,1,0:T(8,128)S(1)}, f32[9,48,768]{2,1,0:T(8,128)}, u32[]{:S(2)}) copy-start(f32[9,48,768]{2,1,0:T(8,128)} %v_ref.1) | copy-start | bytes 3981316
  479.8 8.7 %copy-start = (f32[9,48,768]{2,1,0:T(8,128)S(1)}, f32[9,48,768]{2,1,0:T(8,128)}, u32[]{:S(2)}) copy-start(f32[9,48,768]{2,1,0:T(8,128)} %w_ref.1) | copy-start | bytes 3981316
  (3 other events, 3.8 us)
Sparse Core Ops, SparseCore 0:
  20.2 58.8 all-gather.2
  81.9 116.7 all-gather.4
  278.7 158.5 reduce-scatter.1

commit v3 on v2

--- a/solution.py
+++ b/solution.py
@@ -245,29 +245,20 @@
     return back, jnp.sum(grad * hat, axis=0, keepdims=True), jnp.sum(grad, axis=0, keepdims=True)
 
 
-def exchange_scatter(value, axis):
-    peers = lax.axis_size(axis)
-    me = lax.axis_index(axis)
-    rows = value.shape[0] // peers
-    bit = 1
-    value = value.reshape((peers, rows) + value.shape[1:])
-    while bit < peers:
-        count = value.shape[0]
-        split = value.reshape((count // 2, 2) + value.shape[1:])
-        side = (me // bit) % 2
-        keep = lax.dynamic_index_in_dim(split, side, 1, False)
-        give = lax.dynamic_index_in_dim(split, 1 - side, 1, False)
-        got = swapped(give, axis, bit)
-        value = (keep.astype(f32) + got.astype(f32)).astype(value.dtype)
-        bit *= 2
-    return value[0]
-
-
-def pick_units(slot_of, sources, count):
+def halve(value, axis, bit, dim):
+    side = (lax.axis_index(axis) // bit) % 2
+    keep = lax.dynamic_index_in_dim(value, side, dim, False)
+    got = swapped(lax.dynamic_index_in_dim(value, 1 - side, dim, False), axis, bit)
+    return (keep.astype(f32) + got.astype(f32)).astype(value.dtype)
+
+
+def pick_units(slot_of, sources, count, pad=0):
     slots, rows, width = sources[0].shape
 
     def kernel(slot_ref, *refs):
         out_ref = refs[-1]
+        if pad:
+            out_ref[:, pl.ds(count * width, pad)] = jnp.zeros((rows, pad), out_ref.dtype)
         for u in range(count):
             at = pl.ds(u * width, width)
             for number, ref in enumerate(refs[:-1]):
@@ -281,7 +272,7 @@
         kernel,
         in_specs=[pl.BlockSpec(memory_space=pltpu.SMEM)] + [vmem] * len(sources),
         out_specs=vmem,
-        out_shape=jax.ShapeDtypeStruct((rows, count * width), sources[0].dtype),
+        out_shape=jax.ShapeDtypeStruct((rows, count * width + pad), sources[0].dtype),
         compiler_params=pltpu.CompilerParams(vmem_limit_bytes=24 * 2**20),
         name="pick_units",
     )(slot_of, *sources)
@@ -368,7 +359,7 @@
     return cdf, density
 
 
-RB = 256
+RB = 512
 CHUNK = 256
 
 
@@ -514,7 +505,7 @@
             jax.ShapeDtypeStruct((rows, width), f32),
             jax.ShapeDtypeStruct((rows, width), bf16),
             jax.ShapeDtypeStruct((8, width), f32),
-            jax.ShapeDtypeStruct((width, w_rest.shape[1]), bf16),
+            jax.ShapeDtypeStruct((width, width + 3 * FF), bf16),
         ],
         scratch_shapes=[
             pltpu.VMEM((rows, width), f32),
@@ -539,6 +530,83 @@
         name="feed_forward",
     )(o, x, out_grad, w_rest, w_rest, w_rest, w_rest, norms)
 
+def first_gradients(x_t, dq, dk, dv, tokens):
+    width, total = x_t.shape
+    seqs = dq.shape[0] // tokens
+    keys = total // seqs
+    cols = 256
+    per = width // cols
+
+    def kernel(x_ref, q_ref, k_ref, v_ref, out_ref):
+        unit = pl.program_id(0)
+
+        @pl.when(unit == 0)
+        def _():
+            acc = None
+            for s in range(seqs):
+                part = dot_nn(x_ref[:, pl.ds(s * keys + REACH, tokens)], q_ref[pl.ds(s * tokens, tokens), :])
+                acc = part if s == 0 else acc + part
+            out_ref[...] = acc.astype(bf16)
+
+        @pl.when(unit == 1)
+        def _():
+            out_ref[...] = dot_nn(x_ref[...], k_ref[...]).astype(bf16)
+
+        @pl.when(unit == 2)
+        def _():
+            out_ref[...] = dot_nn(x_ref[...], v_ref[...]).astype(bf16)
+
+    return pl.pallas_call(
+        kernel,
+        grid=(3, per),
+        in_specs=[
+            pl.BlockSpec((width, total), lambda u, c: (0, 0), pipeline_mode=pl.Buffered(1)),
+            pl.BlockSpec((dq.shape[0], cols), lambda u, c: (0, jnp.where(u == 0, c, per - 1))),
+            pl.BlockSpec((total, cols), lambda u, c: (0, jnp.where(u == 0, 0, jnp.where(u == 1, c, per - 1)))),
+            pl.BlockSpec((total, cols), lambda u, c: (0, jnp.where(u == 2, c, 0))),
+        ],
+        out_specs=pl.BlockSpec((width, cols), lambda u, c: (0, u * per + c)),
+        out_shape=jax.ShapeDtypeStruct((width, 3 * width), bf16),
+        compiler_params=pltpu.CompilerParams(vmem_limit_bytes=32 * 2**20),
+        cost_estimate=pl.CostEstimate(flops=9 * 10**9, bytes_accessed=2 * 10**7, transcendentals=0),
+        name="first_gradients",
+    )(x_t, dq, dk, dv)
+
+
+def input_parts(first_grad, dq, dk, dv, w_first):
+    seqs, tokens, width = dq.shape
+    keys = dk.shape[1]
+    pieces = REACH // tokens
+
+    def kernel(first_ref, q_ref, k_ref, v_ref, w_ref, own_ref, rim_ref):
+        block = pl.program_id(1)
+        part = dot_nt(k_ref[0], w_ref[:, width : 2 * width]) + dot_nt(v_ref[0], w_ref[:, 2 * width :])
+
+        @pl.when(block == pieces)
+        def _():
+            own_ref[0] = first_ref[0] + part + dot_nt(q_ref[0], w_ref[:, :width])
+
+        @pl.when(block != pieces)
+        def _():
+            rim_ref[0, 0] = part.astype(bf16)
+
+    own = pl.BlockSpec((1, tokens, width), lambda s, b: (s, 0, 0))
+    key = pl.BlockSpec((1, tokens, width), lambda s, b: (s, b, 0))
+    return pl.pallas_call(
+        kernel,
+        grid=(seqs, keys // tokens),
+        in_specs=[own, own, key, key,
+                  pl.BlockSpec(w_first.shape, lambda s, b: (0, 0), pipeline_mode=pl.Buffered(1))],
+        out_specs=[own, pl.BlockSpec((1, 1, tokens, width), lambda s, b: (s, jnp.where(b < pieces, b, jnp.maximum(b - 1, 0)), 0, 0))],
+        out_shape=[
+            jax.ShapeDtypeStruct((seqs, tokens, width), f32),
+            jax.ShapeDtypeStruct((seqs, 2 * pieces, tokens, width), bf16),
+        ],
+        compiler_params=pltpu.CompilerParams(vmem_limit_bytes=32 * 2**20),
+        cost_estimate=pl.CostEstimate(flops=9 * 10**9, bytes_accessed=2 * 10**7, transcendentals=0),
+        name="input_parts",
+    )(first_grad, dq, dk, dv, w_first)
+
 
 def on_device(inputs, out_grad, segments, windows, owners, weights, first_moments, second_moments,
               norm_params, norm_first, norm_second):
@@ -554,6 +622,7 @@
     groups = FF // width
     units = owners.shape[0]
     rest = units - 3
+    row_count = weights.shape[1]
 
     ids = jnp.arange(units, dtype=jnp.int32)
     before = (owners[None, :] == owners[:, None]) & (ids[None, :] < ids[:, None])
@@ -580,7 +649,7 @@
         sources = [every]
         picked_first = pick_units(place[:, :3], sources, 3)
     w_first = lax.all_gather(picked_first, "ctx", axis=0, tiled=True)
-    picked_rest = pick_units(place[:, 3:], sources, rest)
+    picked_rest = pick_units(place[:, 3:], sources, rest, 1024)
     picked_rest, w_first, left, right = lax.optimization_barrier((picked_rest, w_first, left, right))
     w_rest = lax.all_gather(picked_rest, "ctx", axis=0, tiled=True)
 
@@ -594,6 +663,10 @@
     slopes2 = jnp.power(2.0, -8.0 * (jnp.arange(heads, dtype=f32) + 1.0) / heads) * LOG2E
 
     x_ext = jnp.concatenate(left + [inputs] + right, axis=1)
+    ctx = lax.axis_index("ctx")
+    by_core = jnp.transpose(x_ext.reshape(seqs * keys, width)).reshape(width // (2 * row_count), 2, row_count, seqs * keys)
+    x_t = jnp.concatenate([lax.dynamic_index_in_dim(by_core, ctx % 2, 1, False), lax.dynamic_index_in_dim(by_core, 1 - ctx % 2, 1, False)])
+    x_t = x_t.reshape(width, seqs * keys)
     w_q, w_kv = w_first[:, :width], w_first[:, width:]
     x = inputs.reshape(rows, width)
     q = dot_nn(x, w_q).astype(bf16).reshape(seqs, tokens, width)
@@ -602,6 +675,7 @@
     peak = jnp.max(peaks, axis=(1, 2))
     o = mixed.reshape(rows, width)
 
+    x_t, w_rest = lax.optimization_barrier((x_t, w_rest))
     result, first_grad, o_grad, small, rest_grads = feed_forward(
         o, x, out_grad.reshape(rows, width), w_rest, norm_params
     )
@@ -609,22 +683,42 @@
     rest_sums = lax.psum_scatter(rest_grads, "ctx", scatter_dimension=0, tiled=True)
     dq, dk, dv = attend_bwd(windows, slopes2, q, kv, o_grad.reshape(seqs, tokens, width), mixed, lo, hi, lse)
 
-    xe = x_ext.reshape(seqs * keys, width)
-    dk_flat, dv_flat = dk.reshape(seqs * keys, width), dv.reshape(seqs * keys, width)
-    first_grads = jnp.concatenate(
-        [dot_tn(x, dq.reshape(rows, width)).astype(bf16), dot_tn(xe, dk_flat).astype(bf16), dot_tn(xe, dv_flat).astype(bf16)],
-        axis=1,
+    def owned_pair(columns, lowest):
+        local = unit_of - lowest
+        local = jnp.where((local >= 0) & (local < columns.shape[1] // width), local, -1)
+        if owner_count == 2:
+            ours = lax.dynamic_slice_in_dim(local, me * slots, slots, 0)
+            theirs = lax.dynamic_slice_in_dim(local, (1 - me) * slots, slots, 0)
+            return to_slots(ours, columns, slots, width), to_slots(theirs, columns, slots, width)
+        return None, to_slots(local, columns, owner_count * slots, width)
+
+    first_grads = first_gradients(
+        x_t, dq.reshape(rows, width), dk.reshape(seqs * keys, width), dv.reshape(seqs * keys, width), tokens
     )
-    first_sums = exchange_scatter(first_grads, "ctx")
-
-    key_part = (dot_nt(dk_flat, w_kv[:, :width]) + dot_nt(dv_flat, w_kv[:, width:])).reshape(seqs, keys, width)
-    input_grad = first_grad.reshape(seqs, tokens, width) + dot_nt(dq.reshape(rows, width), w_q).reshape(seqs, tokens, width)
-    input_grad = input_grad + key_part[:, REACH : REACH + tokens]
+    input_grad, rim = input_parts(first_grad.reshape(seqs, tokens, width), dq, dk, dv, w_first)
+    half = width // 2
+    value = (first_grads[:half].astype(f32) + swapped(first_grads[half:], "ctx", 1).astype(f32)).astype(bf16)
+    if owner_count == 2:
+        columns = 3 * width // 2
+        keep = lax.dynamic_slice_in_dim(value, me * columns, columns, 1)
+        got = swapped(lax.dynamic_slice_in_dim(value, (1 - me) * columns, columns, 1), "seq", 1)
+        got, input_grad, rim = lax.optimization_barrier((got, input_grad, rim))
+        value = (keep.astype(f32) + got.astype(f32)).astype(bf16)
+    value = value.reshape(-1, row_count, value.shape[1])
+
+    keep, give = owned_pair(rest_sums, 3)
+    bit = 2
+    while bit < lax.axis_size("ctx"):
+        if 2 * bit == lax.axis_size("ctx"):
+            value, give = lax.optimization_barrier((value, give))
+        value = halve(value.reshape((-1, 2) + value.shape[1:]), "ctx", bit, 1)
+        if bit == 2:
+            value, rim = lax.optimization_barrier((value, rim))
+        bit *= 2
+    first_sums = value[0]
     for n in range(pieces):
-        to_left = key_part[:, n * tokens : (n + 1) * tokens].astype(bf16)
-        to_right = key_part[:, REACH + (n + 1) * tokens : REACH + (n + 2) * tokens].astype(bf16)
-        input_grad = input_grad + shifted(to_left, "ctx", n - pieces).astype(f32)
-        input_grad = input_grad + shifted(to_right, "ctx", n + 1).astype(f32)
+        input_grad = input_grad + shifted(rim[:, n], "ctx", n - pieces).astype(f32)
+        input_grad = input_grad + shifted(rim[:, pieces + n], "ctx", n + 1).astype(f32)
 
     is_peak_row = (jnp.arange(8) == 4)[:, None]
     small = jnp.where(is_peak_row, jnp.pad(peak, (0, width - heads))[None], small)
@@ -639,18 +733,13 @@
     column_scale = jnp.repeat(jnp.sqrt(factors), width // heads)[None, :]
     correction = 1.0 - 0.5**STEP
 
-    def owned(columns, lowest):
-        count = columns.shape[1] // width
-        local = unit_of - lowest
-        local = jnp.where((local >= 0) & (local < count), local, -1)
-        if owner_count == 2:
-            keep = to_slots(lax.dynamic_slice_in_dim(local, me * slots, slots, 0), columns, slots, width)
-            give = to_slots(lax.dynamic_slice_in_dim(local, (1 - me) * slots, slots, 0), columns, slots, width)
-            return [keep, swapped(give, "seq", 1)]
-        every = to_slots(local, columns, owner_count * slots, width)
-        return [lax.psum_scatter(every, "seq", scatter_dimension=0, tiled=True)]
-
-    parts = owned(rest_sums, 3) + owned(first_sums, 0)
+    if owner_count == 2:
+        other = swapped(first_sums, "seq", 1)
+        whole = jnp.concatenate([jnp.where(me == 0, first_sums, other), jnp.where(me == 0, other, first_sums)], axis=1)
+        parts = [keep, swapped(give, "seq", 1), to_slots(jnp.where(my_units < 3, my_units, -1), whole, slots, width)]
+    else:
+        parts = [lax.psum_scatter(give, "seq", scatter_dimension=0, tiled=True),
+                 lax.psum_scatter(owned_pair(first_sums, 0)[1], "seq", scatter_dimension=0, tiled=True)]
     weight_grads, new_weights, new_first, new_second, weights_low = adam_slots(
         my_units, weights, first_moments, second_moments, parts, column_scale, correction, 0.5 / D**0.5
     )

time: 506 us -> 465 us (0.919)
  the two profiles are of different devices: /device:TPU:0 before, /device:TPU:4 now
where the time goes in v3:
time: 465 us; the launch traced here: 460 us
  Pallas kernels  232 us (50%)
  waiting for transfers between devices  110 us (24%)
  local copies, waits for them, and re-layouts  38 us (8%)
  starting transfers between devices  26.5 us (6%)
  other arithmetic  24.4 us (5%)
  between operations  14.7 us (3%)
  matrix products  14 us (3%)
    pallas_call x1, Pallas kernels, attend_bwd(): pl.pallas_call(bwd_kernel, grid=(pairs, seqs), in_specs=[smem, smem, tok,...  76 us
    pallas_call x1, Pallas kernels, feed_forward(): pl.pallas_call(ffn_kernel, grid=(2 * chunks,), in_specs=[full, full, full...  75 us
    ppermute x14, waiting for transfers between devices, swapped(): return lax.ppermute(value, axis, [(i, i ^ bit) for i in range(peers)])  55.8 us
    pallas_call x1, Pallas kernels, attend_fwd(): pl.pallas_call(fwd_kernel, grid=(pairs, seqs), in_specs=[smem, smem, pl.B...  48.3 us
    ppermute x4, waiting for transfers between devices, shifted(): return lax.ppermute(value, axis, pairs)  43.9 us
    unnamed x66, local copies, waits for them, and re-layouts  22.5 us
    ppermute x14, starting transfers between devices, swapped(): return lax.ppermute(value, axis, [(i, i ^ bit) for i in range(peers)])  17.6 us
    dot_general x2, matrix products, dot_nn(): lax.dot_general(a, b, (((1,), (0,)), ((), ())), preferred_element_type=f32)  14 us
  transfers between devices with their start and end apart: 21, of which 16 were waited for; matrix products, arithmetic and copies ran while one was open for 11% of the time, Pallas kernels for 33%

profile of v3, /device:TPU:4, one launch (start us, length us, event | category | flops | bytes accessed | tf_op | source)
XLA Modules:
  0.0 459.7 jit_solution(6818109706550669104)
XLA Ops:
  11.4 1.6 collective-permute-start.1
  13.1 5.6 %collective-permute-done.1 = bf16[48,2304]{1,0:T(8,128)(2,1)S(1)} collective-permute-done((bf16[48,2304]{1,0:T(8,128)(2,1)S(1)}, bf16[48,2304]{1,0:T(8,128)(2,1)S(1)}, u32[]{:S(2)}, u32[]{:S(2)}) %collective-permute-start.1) | collective-permute-done | bytes 221216 | tf_op jit(solution)/shard_map/ppermute | solution.py:230
  19.4 1.9 collective-permute-start.3
  21.4 2.4 collective-permute-start.2
  23.8 1.6 collective-permute-start
  25.4 16.0 %collective-permute-done.refs_1_ = bf16[9,48,768]{2,1,0:T(8,128)(2,1)S(1)} collective-permute-done((bf16[9,48,768]{2,1,0:T(8,128)(2,1)S(1)}, bf16[9,48,768]{2,1,0:T(8,128)(2,1)S(1)}, u32[]{:S(2)}, u32[]{:S(2)}) %collective-permute-start) | collective-permute-done | bytes 663584 | tf_op jit(solution)/shard_map/ppermute | solution.py:230
  41.5 1.8 pick_units.2
  43.3 26.8 %collective-permute-done.2 = bf16[2,512,768]{2,1,0:T(8,128)(2,1)} collective-permute-done((bf16[2,512,768]{2,1,0:T(8,128)(2,1)S(1)}, bf16[2,512,768]{2,1,0:T(8,128)(2,1)}, u32[]{:S(2)}, u32[]{:S(2)}) %collective-permute-start.2) | collective-permute-done | bytes 1572896 | tf_op jit(solution)/shard_map/ppermute | solution.py:225
  70.1 6.8 %all-gather.3.cloned.1.call-done.w_ref = bf16[768,2304]{1,0:T(8,128)(2,1)} async-done(((bf16[48,2304]{1,0:T(8,128)(2,1)}), bf16[768,2304]{1,0:T(8,128)(2,1)}) %all-gather.3.cloned.1.call-update) | async-done | bytes 3538960 | tf_op jit(solution)/shard_map/all_gather | solution.py:651
  78.5 4.4 fusion.1
  82.9 1.7 copy.33
  84.6 5.0 %pad_maximum_fusion = bf16[2,1536,768]{2,1,0:T(8,128)(2,1)} fusion(bf16[2,512,768]{2,1,0:T(8,128)(2,1)} %collective-permute-done.3, bf16[2,512,768]{2,1,0:T(8,128)(2,1)} %param.12, bf16[2,512,768]{2,1,0:T(8,128)(2,1)} %collective-permute-done.2), kind=kLoop, calls=%fused_computation.3 | loop fusion | flops 14155776 | bytes 9437184 | tf_op jit(solution)/shard_map/concatenate | solution.py:665
  89.6 6.8 %copy.38 = bf16[3072,768]{0,1:T(8,128)(2,1)} copy(bf16[3072,768]{1,0:T(8,128)(2,1)} %bitcast.67) | data formatting | bytes 9437184 | tf_op jit(solution)/shard_map/reshape | solution.py:673
  96.4 3.0 dynamic-slice_bitcast_fusion.1
  99.4 2.8 pad_maximum_fusion.1
  103.3 9.6 %convolution_convert_fusion = bf16[3072,1536]{1,0:T(8,128)(2,1)} fusion(bf16[3072,768]{1,0:T(8,128)(2,1)S(1)} %bitcast.70, bf16[768,2304]{1,0:T(8,128)(2,1)S(1)} %copy-done.7), kind=kOutput, calls=%fused_computation | convolution fusion | flops 7252475904 | bytes 16515072 | tf_op jit(solution)/shard_map/dot_general | solution.py:25
  112.9 3.9 copy-done.10
  116.8 48.3 %attend_fwd.1 = (bf16[2,512,768]{2,1,0:T(8,128)(2,1)S(1)}, f32[2,6,2,512]{3,2,1,0:T(2,128)S(1)}, f32[12,8,256]{2,1,0:T(8,128)S(1)}) custom-call(s32[12]{0:T(128)S(1)} %copy-done.9, f32[12]{0:T(128)S(1)} %power_multiply_fusion.slope_ref, bf16[2,512,768]{2,1,0:T(8,128)(2,1)S(1)} %bitcast.55, bf16[2,1536,1536]{2,1,0:T(8,128)(2,1)S(1)} %bitcast.59, ...), custom_call_target="tpu_custom_call" | custom-call | flops 20000000000 | bytes 10000000 | tf_op jit(solution)/shard_map/attend_fwd/pallas_call | solution.py:106
  166.2 2.4 all-gather.5.cloned.1.call-done.wo_ref.wg_ref.wu_ref.wd_ref
  168.6 75.0 %feed_forward.1 = (bf16[1024,768]{1,0:T(8,128)(2,1)}, f32[1024,768]{1,0:T(8,128)}, bf16[1024,768]{1,0:T(8,128)(2,1)}, f32[8,768]{1,0:T(8,128)}, bf16[768,9984]{1,0:T(8,128)(2,1)}) custom-call(bf16[1024,768]{1,0:T(8,128)(2,1)} %bitcast.65, bf16[1024,768]{1,0:T(8,128)(2,1)} %bitcast.77, bf16[1024,768]{1,0:T(8,128)(2,1)} %bitcast.79, ...), custom_call_target="tpu_custom_call" | custom-call | flops 46000001024 | bytes 60000000 | tf_op jit(solution)/shard_map/feed_forward/pallas_call | solution.py:491
  243.7 1.5 copy-done.18
  245.2 1.4 copy-done.19
  246.6 76.0 %attend_bwd.1 = (bf16[2,512,768]{2,1,0:T(8,128)(2,1)S(1)}, bf16[2,1536,768]{2,1,0:T(8,128)(2,1)S(1)}, bf16[2,1536,768]{2,1,0:T(8,128)(2,1)}) custom-call(s32[12]{0:T(128)S(1)} %copy-done.9, f32[12]{0:T(128)S(1)} %power_multiply_fusion.slope_ref, bf16[2,512,768]{2,1,0:T(8,128)(2,1)S(1)} %bitcast.56, bf16[2,1536,1536]{2,1,0:T(8,128)(2,1)} %bitcast.57, ...), custom_call_target="tpu_custom_call" | custom-call | flops 49999998976 | bytes 20000000 | tf_op jit(solution)/shard_map/attend_bwd/pallas_call | solution.py:200
  322.6 4.6 copy-done.13
  327.2 11.5 %first_gradients.1 = bf16[768,2304]{1,0:T(8,128)(2,1)S(1)} custom-call(bf16[768,3072]{1,0:T(8,128)(2,1)S(1)} %bitcast.54, bf16[1024,768]{1,0:T(8,128)(2,1)S(1)} %bitcast.64, bf16[3072,768]{1,0:T(8,128)(2,1)S(1)} %bitcast.61, bf16[3072,768]{1,0:T(8,128)(2,1)S(1)} %bitcast.62), custom_call_target="tpu_custom_call" | custom-call | flops 8999999488 | bytes 20000000 | tf_op jit(solution)/shard_map/first_gradients/pallas_call | solution.py:559
  338.7 1.7 copy-done.3
  341.7 2.7 collective-permute-done.9
  345.2 3.4 collective-permute-done.10
  348.7 1.6 collective-permute-start.11
  350.4 2.7 add_convert_fusion
  353.2 1.5 collective-permute-start.5
  354.7 2.6 copy-done.12
  358.7 11.7 %input_parts.1 = (f32[2,512,768]{2,1,0:T(8,128)S(1)}, bf16[2,2,512,768]{3,2,1,0:T(8,128)(2,1)S(1)}) custom-call(f32[2,512,768]{2,1,0:T(8,128)S(1)} %bitcast.63, bf16[2,512,768]{2,1,0:T(8,128)(2,1)S(1)} %copy-done.16, bf16[2,1536,768]{2,1,0:T(8,128)(2,1)S(1)} %copy-done.12, bf16[2,1536,768]{2,1,0:T(8,128)(2,1)} %get-tuple-element.55.v_ref, ...), custom_call_target="tpu_custom_call" | custom-call | flops 8999999488 | bytes 20000000 | tf_op jit(solution)/shard_map/input_parts/pallas_call | solution.py:595
  370.4 1.7 copy-done.4
  372.1 1.5 collective-permute-start.12
  376.3 1.7 collective-permute-done.12
  379.5 2.4 collective-permute-done.13
  382.0 4.2 collective-permute-done.6
  389.8 2.0 collective-permute-start.7
  393.1 2.4 collective-permute-start.8
  396.2 5.8 %collective-permute-done.14 = bf16[2,48,1152]{2,1,0:T(8,128)(2,1)S(1)} collective-permute-done((bf16[2,48,1152]{2,1,0:T(8,128)(2,1)S(1)}, bf16[2,48,1152]{2,1,0:T(8,128)(2,1)S(1)}, u32[]{:S(2)}, u32[]{:S(2)}) %collective-permute-start.14) | collective-permute-done | bytes 221216 | tf_op jit(solution)/shard_map/ppermute | solution.py:230
  404.8 2.9 collective-permute-start.16
  408.4 4.8 %collective-permute-done.16 = bf16[1,48,1152]{2,1,0:T(8,128)(2,1)S(1)} collective-permute-done((bf16[1,48,1152]{2,1,0:T(8,128)(2,1)S(1)}, bf16[1,48,1152]{2,1,0:T(8,128)(2,1)S(1)}, u32[]{:S(2)}, u32[]{:S(2)}) %collective-permute-start.16) | collective-permute-done | bytes 110624 | tf_op jit(solution)/shard_map/ppermute | solution.py:230
  413.2 1.6 collective-permute-start.17
  414.8 17.1 %collective-permute-done.8 = bf16[2,512,768]{2,1,0:T(8,128)(2,1)S(1)} collective-permute-done((bf16[2,512,768]{2,1,0:T(8,128)(2,1)}, bf16[2,512,768]{2,1,0:T(8,128)(2,1)S(1)}, u32[]{:S(2)}, u32[]{:S(2)}) %collective-permute-start.8) | collective-permute-done | bytes 1572896 | tf_op jit(solution)/shard_map/ppermute | solution.py:225
  431.9 4.6 %convert_add_fusion = f32[2,512,768]{2,1,0:T(8,128)} fusion(bf16[2,512,768]{2,1,0:T(8,128)(2,1)S(1)} %collective-permute-done.8, f32[2,512,768]{2,1,0:T(8,128)} %copy-done.4, bf16[2,512,768]{2,1,0:T(8,128)(2,1)} %collective-permute-done.7), kind=kLoop, calls=%fused_computation.6 | loop fusion | flops 3145728 | bytes 9437184 | tf_op jit(solution)/shard_map/add | solution.py:721
  438.5 8.7 %collective-permute-done.15.refs_1_ = bf16[9,48,768]{2,1,0:T(8,128)(2,1)S(1)} collective-permute-done((bf16[9,48,768]{2,1,0:T(8,128)(2,1)S(1)}, bf16[9,48,768]{2,1,0:T(8,128)(2,1)S(1)}, u32[]{:S(2)}, u32[]{:S(2)}) %collective-permute-start.15) | collective-permute-done | bytes 663584 | tf_op jit(solution)/shard_map/ppermute | solution.py:230
  447.2 5.5 %adam_slots.1 = (f32[9,48,768]{2,1,0:T(8,128)}, f32[9,48,768]{2,1,0:T(8,128)}, f32[9,48,768]{2,1,0:T(8,128)}, f32[9,48,768]{2,1,0:T(8,128)}, bf16[9,48,768]{2,1,0:T(8,128)(2,1)}) custom-call(s32[9]{0:T(128)S(1)} %get-tuple-element.81.unit_ref, f32[9,48,768]{2,1,0:T(8,128)S(1)} %copy-done, f32[9,48,768]{2,1,0:T(8,128)S(1)} %copy-done.5, ...), custom_call_target="tpu_custom_call" | custom-call | tf_op jit(solution)/shard_map/adam_slots/pallas_call | solution.py:333
  (132 shorter events, 27.9 us)
Async XLA Ops:
  7.2 5.8 %copy-start.27 = (s32[16]{0:T(128)S(1)}, s32[16]{0:T(128)}, u32[]{:S(2)}) copy-start(s32[16]{0:T(128)} %param.16) | copy-start | bytes 196
  7.2 12.2 %copy-start.21 = (bf16[2,512,768]{2,1,0:T(8,128)(2,1)S(1)}, bf16[2,512,768]{2,1,0:T(8,128)(2,1)}, u32[]{:S(2)}) copy-start(bf16[2,512,768]{2,1,0:T(8,128)(2,1)} %param.12) | copy-start | bytes 4718596
  7.2 69.7 %all-gather.3.cloned.1.call-start = ((), (), s32[]{:S(2)}) async-start(), calls=%async_computation.1 | async-start | bytes 3760128 | tf_op jit(solution)/shard_map/all_gather | solution.py:651
  11.4 65.6 %copy-start.23 = (s32[2,8192]{1,0:T(2,128)S(1)}, s32[2,8192]{1,0:T(2,128)}, u32[]{:S(2)}) copy-start(s32[2,8192]{1,0:T(2,128)} %param.14) | copy-start | bytes 196612
  11.4 7.2 %collective-permute-start.1 = (bf16[48,2304]{1,0:T(8,128)(2,1)S(1)}, bf16[48,2304]{1,0:T(8,128)(2,1)S(1)}, u32[]{:S(2)}, u32[]{:S(2)}) collective-permute-start(bf16[48,2304]{1,0:T(8,128)(2,1)S(1)} %pick_units.3), channel_id=1, source_target_pairs={{0,1},{1,0},{2,3},{3,2},{4,5},{5,4},{6,7},{7,6},{8,9},{9,8},{10,11... | collective-permute-start | bytes 663560 | tf_op jit(solution)/shard_map/ppermute | solution.py:230
  19.4 149.2 %all-gather.5.cloned.1.call-start = ((), (), s32[]{:S(2)}) async-start(), calls=%async_computation.2 | async-start | bytes 17965056 | tf_op jit(solution)/shard_map/all_gather | solution.py:654
  19.4 23.8 %collective-permute-start.3 = (bf16[2,512,768]{2,1,0:T(8,128)(2,1)S(1)}, bf16[2,512,768]{2,1,0:T(8,128)(2,1)}, u32[]{:S(2)}, u32[]{:S(2)}) collective-permute-start(bf16[2,512,768]{2,1,0:T(8,128)(2,1)S(1)} %copy-done.21), channel_id=1, source_target_pairs={{2,0},{4,2},{6,4},{8,6},{10,8},{12,10},{14,12},{16,14},{18,16},{20... | collective-permute-start | bytes 4718600 | tf_op jit(solution)/shard_map/ppermute | solution.py:225
  21.4 48.7 %collective-permute-start.2 = (bf16[2,512,768]{2,1,0:T(8,128)(2,1)S(1)}, bf16[2,512,768]{2,1,0:T(8,128)(2,1)}, u32[]{:S(2)}, u32[]{:S(2)}) collective-permute-start(bf16[2,512,768]{2,1,0:T(8,128)(2,1)S(1)} %copy-done.21), channel_id=1, source_target_pairs={{0,2},{2,4},{4,6},{6,8},{8,10},{10,12},{12,14},{14,16},{16,18},{18... | collective-permute-start | bytes 4718600 | tf_op jit(solution)/shard_map/ppermute | solution.py:225
  23.8 17.7 %collective-permute-start = (bf16[9,48,768]{2,1,0:T(8,128)(2,1)S(1)}, bf16[9,48,768]{2,1,0:T(8,128)(2,1)S(1)}, u32[]{:S(2)}, u32[]{:S(2)}) collective-permute-start(bf16[9,48,768]{2,1,0:T(8,128)(2,1)S(1)} %convert_element_type.83.refs_0_), channel_id=1, source_target_pairs={{0,1},{1,0},{2,3},{3,2},{4,5},{5,4},{6,7},{7,6},{8,9},{9,8},{10,11... | collective-permute-start | bytes 1990664 | tf_op jit(solution)/shard_map/ppermute | solution.py:230
  76.9 325.9 %reduce-scatter.2.cloned.1.call-start = ((), (), s32[]{:S(2)}) async-start(), calls=%async_computation.3 | async-start | bytes 16293888 | tf_op jit(solution)/shard_map/reduce_scatter | solution.py:683
  89.6 12.6 %slice-start.2 = ((s8[4718592]{0:T(1024)(128)(4,1)}), s8[524288]{0:T(1024)(128)(4,1)S(1)}, s32[]{:S(2)}) async-start(s8[4718592]{0:T(1024)(128)(4,1)} %bitcast.68), calls=%async_computation.6 | async-start | bytes 1048576
  96.4 5.8 %slice-start.3 = ((s8[4718592]{0:T(1024)(128)(4,1)}), s8[4194304]{0:T(1024)(128)(4,1)S(1)}, s32[]{:S(2)}) async-start(s8[4718592]{0:T(1024)(128)(4,1)} %bitcast.68), calls=%async_computation.7 | async-start | bytes 8388608
  99.4 3.9 copy-start.7
  103.3 9.6 %copy-start.9 = (s32[12]{0:T(128)S(1)}, s32[12]{0:T(128)}, u32[]{:S(2)}) copy-start(s32[12]{0:T(128)} %win_ref.3) | copy-start | bytes 148
  112.9 3.9 copy-start.10
  243.7 78.9 %slice-start = ((s8[4718592]{0:T(1024)(128)(4,1)}), s8[524288]{0:T(1024)(128)(4,1)S(1)}, s32[]{:S(2)}) async-start(s8[4718592]{0:T(1024)(128)(4,1)} %bitcast.52), calls=%async_computation.4 | async-start | bytes 1048576
  243.7 1.5 copy-start.18
  246.6 76.0 %slice-start.1 = ((s8[4718592]{0:T(1024)(128)(4,1)}), s8[4194304]{0:T(1024)(128)(4,1)S(1)}, s32[]{:S(2)}) async-start(s8[4718592]{0:T(1024)(128)(4,1)} %bitcast.52), calls=%async_computation.5 | async-start | bytes 8388608
  322.6 16.2 %copy-start.11 = (bf16[2,1536,768]{2,1,0:T(8,128)(2,1)}, bf16[2,1536,768]{2,1,0:T(8,128)(2,1)S(1)}, u32[]{:S(2)}) copy-start(bf16[2,1536,768]{2,1,0:T(8,128)(2,1)S(1)} %get-tuple-element.54.k_ref) | copy-start | bytes 14155780
  322.6 16.2 %copy-start.15 = (bf16[2,512,768]{2,1,0:T(8,128)(2,1)}, bf16[2,512,768]{2,1,0:T(8,128)(2,1)S(1)}, u32[]{:S(2)}) copy-start(bf16[2,512,768]{2,1,0:T(8,128)(2,1)S(1)} %get-tuple-element.53.q_ref) | copy-start | bytes 4718596
  322.6 4.6 copy-start.13
  338.7 1.7 copy-start.3
  340.6 9.8 %collective-permute-start.4 = (bf16[384,2304]{1,0:T(8,128)(2,1)S(1)}, bf16[384,2304]{1,0:T(8,128)(2,1)}, u32[]{:S(2)}, u32[]{:S(2)}) collective-permute-start(bf16[384,2304]{1,0:T(8,128)(2,1)S(1)} %slice.50), channel_id=1, source_target_pairs={{0,2},{2,0},{4,6},{6,4},{8,10},{10,8},{12,14},{14,12},{16,18},{18,... | collective-permute-start | bytes 5308424 | tf_op jit(solution)/shard_map/ppermute | solution.py:230
  341.5 2.9 collective-permute-start.9
  344.5 4.2 collective-permute-start.10
  348.7 6.0 %copy-start.8 = (bf16[768,2304]{1,0:T(8,128)(2,1)S(1)}, bf16[768,2304]{1,0:T(8,128)(2,1)}, u32[]{:S(2)}) copy-start(bf16[768,2304]{1,0:T(8,128)(2,1)} %all-gather.3.cloned.1.call-done.w_ref) | copy-start | bytes 10616836
  348.7 6.0 %copy-start.14 = (f32[1024,768]{1,0:T(8,128)S(1)}, f32[1024,768]{1,0:T(8,128)}, u32[]{:S(2)}) copy-start(f32[1024,768]{1,0:T(8,128)} %get-tuple-element.56) | copy-start | bytes 9437188
  348.7 23.3 %collective-permute-start.11 = (f32[8,768]{1,0:T(8,128)S(1)}, f32[8,768]{1,0:T(8,128)S(1)}, u32[]{:S(2)}, u32[]{:S(2)}) collective-permute-start(f32[8,768]{1,0:T(8,128)S(1)} %add_select_fusion.3), channel_id=1, source_target_pairs={{0,8},{2,10},{4,12},{6,14},{8,0},{10,2},{12,4},{14,6},{16,24},{18,... | collective-permute-start | bytes 73736 | tf_op jit(solution)/shard_map/ppermute | solution.py:230
  353.2 21.0 %collective-permute-start.5 = (bf16[384,1152]{1,0:T(8,128)(2,1)S(1)}, bf16[384,1152]{1,0:T(8,128)(2,1)S(1)}, u32[]{:S(2)}, u32[]{:S(2)}) collective-permute-start(bf16[384,1152]{1,0:T(8,128)(2,1)S(1)} %constant_dynamic-slice_fusion.1), channel_id=1, source_target_pairs={{0,1},{1,0},{2,3},{3,2},{4,5},{5,4},{6,7},{7,6},{8,9},{9,8},{10,11... | collective-permute-start | bytes 2654216 | tf_op jit(solution)/shard_map/ppermute | solution.py:230
  354.7 2.6 copy-start.12
  370.4 1.7 copy-start.4
  372.1 5.9 %collective-permute-start.12 = (f32[8,768]{1,0:T(8,128)S(1)}, f32[8,768]{1,0:T(8,128)S(1)}, u32[]{:S(2)}, u32[]{:S(2)}) collective-permute-start(f32[8,768]{1,0:T(8,128)S(1)} %add_select_fusion.2), channel_id=1, source_target_pairs={{0,16},{2,18},{4,20},{6,22},{8,24},{10,26},{12,28},{14,30},{16,0},... | collective-permute-start | bytes 73736 | tf_op jit(solution)/shard_map/ppermute | solution.py:230
  374.4 3.7 copy-start.20
  375.3 11.0 %collective-permute-start.6 = (bf16[4,48,1152]{2,1,0:T(8,128)(2,1)}, bf16[4,48,1152]{2,1,0:T(8,128)(2,1)}, u32[]{:S(2)}, u32[]{:S(2)}) collective-permute-start(bf16[4,48,1152]{2,1,0:T(8,128)(2,1)} %dynamic-slice_bitcast_fusion.2), channel_id=1, source_target_pairs={{0,4},{2,6},{4,0},{6,2},{8,12},{10,14},{12,8},{14,10},{16,20},{18,... | collective-permute-start | bytes 1327112 | tf_op jit(solution)/shard_map/ppermute | solution.py:230
  378.1 3.8 collective-permute-start.13
  387.5 14.5 %collective-permute-start.14 = (bf16[2,48,1152]{2,1,0:T(8,128)(2,1)S(1)}, bf16[2,48,1152]{2,1,0:T(8,128)(2,1)S(1)}, u32[]{:S(2)}, u32[]{:S(2)}) collective-permute-start(bf16[2,48,1152]{2,1,0:T(8,128)(2,1)S(1)} %dynamic-slice_bitcast_fusion.3), channel_id=1, source_target_pairs={{0,8},{2,10},{4,12},{6,14},{8,0},{10,2},{12,4},{14,6},{16,24},{18,... | collective-permute-start | bytes 663560 | tf_op jit(solution)/shard_map/ppermute | solution.py:230
  389.8 5.7 %copy-start.24 = (f32[4,768]{1,0:T(4,128)S(1)}, f32[4,768]{1,0:T(4,128)}, u32[]{:S(2)}) copy-start(f32[4,768]{1,0:T(4,128)} %norm_ref.1) | copy-start | bytes 36868
  389.8 5.7 %copy-start.25 = (f32[4,768]{1,0:T(4,128)S(1)}, f32[4,768]{1,0:T(4,128)}, u32[]{:S(2)}) copy-start(f32[4,768]{1,0:T(4,128)} %param.21) | copy-start | bytes 36868
  389.8 5.7 %copy-start.26 = (f32[4,768]{1,0:T(4,128)S(1)}, f32[4,768]{1,0:T(4,128)}, u32[]{:S(2)}) copy-start(f32[4,768]{1,0:T(4,128)} %param.22) | copy-start | bytes 36868
  389.8 25.0 %collective-permute-start.7 = (bf16[2,512,768]{2,1,0:T(8,128)(2,1)}, bf16[2,512,768]{2,1,0:T(8,128)(2,1)}, u32[]{:S(2)}, u32[]{:S(2)}) collective-permute-start(bf16[2,512,768]{2,1,0:T(8,128)(2,1)} %slice_bitcast_fusion), channel_id=1, source_target_pairs={{2,0},{4,2},{6,4},{8,6},{10,8},{12,10},{14,12},{16,14},{18,16},{20... | collective-permute-start | bytes 4718600 | tf_op jit(solution)/shard_map/ppermute | solution.py:225
  393.1 38.8 %collective-permute-start.8 = (bf16[2,512,768]{2,1,0:T(8,128)(2,1)}, bf16[2,512,768]{2,1,0:T(8,128)(2,1)S(1)}, u32[]{:S(2)}, u32[]{:S(2)}) collective-permute-start(bf16[2,512,768]{2,1,0:T(8,128)(2,1)} %slice_bitcast_fusion.1), channel_id=1, source_target_pairs={{0,2},{2,4},{4,6},{6,8},{8,10},{10,12},{12,14},{14,16},{16,18},{18... | collective-permute-start | bytes 4718600 | tf_op jit(solution)/shard_map/ppermute | solution.py:225
  404.8 8.4 %collective-permute-start.16 = (bf16[1,48,1152]{2,1,0:T(8,128)(2,1)S(1)}, bf16[1,48,1152]{2,1,0:T(8,128)(2,1)S(1)}, u32[]{:S(2)}, u32[]{:S(2)}) collective-permute-start(bf16[1,48,1152]{2,1,0:T(8,128)(2,1)S(1)} %constant_dynamic-slice_fusion), channel_id=1, source_target_pairs={{0,16},{2,18},{4,20},{6,22},{8,24},{10,26},{12,28},{14,30},{16,0},... | collective-permute-start | bytes 331784 | tf_op jit(solution)/shard_map/ppermute | solution.py:230
  413.2 23.9 %copy-start.2 = (bf16[48,9984]{1,0:T(8,128)(2,1)S(1)}, bf16[48,9984]{1,0:T(8,128)(2,1)}, u32[]{:S(2)}) copy-start(bf16[48,9984]{1,0:T(8,128)(2,1)} %reduce-scatter.2.cloned.1.call-done.col_ref) | copy-start | bytes 2875396
  413.2 24.6 %collective-permute-start.17 = (bf16[48,1152]{1,0:T(8,128)(2,1)S(1)}, bf16[48,1152]{1,0:T(8,128)(2,1)S(1)}, u32[]{:S(2)}, u32[]{:S(2)}) collective-permute-start(bf16[48,1152]{1,0:T(8,128)(2,1)S(1)} %fusion.5), channel_id=1, source_target_pairs={{0,1},{1,0},{2,3},{3,2},{4,5},{5,4},{6,7},{7,6},{8,9},{9,8},{10,11... | collective-permute-start | bytes 331784 | tf_op jit(solution)/shard_map/ppermute | solution.py:230
  431.9 15.3 %copy-start.6 = (f32[9,48,768]{2,1,0:T(8,128)S(1)}, f32[9,48,768]{2,1,0:T(8,128)}, u32[]{:S(2)}) copy-start(f32[9,48,768]{2,1,0:T(8,128)} %v_ref.1) | copy-start | bytes 3981316
  436.5 10.7 %copy-start = (f32[9,48,768]{2,1,0:T(8,128)S(1)}, f32[9,48,768]{2,1,0:T(8,128)}, u32[]{:S(2)}) copy-start(f32[9,48,768]{2,1,0:T(8,128)} %w_ref.1) | copy-start | bytes 3981316
  436.5 10.7 %copy-start.5 = (f32[9,48,768]{2,1,0:T(8,128)S(1)}, f32[9,48,768]{2,1,0:T(8,128)}, u32[]{:S(2)}) copy-start(f32[9,48,768]{2,1,0:T(8,128)} %m_ref.1) | copy-start | bytes 3981316
  436.5 10.7 %collective-permute-start.15 = (bf16[9,48,768]{2,1,0:T(8,128)(2,1)S(1)}, bf16[9,48,768]{2,1,0:T(8,128)(2,1)S(1)}, u32[]{:S(2)}, u32[]{:S(2)}) collective-permute-start(bf16[9,48,768]{2,1,0:T(8,128)(2,1)S(1)} %to_slots.4), channel_id=1, source_target_pairs={{0,1},{1,0},{2,3},{3,2},{4,5},{5,4},{6,7},{7,6},{8,9},{9,8},{10,11... | collective-permute-start | bytes 1990664 | tf_op jit(solution)/shard_map/ppermute | solution.py:230
  (6 other events, 6.7 us)
Sparse Core Ops, SparseCore 0:
  19.5 57.3 all-gather.2
  79.1 89.4 all-gather.4
  243.8 159.0 reduce-scatter.1

commit v4 on v3

--- a/solution.py
+++ b/solution.py
@@ -143,7 +143,6 @@
     kt_ref[...] = k_ref[0].T
     dka_ref[...] = jnp.zeros(dka_ref.shape, f32)
     dva_ref[...] = jnp.zeros(dva_ref.shape, f32)
-    rows = lax.broadcasted_iota(jnp.int32, (QB, QB), 0)
     lane = lax.broadcasted_iota(jnp.int32, (1, 128), 1)
     ones = jnp.ones((16, 128), bf16)
     for h in range(2):
@@ -167,14 +166,16 @@
             def branch(c):
                 first = REACH - c * 128
                 dqt = None
-                for t in range(1 + c):
-                    b = first + t * QB
-                    at = pl.ds(qb * QB + b, QB)
+                KB = (1 + c) * QB
+                for t in range(1):
+                    b = first
+                    at = pl.ds(qb * QB + b, KB)
                     s = dot_nt(k_ref[0, at, :], q)
                     dp = dot_nt(v_ref[0, at, :], do)
-                    kk = rows + (qb * QB + b)
-                    z = s * LOG2E + (bias_ref[h, pl.ds(b, QB), :] - lse)
-                    p = jnp.exp2(jnp.where((kk >= lo) & (kk <= hi), z, NEG))
+                    at_first = qb * QB + b
+                    rows = lax.broadcasted_iota(jnp.int32, (KB, QB), 0)
+                    z = s * LOG2E + (bias_ref[h, pl.ds(b, KB), :] - lse)
+                    p = jnp.exp2(jnp.where((rows >= lo - at_first) & (rows <= hi - at_first), z, NEG))
                     ds = (p * (dp - dsum)).astype(bf16)
                     dva_ref[at, :] += dot_nn(p.astype(bf16), do)
                     dka_ref[at, :] += dot_nn(ds, q)
@@ -245,11 +246,28 @@
     return back, jnp.sum(grad * hat, axis=0, keepdims=True), jnp.sum(grad, axis=0, keepdims=True)
 
 
-def halve(value, axis, bit, dim):
+def exchange(small, keep, give, axis, bit, beside=()):
+    high = small.astype(bf16)
+    both = jnp.concatenate([high, (small - high.astype(f32)).astype(bf16)])
+    lead, cols = give.shape[:-2], give.shape[-1]
+    flat = give.reshape(-1, cols)
+    tail = jnp.pad(both, ((0, 0), (0, cols - both.shape[1])))
+    got = swapped(jnp.concatenate([flat, tail]), axis, bit)
+    if beside:
+        got, beside = lax.optimization_barrier((got, beside))
+    terms = got[flat.shape[0] :, : both.shape[1]].astype(f32)
+    theirs = terms[:8] + terms[8:]
+    ours = both[:8].astype(f32) + both[8:].astype(f32)
+    is_peak_row = lax.broadcasted_iota(jnp.int32, (8, 1), 0) == 4
+    small = jnp.where(is_peak_row, jnp.maximum(ours, theirs), ours + theirs)
+    total = (keep.astype(f32) + got[: flat.shape[0]].reshape(give.shape).astype(f32)).astype(bf16)
+    return (small, total, *beside)
+
+
+def halve(small, value, axis, bit):
     side = (lax.axis_index(axis) // bit) % 2
-    keep = lax.dynamic_index_in_dim(value, side, dim, False)
-    got = swapped(lax.dynamic_index_in_dim(value, 1 - side, dim, False), axis, bit)
-    return (keep.astype(f32) + got.astype(f32)).astype(value.dtype)
+    keep = lax.dynamic_index_in_dim(value, side, 1, False)
+    return exchange(small, keep, lax.dynamic_index_in_dim(value, 1 - side, 1, False), axis, bit)
 
 
 def pick_units(slot_of, sources, count, pad=0):
@@ -692,42 +710,43 @@
             return to_slots(ours, columns, slots, width), to_slots(theirs, columns, slots, width)
         return None, to_slots(local, columns, owner_count * slots, width)
 
+    input_grad, rim = input_parts(first_grad.reshape(seqs, tokens, width), dq, dk, dv, w_first)
+
+    is_peak_row = (jnp.arange(8) == 4)[:, None]
+    small = jnp.where(is_peak_row, jnp.pad(peak, (0, width - heads))[None], small)
     first_grads = first_gradients(
         x_t, dq.reshape(rows, width), dk.reshape(seqs * keys, width), dv.reshape(seqs * keys, width), tokens
     )
-    input_grad, rim = input_parts(first_grad.reshape(seqs, tokens, width), dq, dk, dv, w_first)
     half = width // 2
-    value = (first_grads[:half].astype(f32) + swapped(first_grads[half:], "ctx", 1).astype(f32)).astype(bf16)
+    small, value = exchange(small, first_grads[:half], first_grads[half:], "ctx", 1)
     if owner_count == 2:
         columns = 3 * width // 2
-        keep = lax.dynamic_slice_in_dim(value, me * columns, columns, 1)
-        got = swapped(lax.dynamic_slice_in_dim(value, (1 - me) * columns, columns, 1), "seq", 1)
-        got, input_grad, rim = lax.optimization_barrier((got, input_grad, rim))
-        value = (keep.astype(f32) + got.astype(f32)).astype(bf16)
+        small, value, input_grad, rim = exchange(
+            small,
+            lax.dynamic_slice_in_dim(value, me * columns, columns, 1),
+            lax.dynamic_slice_in_dim(value, (1 - me) * columns, columns, 1),
+            "seq", 1, (input_grad, rim),
+        )
     value = value.reshape(-1, row_count, value.shape[1])
-
     keep, give = owned_pair(rest_sums, 3)
     bit = 2
+    arrived = []
     while bit < lax.axis_size("ctx"):
         if 2 * bit == lax.axis_size("ctx"):
-            value, give = lax.optimization_barrier((value, give))
-        value = halve(value.reshape((-1, 2) + value.shape[1:]), "ctx", bit, 1)
+            value, arrived, _ = lax.optimization_barrier((value, arrived, give))
+        small, value = halve(small, value.reshape((-1, 2) + value.shape[1:]), "ctx", bit)
         if bit == 2:
-            value, rim = lax.optimization_barrier((value, rim))
+            for n in range(pieces):
+                arrived += [shifted(rim[:, n], "ctx", n - pieces), shifted(rim[:, pieces + n], "ctx", n + 1)]
         bit *= 2
+    for piece in arrived:
+        input_grad = input_grad + piece.astype(f32)
     first_sums = value[0]
-    for n in range(pieces):
-        input_grad = input_grad + shifted(rim[:, n], "ctx", n - pieces).astype(f32)
-        input_grad = input_grad + shifted(rim[:, pieces + n], "ctx", n + 1).astype(f32)
-
-    is_peak_row = (jnp.arange(8) == 4)[:, None]
-    small = jnp.where(is_peak_row, jnp.pad(peak, (0, width - heads))[None], small)
-    for axis in ("ctx", "seq"):
-        bit = 1
-        while bit < lax.axis_size(axis):
-            other = swapped(small, axis, bit)
-            small = jnp.where(is_peak_row, jnp.maximum(small, other), small + other)
-            bit *= 2
+    bit = 1
+    while owner_count != 2 and bit < owner_count:
+        other = swapped(small, "seq", bit)
+        small = jnp.where(is_peak_row, jnp.maximum(small, other), small + other)
+        bit *= 2
     norm_grads = small[:4]
     factors = clip_level / jnp.maximum(small[4, :heads], clip_level)
     column_scale = jnp.repeat(jnp.sqrt(factors), width // heads)[None, :]

time: 465 us -> 464 us (level)
  waiting for transfers between devices: 110 us -> 123 us
  Pallas kernels: 232 us -> 224 us
  starting transfers between devices: 26.5 us -> 20.2 us
    ppermute x14 -> x9, waiting for transfers between devices: 55.8 us -> 67.7 us  [swapped(): return lax.ppermute(value, axis, [(i, i ^ bit) for i in range(peers)])]
    pallas_call x1, Pallas kernels: 76 us -> 65.3 us  [attend_bwd(): pl.pallas_call(bwd_kernel, grid=(pairs, seqs), in_specs=[smem, smem, tok,...]
    ppermute x14 -> x9, starting transfers between devices: 17.6 us -> 11.5 us  [swapped(): return lax.ppermute(value, axis, [(i, i ^ bit) for i in range(peers)])]
  transfers between devices with their start and end apart: 21 -> 16, of which waited for: 16 -> 13; matrix products, arithmetic and copies ran while one was open for 11% -> 11% of each run, Pallas kernels for 33% -> 31%
where the time goes in v4:
time: 464 us; the launch traced here: 457 us
  Pallas kernels  224 us (48%)
  waiting for transfers between devices  123 us (27%)
  local copies, waits for them, and re-layouts  34.9 us (8%)
  other arithmetic  25.1 us (5%)
  starting transfers between devices  20.2 us (4%)
  between operations  14.6 us (3%)
  matrix products  14 us (3%)
    pallas_call x1, Pallas kernels, feed_forward(): pl.pallas_call(ffn_kernel, grid=(2 * chunks,), in_specs=[full, full, full...  75.3 us
    ppermute x9, waiting for transfers between devices, swapped(): return lax.ppermute(value, axis, [(i, i ^ bit) for i in range(peers)])  67.7 us
    pallas_call x1, Pallas kernels, attend_bwd(): pl.pallas_call(bwd_kernel, grid=(pairs, seqs), in_specs=[smem, smem, tok,...  65.3 us
    pallas_call x1, Pallas kernels, attend_fwd(): pl.pallas_call(fwd_kernel, grid=(pairs, seqs), in_specs=[smem, smem, pl.B...  47.9 us
    ppermute x4, waiting for transfers between devices, shifted(): return lax.ppermute(value, axis, pairs)  42.1 us
    unnamed x66, local copies, waits for them, and re-layouts  20.1 us
    dot_general x2, matrix products, dot_nn(): lax.dot_general(a, b, (((1,), (0,)), ((), ())), preferred_element_type=f32)  14 us
    pallas_call x1, Pallas kernels, first_gradients(): pl.pallas_call(kernel, grid=(3, per), in_specs=[pl.BlockSpec((width, tota...  11.8 us
  transfers between devices with their start and end apart: 16, of which 13 were waited for; matrix products, arithmetic and copies ran while one was open for 11% of the time, Pallas kernels for 31%

profile of v4, /device:TPU:4, one launch (start us, length us, event | category | flops | bytes accessed | tf_op | source)
XLA Modules:
  0.0 456.5 jit_solution(12711647150554493388)
XLA Ops:
  9.4 1.4 convert_element_type.183.refs_0_
  11.4 1.6 collective-permute-start.1
  13.1 5.6 %collective-permute-done.1 = bf16[48,2304]{1,0:T(8,128)(2,1)S(1)} collective-permute-done((bf16[48,2304]{1,0:T(8,128)(2,1)S(1)}, bf16[48,2304]{1,0:T(8,128)(2,1)S(1)}, u32[]{:S(2)}, u32[]{:S(2)}) %collective-permute-start.1) | collective-permute-done | bytes 221216 | tf_op jit(solution)/shard_map/ppermute | solution.py:231
  19.4 1.9 collective-permute-start.3
  21.4 2.4 collective-permute-start.2
  23.8 1.6 collective-permute-start
  25.4 16.0 %collective-permute-done.refs_1_ = bf16[9,48,768]{2,1,0:T(8,128)(2,1)S(1)} collective-permute-done((bf16[9,48,768]{2,1,0:T(8,128)(2,1)S(1)}, bf16[9,48,768]{2,1,0:T(8,128)(2,1)S(1)}, u32[]{:S(2)}, u32[]{:S(2)}) %collective-permute-start) | collective-permute-done | bytes 663584 | tf_op jit(solution)/shard_map/ppermute | solution.py:231
  41.5 1.8 pick_units.2
  43.3 26.8 %collective-permute-done.2 = bf16[2,512,768]{2,1,0:T(8,128)(2,1)} collective-permute-done((bf16[2,512,768]{2,1,0:T(8,128)(2,1)S(1)}, bf16[2,512,768]{2,1,0:T(8,128)(2,1)}, u32[]{:S(2)}, u32[]{:S(2)}) %collective-permute-start.2) | collective-permute-done | bytes 1572896 | tf_op jit(solution)/shard_map/ppermute | solution.py:226
  70.1 6.8 %all-gather.3.cloned.1.call-done.w_ref = bf16[768,2304]{1,0:T(8,128)(2,1)} async-done(((bf16[48,2304]{1,0:T(8,128)(2,1)}), bf16[768,2304]{1,0:T(8,128)(2,1)}) %all-gather.3.cloned.1.call-update) | async-done | bytes 3538960 | tf_op jit(solution)/shard_map/all_gather | solution.py:669
  77.1 1.4 convert_reduce_fusion
  78.5 4.4 fusion.1
  82.9 1.7 copy.35
  84.6 5.0 %pad_maximum_fusion = bf16[2,1536,768]{2,1,0:T(8,128)(2,1)} fusion(bf16[2,512,768]{2,1,0:T(8,128)(2,1)} %collective-permute-done.3, bf16[2,512,768]{2,1,0:T(8,128)(2,1)} %param.12, bf16[2,512,768]{2,1,0:T(8,128)(2,1)} %collective-permute-done.2), kind=kLoop, calls=%fused_computation.3 | loop fusion | flops 14155776 | bytes 9437184 | tf_op jit(solution)/shard_map/concatenate | solution.py:683
  89.6 6.8 %copy.41 = bf16[3072,768]{0,1:T(8,128)(2,1)} copy(bf16[3072,768]{1,0:T(8,128)(2,1)} %bitcast.72) | data formatting | bytes 9437184 | tf_op jit(solution)/shard_map/reshape | solution.py:691
  96.3 3.0 dynamic-slice_bitcast_fusion.1
  99.4 2.8 pad_maximum_fusion.1
  103.3 9.7 %convolution_convert_fusion = bf16[3072,1536]{1,0:T(8,128)(2,1)} fusion(bf16[3072,768]{1,0:T(8,128)(2,1)S(1)} %bitcast.75, bf16[768,2304]{1,0:T(8,128)(2,1)S(1)} %copy-done.6), kind=kOutput, calls=%fused_computation | convolution fusion | flops 7252475904 | bytes 16515072 | tf_op jit(solution)/shard_map/dot_general | solution.py:25
  113.0 3.9 copy-done.9
  116.8 47.9 %attend_fwd.1 = (bf16[2,512,768]{2,1,0:T(8,128)(2,1)S(1)}, f32[2,6,2,512]{3,2,1,0:T(2,128)S(1)}, f32[12,8,256]{2,1,0:T(8,128)S(1)}) custom-call(s32[12]{0:T(128)S(1)} %copy-done.8, f32[12]{0:T(128)S(1)} %power_multiply_fusion.slope_ref, bf16[2,512,768]{2,1,0:T(8,128)(2,1)S(1)} %bitcast.60, bf16[2,1536,1536]{2,1,0:T(8,128)(2,1)S(1)} %bitcast.64, ...), custom_call_target="tpu_custom_call" | custom-call | flops 20000000000 | bytes 10000000 | tf_op jit(solution)/shard_map/attend_fwd/pallas_call | solution.py:106
  165.9 2.7 all-gather.5.cloned.1.call-done.wo_ref.wg_ref.wu_ref.wd_ref
  168.6 75.3 %feed_forward.1 = (bf16[1024,768]{1,0:T(8,128)(2,1)}, f32[1024,768]{1,0:T(8,128)}, bf16[1024,768]{1,0:T(8,128)(2,1)}, f32[8,768]{1,0:T(8,128)}, bf16[768,9984]{1,0:T(8,128)(2,1)}) custom-call(bf16[1024,768]{1,0:T(8,128)(2,1)} %bitcast.70, bf16[1024,768]{1,0:T(8,128)(2,1)} %bitcast.82, bf16[1024,768]{1,0:T(8,128)(2,1)} %bitcast.86, ...), custom_call_target="tpu_custom_call" | custom-call | flops 46000001024 | bytes 60000000 | tf_op jit(solution)/shard_map/feed_forward/pallas_call | solution.py:509
  244.2 1.4 copy-done.17
  245.6 1.4 copy-done.18
  247.0 65.3 %attend_bwd.1 = (bf16[2,512,768]{2,1,0:T(8,128)(2,1)S(1)}, bf16[2,1536,768]{2,1,0:T(8,128)(2,1)S(1)}, bf16[2,1536,768]{2,1,0:T(8,128)(2,1)}) custom-call(s32[12]{0:T(128)S(1)} %copy-done.8, f32[12]{0:T(128)S(1)} %power_multiply_fusion.slope_ref, bf16[2,512,768]{2,1,0:T(8,128)(2,1)S(1)} %bitcast.61, bf16[2,1536,1536]{2,1,0:T(8,128)(2,1)} %bitcast.62, ...), custom_call_target="tpu_custom_call" | custom-call | flops 49999998976 | bytes 20000000 | tf_op jit(solution)/shard_map/attend_bwd/pallas_call | solution.py:201
  312.4 4.6 %copy-done.12 = bf16[2,1536,768]{2,1,0:T(8,128)(2,1)S(1)} copy-done((bf16[2,1536,768]{2,1,0:T(8,128)(2,1)S(1)}, bf16[2,1536,768]{2,1,0:T(8,128)(2,1)}, u32[]{:S(2)}) %copy-start.12) | copy-done | bytes 4718616
  317.0 11.8 %first_gradients.1 = bf16[768,2304]{1,0:T(8,128)(2,1)S(1)} custom-call(bf16[768,3072]{1,0:T(8,128)(2,1)S(1)} %bitcast.59, bf16[1024,768]{1,0:T(8,128)(2,1)S(1)} %bitcast.69, bf16[3072,768]{1,0:T(8,128)(2,1)S(1)} %bitcast.66, bf16[3072,768]{1,0:T(8,128)(2,1)S(1)} %bitcast.67), custom_call_target="tpu_custom_call" | custom-call | flops 8999999488 | bytes 20000000 | tf_op jit(solution)/shard_map/first_gradients/pallas_call | solution.py:577
  330.7 3.7 collective-permute-done.4
  335.3 2.7 add_convert_fusion
  338.1 1.5 collective-permute-start.5
  340.2 1.9 copy-done.13
  342.1 1.5 copy-done.15
  343.6 11.7 %input_parts.1 = (f32[2,512,768]{2,1,0:T(8,128)S(1)}, bf16[2,2,512,768]{3,2,1,0:T(8,128)(2,1)S(1)}) custom-call(f32[2,512,768]{2,1,0:T(8,128)S(1)} %bitcast.68, bf16[2,512,768]{2,1,0:T(8,128)(2,1)S(1)} %copy-done.15, bf16[2,1536,768]{2,1,0:T(8,128)(2,1)S(1)} %copy-done.11, bf16[2,1536,768]{2,1,0:T(8,128)(2,1)} %get-tuple-element.54.v_ref, ...), custom_call_target="tpu_custom_call" | custom-call | flops 8999999488 | bytes 20000000 | tf_op jit(solution)/shard_map/input_parts/pallas_call | solution.py:613
  355.3 5.6 %collective-permute-done.5 = bf16[400,1152]{1,0:T(8,128)(2,1)S(1)} collective-permute-done((bf16[400,1152]{1,0:T(8,128)(2,1)S(1)}, bf16[400,1152]{1,0:T(8,128)(2,1)S(1)}, u32[]{:S(2)}, u32[]{:S(2)}) %collective-permute-start.5) | collective-permute-done | bytes 921632 | tf_op jit(solution)/shard_map/ppermute | solution.py:231
  363.3 20.7 %collective-permute-done.6 = bf16[208,1152]{1,0:T(8,128)(2,1)S(1)} collective-permute-done((bf16[208,1152]{1,0:T(8,128)(2,1)S(1)}, bf16[208,1152]{1,0:T(8,128)(2,1)S(1)}, u32[]{:S(2)}, u32[]{:S(2)}) %collective-permute-start.6) | collective-permute-done | bytes 479264 | tf_op jit(solution)/shard_map/ppermute | solution.py:231
  386.8 1.9 collective-permute-start.8
  388.7 2.4 collective-permute-start.9
  391.3 12.2 %collective-permute-done.7 = bf16[112,1152]{1,0:T(8,128)(2,1)S(1)} collective-permute-done((bf16[112,1152]{1,0:T(8,128)(2,1)S(1)}, bf16[112,1152]{1,0:T(8,128)(2,1)S(1)}, u32[]{:S(2)}, u32[]{:S(2)}) %collective-permute-start.7) | collective-permute-done | bytes 258080 | tf_op jit(solution)/shard_map/ppermute | solution.py:231
  403.6 4.0 reduce-scatter.2.cloned.1.call-done.col_ref
  408.9 1.5 to_slots.3
  410.4 1.9 collective-permute-start.11
  412.2 15.4 %collective-permute-done.9 = bf16[2,512,768]{2,1,0:T(8,128)(2,1)} collective-permute-done((bf16[2,512,768]{2,1,0:T(8,128)(2,1)}, bf16[2,512,768]{2,1,0:T(8,128)(2,1)}, u32[]{:S(2)}, u32[]{:S(2)}) %collective-permute-start.9) | collective-permute-done | bytes 1572896 | tf_op jit(solution)/shard_map/ppermute | solution.py:226
  427.7 1.3 collective-permute-start.10
  429.0 4.0 convert_add_fusion
  433.6 1.7 collective-permute-done.10
  436.1 1.5 collective-permute-start.12
  438.9 2.2 collective-permute-done.12
  442.8 7.0 %adam_slots.1 = (f32[9,48,768]{2,1,0:T(8,128)}, f32[9,48,768]{2,1,0:T(8,128)}, f32[9,48,768]{2,1,0:T(8,128)}, f32[9,48,768]{2,1,0:T(8,128)}, bf16[9,48,768]{2,1,0:T(8,128)(2,1)}) custom-call(s32[9]{0:T(128)S(1)} %get-tuple-element.79.unit_ref, f32[9,48,768]{2,1,0:T(8,128)S(1)} %copy-done, f32[9,48,768]{2,1,0:T(8,128)S(1)} %copy-done.4, ...), custom_call_target="tpu_custom_call" | custom-call | tf_op jit(solution)/shard_map/adam_slots/pallas_call | solution.py:351
  (143 shorter events, 21.0 us)
Async XLA Ops:
  7.2 5.8 %copy-start.27 = (s32[16]{0:T(128)S(1)}, s32[16]{0:T(128)}, u32[]{:S(2)}) copy-start(s32[16]{0:T(128)} %param.16) | copy-start | bytes 196
  7.2 12.2 %copy-start.19 = (bf16[2,512,768]{2,1,0:T(8,128)(2,1)S(1)}, bf16[2,512,768]{2,1,0:T(8,128)(2,1)}, u32[]{:S(2)}) copy-start(bf16[2,512,768]{2,1,0:T(8,128)(2,1)} %param.12) | copy-start | bytes 4718596
  7.2 69.7 %all-gather.3.cloned.1.call-start = ((), (), s32[]{:S(2)}) async-start(), calls=%async_computation.1 | async-start | bytes 3760128 | tf_op jit(solution)/shard_map/all_gather | solution.py:669
  11.4 65.6 %copy-start.22 = (s32[2,8192]{1,0:T(2,128)S(1)}, s32[2,8192]{1,0:T(2,128)}, u32[]{:S(2)}) copy-start(s32[2,8192]{1,0:T(2,128)} %param.14) | copy-start | bytes 196612
  11.4 7.2 %collective-permute-start.1 = (bf16[48,2304]{1,0:T(8,128)(2,1)S(1)}, bf16[48,2304]{1,0:T(8,128)(2,1)S(1)}, u32[]{:S(2)}, u32[]{:S(2)}) collective-permute-start(bf16[48,2304]{1,0:T(8,128)(2,1)S(1)} %pick_units.3), channel_id=1, source_target_pairs={{0,1},{1,0},{2,3},{3,2},{4,5},{5,4},{6,7},{7,6},{8,9},{9,8},{10,11... | collective-permute-start | bytes 663560 | tf_op jit(solution)/shard_map/ppermute | solution.py:231
  19.4 149.2 %all-gather.5.cloned.1.call-start = ((), (), s32[]{:S(2)}) async-start(), calls=%async_computation.2 | async-start | bytes 17965056 | tf_op jit(solution)/shard_map/all_gather | solution.py:672
  19.4 23.8 %collective-permute-start.3 = (bf16[2,512,768]{2,1,0:T(8,128)(2,1)S(1)}, bf16[2,512,768]{2,1,0:T(8,128)(2,1)}, u32[]{:S(2)}, u32[]{:S(2)}) collective-permute-start(bf16[2,512,768]{2,1,0:T(8,128)(2,1)S(1)} %copy-done.19), channel_id=1, source_target_pairs={{2,0},{4,2},{6,4},{8,6},{10,8},{12,10},{14,12},{16,14},{18,16},{20... | collective-permute-start | bytes 4718600 | tf_op jit(solution)/shard_map/ppermute | solution.py:226
  21.4 48.7 %collective-permute-start.2 = (bf16[2,512,768]{2,1,0:T(8,128)(2,1)S(1)}, bf16[2,512,768]{2,1,0:T(8,128)(2,1)}, u32[]{:S(2)}, u32[]{:S(2)}) collective-permute-start(bf16[2,512,768]{2,1,0:T(8,128)(2,1)S(1)} %copy-done.19), channel_id=1, source_target_pairs={{0,2},{2,4},{4,6},{6,8},{8,10},{10,12},{12,14},{14,16},{16,18},{18... | collective-permute-start | bytes 4718600 | tf_op jit(solution)/shard_map/ppermute | solution.py:226
  23.8 17.7 %collective-permute-start = (bf16[9,48,768]{2,1,0:T(8,128)(2,1)S(1)}, bf16[9,48,768]{2,1,0:T(8,128)(2,1)S(1)}, u32[]{:S(2)}, u32[]{:S(2)}) collective-permute-start(bf16[9,48,768]{2,1,0:T(8,128)(2,1)S(1)} %convert_element_type.183.refs_0_), channel_id=1, source_target_pairs={{0,1},{1,0},{2,3},{3,2},{4,5},{5,4},{6,7},{7,6},{8,9},{9,8},{10,11... | collective-permute-start | bytes 1990664 | tf_op jit(solution)/shard_map/ppermute | solution.py:231
  76.9 330.7 %reduce-scatter.2.cloned.1.call-start = ((), (), s32[]{:S(2)}) async-start(), calls=%async_computation.3 | async-start | bytes 16293888 | tf_op jit(solution)/shard_map/reduce_scatter | solution.py:701
  89.6 12.6 %slice-start.2 = ((s8[4718592]{0:T(1024)(128)(4,1)}), s8[524288]{0:T(1024)(128)(4,1)S(1)}, s32[]{:S(2)}) async-start(s8[4718592]{0:T(1024)(128)(4,1)} %bitcast.73), calls=%async_computation.6 | async-start | bytes 1048576
  96.3 5.8 %slice-start.3 = ((s8[4718592]{0:T(1024)(128)(4,1)}), s8[4194304]{0:T(1024)(128)(4,1)S(1)}, s32[]{:S(2)}) async-start(s8[4718592]{0:T(1024)(128)(4,1)} %bitcast.73), calls=%async_computation.7 | async-start | bytes 8388608
  99.4 3.9 copy-start.6
  103.3 9.7 %copy-start.8 = (s32[12]{0:T(128)S(1)}, s32[12]{0:T(128)}, u32[]{:S(2)}) copy-start(s32[12]{0:T(128)} %win_ref.3) | copy-start | bytes 148
  113.0 3.9 copy-start.9
  164.7 1.2 copy-start.16
  244.0 68.4 %slice-start = ((s8[4718592]{0:T(1024)(128)(4,1)}), s8[524288]{0:T(1024)(128)(4,1)S(1)}, s32[]{:S(2)}) async-start(s8[4718592]{0:T(1024)(128)(4,1)} %bitcast.57), calls=%async_computation.4 | async-start | bytes 1048576
  244.2 1.4 copy-start.17
  245.6 1.4 copy-start.18
  247.0 65.3 %slice-start.1 = ((s8[4718592]{0:T(1024)(128)(4,1)}), s8[4194304]{0:T(1024)(128)(4,1)S(1)}, s32[]{:S(2)}) async-start(s8[4718592]{0:T(1024)(128)(4,1)} %bitcast.57), calls=%async_computation.5 | async-start | bytes 8388608
  312.3 16.4 %copy-start.10 = (bf16[2,1536,768]{2,1,0:T(8,128)(2,1)}, bf16[2,1536,768]{2,1,0:T(8,128)(2,1)S(1)}, u32[]{:S(2)}) copy-start(bf16[2,1536,768]{2,1,0:T(8,128)(2,1)S(1)} %get-tuple-element.53.k_ref) | copy-start | bytes 14155780
  312.3 16.4 %copy-start.14 = (bf16[2,512,768]{2,1,0:T(8,128)(2,1)}, bf16[2,512,768]{2,1,0:T(8,128)(2,1)S(1)}, u32[]{:S(2)}) copy-start(bf16[2,512,768]{2,1,0:T(8,128)(2,1)S(1)} %get-tuple-element.52.q_ref) | copy-start | bytes 4718596
  312.3 4.6 %copy-start.12 = (bf16[2,1536,768]{2,1,0:T(8,128)(2,1)S(1)}, bf16[2,1536,768]{2,1,0:T(8,128)(2,1)}, u32[]{:S(2)}) copy-start(bf16[2,1536,768]{2,1,0:T(8,128)(2,1)} %get-tuple-element.54.v_ref) | copy-start | bytes 14155780
  328.8 1.7 copy-start.3
  330.5 3.9 collective-permute-start.4
  335.2 4.5 copy-start.11
  337.9 1.7 copy-start.28
  337.9 2.3 copy-start.7
  338.1 22.7 %collective-permute-start.5 = (bf16[400,1152]{1,0:T(8,128)(2,1)S(1)}, bf16[400,1152]{1,0:T(8,128)(2,1)S(1)}, u32[]{:S(2)}, u32[]{:S(2)}) collective-permute-start(bf16[400,1152]{1,0:T(8,128)(2,1)S(1)} %pad_maximum_fusion.3), channel_id=1, source_target_pairs={{0,1},{1,0},{2,3},{3,2},{4,5},{5,4},{6,7},{7,6},{8,9},{9,8},{10,11... | collective-permute-start | bytes 2764808 | tf_op jit(solution)/shard_map/ppermute | solution.py:231
  340.2 1.9 copy-start.13
  342.1 1.5 copy-start.15
  361.3 22.7 %collective-permute-start.6 = (bf16[208,1152]{1,0:T(8,128)(2,1)S(1)}, bf16[208,1152]{1,0:T(8,128)(2,1)S(1)}, u32[]{:S(2)}, u32[]{:S(2)}) collective-permute-start(bf16[208,1152]{1,0:T(8,128)(2,1)S(1)} %pad_maximum_fusion.4), channel_id=1, source_target_pairs={{0,4},{2,6},{4,0},{6,2},{8,12},{10,14},{12,8},{14,10},{16,20},{18,... | collective-permute-start | bytes 1437704 | tf_op jit(solution)/shard_map/ppermute | solution.py:231
  384.3 19.1 %collective-permute-start.7 = (bf16[112,1152]{1,0:T(8,128)(2,1)S(1)}, bf16[112,1152]{1,0:T(8,128)(2,1)S(1)}, u32[]{:S(2)}, u32[]{:S(2)}) collective-permute-start(bf16[112,1152]{1,0:T(8,128)(2,1)S(1)} %pad_maximum_fusion.5), channel_id=1, source_target_pairs={{0,8},{2,10},{4,12},{6,14},{8,0},{10,2},{12,4},{14,6},{16,24},{18,... | collective-permute-start | bytes 774152 | tf_op jit(solution)/shard_map/ppermute | solution.py:231
  386.8 25.5 %collective-permute-start.8 = (bf16[2,512,768]{2,1,0:T(8,128)(2,1)}, bf16[2,512,768]{2,1,0:T(8,128)(2,1)}, u32[]{:S(2)}, u32[]{:S(2)}) collective-permute-start(bf16[2,512,768]{2,1,0:T(8,128)(2,1)} %slice_bitcast_fusion), channel_id=1, source_target_pairs={{2,0},{4,2},{6,4},{8,6},{10,8},{12,10},{14,12},{16,14},{18,16},{20... | collective-permute-start | bytes 4718600 | tf_op jit(solution)/shard_map/ppermute | solution.py:226
  388.7 38.9 %collective-permute-start.9 = (bf16[2,512,768]{2,1,0:T(8,128)(2,1)}, bf16[2,512,768]{2,1,0:T(8,128)(2,1)}, u32[]{:S(2)}, u32[]{:S(2)}) collective-permute-start(bf16[2,512,768]{2,1,0:T(8,128)(2,1)} %slice_bitcast_fusion.1), channel_id=1, source_target_pairs={{0,2},{2,4},{4,6},{6,8},{8,10},{10,12},{12,14},{14,16},{16,18},{18... | collective-permute-start | bytes 4718600 | tf_op jit(solution)/shard_map/ppermute | solution.py:226
  403.5 8.7 %copy-start.20 = (f32[8,768]{1,0:T(8,128)}, f32[8,768]{1,0:T(8,128)S(1)}, u32[]{:S(2)}) copy-start(f32[8,768]{1,0:T(8,128)S(1)} %get-tuple-element.83) | copy-start | bytes 73732
  407.7 1.2 copy-start.1
  410.4 32.4 %collective-permute-start.11 = (bf16[9,48,768]{2,1,0:T(8,128)(2,1)}, bf16[9,48,768]{2,1,0:T(8,128)(2,1)}, u32[]{:S(2)}, u32[]{:S(2)}) collective-permute-start(bf16[9,48,768]{2,1,0:T(8,128)(2,1)} %to_slots.3), channel_id=1, source_target_pairs={{0,1},{1,0},{2,3},{3,2},{4,5},{5,4},{6,7},{7,6},{8,9},{9,8},{10,11... | collective-permute-start | bytes 1990664 | tf_op jit(solution)/shard_map/ppermute | solution.py:231
  427.6 5.3 %copy-start.2 = (bf16[48,9984]{1,0:T(8,128)(2,1)S(1)}, bf16[48,9984]{1,0:T(8,128)(2,1)}, u32[]{:S(2)}) copy-start(bf16[48,9984]{1,0:T(8,128)(2,1)} %reduce-scatter.2.cloned.1.call-done.col_ref) | copy-start | bytes 2875396
  427.6 7.7 %copy-start.21 = (f32[8,768]{1,0:T(8,128)S(1)}, f32[8,768]{1,0:T(8,128)}, u32[]{:S(2)}) copy-start(f32[8,768]{1,0:T(8,128)} %copy-done.20) | copy-start | bytes 73732
  427.7 10.0 %copy-start.24 = (f32[4,768]{1,0:T(4,128)S(1)}, f32[4,768]{1,0:T(4,128)}, u32[]{:S(2)}) copy-start(f32[4,768]{1,0:T(4,128)} %norm_ref.1) | copy-start | bytes 36868
  427.7 10.0 %copy-start.25 = (f32[4,768]{1,0:T(4,128)S(1)}, f32[4,768]{1,0:T(4,128)}, u32[]{:S(2)}) copy-start(f32[4,768]{1,0:T(4,128)} %param.21) | copy-start | bytes 36868
  427.7 9.9 %copy-start.26 = (f32[4,768]{1,0:T(4,128)S(1)}, f32[4,768]{1,0:T(4,128)}, u32[]{:S(2)}) copy-start(f32[4,768]{1,0:T(4,128)} %param.22) | copy-start | bytes 36868
  427.7 7.7 %collective-permute-start.10 = (bf16[64,1152]{1,0:T(8,128)(2,1)S(1)}, bf16[64,1152]{1,0:T(8,128)(2,1)S(1)}, u32[]{:S(2)}, u32[]{:S(2)}) collective-permute-start(bf16[64,1152]{1,0:T(8,128)(2,1)S(1)} %pad_maximum_fusion.7), channel_id=1, source_target_pairs={{0,16},{2,18},{4,20},{6,22},{8,24},{10,26},{12,28},{14,30},{16,0},... | collective-permute-start | bytes 442376 | tf_op jit(solution)/shard_map/ppermute | solution.py:231
  432.9 9.8 %copy-start = (f32[9,48,768]{2,1,0:T(8,128)S(1)}, f32[9,48,768]{2,1,0:T(8,128)}, u32[]{:S(2)}) copy-start(f32[9,48,768]{2,1,0:T(8,128)} %w_ref.1) | copy-start | bytes 3981316
  432.9 9.8 %copy-start.4 = (f32[9,48,768]{2,1,0:T(8,128)S(1)}, f32[9,48,768]{2,1,0:T(8,128)}, u32[]{:S(2)}) copy-start(f32[9,48,768]{2,1,0:T(8,128)} %m_ref.1) | copy-start | bytes 3981316
  436.1 5.0 %collective-permute-start.12 = (bf16[48,1152]{1,0:T(8,128)(2,1)}, bf16[48,1152]{1,0:T(8,128)(2,1)S(1)}, u32[]{:S(2)}, u32[]{:S(2)}) collective-permute-start(bf16[48,1152]{1,0:T(8,128)(2,1)} %fusion.5), channel_id=1, source_target_pairs={{0,1},{1,0},{2,3},{3,2},{4,5},{5,4},{6,7},{7,6},{8,9},{9,8},{10,11... | collective-permute-start | bytes 331784 | tf_op jit(solution)/shard_map/ppermute | solution.py:231
  438.9 3.8 copy-start.5
  (1 other events, 0.8 us)
Sparse Core Ops, SparseCore 0:
  19.5 57.3 all-gather.2
  79.1 89.4 all-gather.4
  244.1 163.5 reduce-scatter.1

commit v5 on v4

--- a/solution.py
+++ b/solution.py
@@ -733,14 +733,12 @@
     arrived = []
     while bit < lax.axis_size("ctx"):
         if 2 * bit == lax.axis_size("ctx"):
-            value, arrived, _ = lax.optimization_barrier((value, arrived, give))
+            value, _ = lax.optimization_barrier((value, give))
         small, value = halve(small, value.reshape((-1, 2) + value.shape[1:]), "ctx", bit)
         if bit == 2:
             for n in range(pieces):
                 arrived += [shifted(rim[:, n], "ctx", n - pieces), shifted(rim[:, pieces + n], "ctx", n + 1)]
         bit *= 2
-    for piece in arrived:
-        input_grad = input_grad + piece.astype(f32)
     first_sums = value[0]
     bit = 1
     while owner_count != 2 and bit < owner_count:
@@ -754,6 +752,7 @@
 
     if owner_count == 2:
         other = swapped(first_sums, "seq", 1)
+        other, arrived = lax.optimization_barrier((other, arrived))
         whole = jnp.concatenate([jnp.where(me == 0, first_sums, other), jnp.where(me == 0, other, first_sums)], axis=1)
         parts = [keep, swapped(give, "seq", 1), to_slots(jnp.where(my_units < 3, my_units, -1), whole, slots, width)]
     else:
@@ -762,6 +761,8 @@
     weight_grads, new_weights, new_first, new_second, weights_low = adam_slots(
         my_units, weights, first_moments, second_moments, parts, column_scale, correction, 0.5 / D**0.5
     )
+    for piece in arrived:
+        input_grad = input_grad + piece.astype(f32)
     new_norms, new_norm_first, new_norm_second = adam_step(
         norm_params, norm_grads, norm_first, norm_second, correction, norm_rate
     )

time: 464 us -> 464 us (level)
  the two profiles are of different devices: /device:TPU:4 before, /device:TPU:0 now
where the time goes in v5:
time: 464 us; the launch traced here: 458 us
  Pallas kernels  217 us (47%)
  waiting for transfers between devices  124 us (27%)
  local copies, waits for them, and re-layouts  36.6 us (8%)
  other arithmetic  26.9 us (6%)
  starting transfers between devices  25.3 us (5%)
  between operations  14.6 us (3%)
  matrix products  14 us (3%)
    ppermute x9, waiting for transfers between devices, swapped(): return lax.ppermute(value, axis, [(i, i ^ bit) for i in range(peers)])  84.8 us
    pallas_call x1, Pallas kernels, feed_forward(): pl.pallas_call(ffn_kernel, grid=(2 * chunks,), in_specs=[full, full, full...  75.3 us
    pallas_call x1, Pallas kernels, attend_bwd(): pl.pallas_call(bwd_kernel, grid=(pairs, seqs), in_specs=[smem, smem, tok,...  62.5 us
    pallas_call x1, Pallas kernels, attend_fwd(): pl.pallas_call(fwd_kernel, grid=(pairs, seqs), in_specs=[smem, smem, pl.B...  46 us
    all_gather x1, waiting for transfers between devices, on_device(): w_first = lax.all_gather(picked_first, 'ctx', axis=0, tiled=True)  34.5 us
    unnamed x66, local copies, waits for them, and re-layouts  20 us
    ppermute x9, starting transfers between devices, swapped(): return lax.ppermute(value, axis, [(i, i ^ bit) for i in range(peers)])  15.8 us
    dot_general x2, matrix products, dot_nn(): lax.dot_general(a, b, (((1,), (0,)), ((), ())), preferred_element_type=f32)  14 us
  transfers between devices with their start and end apart: 16, of which 10 were waited for; matrix products, arithmetic and copies ran while one was open for 12% of the time, Pallas kernels for 30%

profile of v5, /device:TPU:0, one launch (start us, length us, event | category | flops | bytes accessed | tf_op | source)
XLA Modules:
  0.0 458.4 jit_solution(13891633135184906477)
XLA Ops:
  9.4 1.4 convert_element_type.183.refs_0_
  11.4 3.0 collective-permute-start.1
  14.5 5.3 %collective-permute-done.1 = bf16[48,2304]{1,0:T(8,128)(2,1)S(1)} collective-permute-done((bf16[48,2304]{1,0:T(8,128)(2,1)S(1)}, bf16[48,2304]{1,0:T(8,128)(2,1)S(1)}, u32[]{:S(2)}, u32[]{:S(2)}) %collective-permute-start.1) | collective-permute-done | bytes 221216 | tf_op jit(solution)/shard_map/ppermute | solution.py:231
  20.6 1.3 collective-permute-start.3
  21.9 4.3 collective-permute-start.2
  26.2 1.7 collective-permute-start
  28.0 15.2 %collective-permute-done.refs_1_ = bf16[9,48,768]{2,1,0:T(8,128)(2,1)S(1)} collective-permute-done((bf16[9,48,768]{2,1,0:T(8,128)(2,1)S(1)}, bf16[9,48,768]{2,1,0:T(8,128)(2,1)S(1)}, u32[]{:S(2)}, u32[]{:S(2)}) %collective-permute-start) | collective-permute-done | bytes 663584 | tf_op jit(solution)/shard_map/ppermute | solution.py:231
  43.3 1.8 pick_units.2
  45.1 34.5 %all-gather.3.cloned.1.call-done.w_ref = bf16[768,2304]{1,0:T(8,128)(2,1)} async-done(((bf16[48,2304]{1,0:T(8,128)(2,1)}), bf16[768,2304]{1,0:T(8,128)(2,1)}) %all-gather.3.cloned.1.call-update) | async-done | bytes 3538960 | tf_op jit(solution)/shard_map/all_gather | solution.py:669
  79.7 1.4 convert_reduce_fusion
  81.2 4.4 fusion.1
  85.5 1.7 copy.35
  87.3 4.1 pad_maximum_fusion
  91.3 6.7 %copy.41 = bf16[3072,768]{0,1:T(8,128)(2,1)} copy(bf16[3072,768]{1,0:T(8,128)(2,1)} %bitcast.72) | data formatting | bytes 9437184 | tf_op jit(solution)/shard_map/reshape | solution.py:691
  98.0 3.1 dynamic-slice_bitcast_fusion.1
  101.2 2.8 pad_maximum_fusion.1
  105.1 9.7 %convolution_convert_fusion = bf16[3072,1536]{1,0:T(8,128)(2,1)} fusion(bf16[3072,768]{1,0:T(8,128)(2,1)S(1)} %bitcast.75, bf16[768,2304]{1,0:T(8,128)(2,1)S(1)} %copy-done.7), kind=kOutput, calls=%fused_computation | convolution fusion | flops 7252475904 | bytes 16515072 | tf_op jit(solution)/shard_map/dot_general | solution.py:25
  114.8 3.9 copy-done.10
  118.7 46.0 %attend_fwd.1 = (bf16[2,512,768]{2,1,0:T(8,128)(2,1)S(1)}, f32[2,6,2,512]{3,2,1,0:T(2,128)S(1)}, f32[12,8,256]{2,1,0:T(8,128)S(1)}) custom-call(s32[12]{0:T(128)S(1)} %copy-done.9, f32[12]{0:T(128)S(1)} %power_multiply_fusion.slope_ref, bf16[2,512,768]{2,1,0:T(8,128)(2,1)S(1)} %bitcast.60, bf16[2,1536,1536]{2,1,0:T(8,128)(2,1)S(1)} %bitcast.64, ...), custom_call_target="tpu_custom_call" | custom-call | flops 20000000000 | bytes 10000000 | tf_op jit(solution)/shard_map/attend_fwd/pallas_call | solution.py:106
  165.9 4.4 all-gather.5.cloned.1.call-done.wo_ref.wg_ref.wu_ref.wd_ref
  170.3 75.3 %feed_forward.1 = (bf16[1024,768]{1,0:T(8,128)(2,1)}, f32[1024,768]{1,0:T(8,128)}, bf16[1024,768]{1,0:T(8,128)(2,1)}, f32[8,768]{1,0:T(8,128)}, bf16[768,9984]{1,0:T(8,128)(2,1)}) custom-call(bf16[1024,768]{1,0:T(8,128)(2,1)} %bitcast.70, bf16[1024,768]{1,0:T(8,128)(2,1)} %bitcast.82, bf16[1024,768]{1,0:T(8,128)(2,1)} %bitcast.86, ...), custom_call_target="tpu_custom_call" | custom-call | flops 46000001024 | bytes 60000000 | tf_op jit(solution)/shard_map/feed_forward/pallas_call | solution.py:509
  245.8 1.4 copy-done.18
  247.3 1.4 copy-done.19
  248.7 62.5 %attend_bwd.1 = (bf16[2,512,768]{2,1,0:T(8,128)(2,1)S(1)}, bf16[2,1536,768]{2,1,0:T(8,128)(2,1)S(1)}, bf16[2,1536,768]{2,1,0:T(8,128)(2,1)}) custom-call(s32[12]{0:T(128)S(1)} %copy-done.9, f32[12]{0:T(128)S(1)} %power_multiply_fusion.slope_ref, bf16[2,512,768]{2,1,0:T(8,128)(2,1)S(1)} %bitcast.61, bf16[2,1536,1536]{2,1,0:T(8,128)(2,1)} %bitcast.62, ...), custom_call_target="tpu_custom_call" | custom-call | flops 49999998976 | bytes 20000000 | tf_op jit(solution)/shard_map/attend_bwd/pallas_call | solution.py:201
  311.2 4.6 copy-done.13
  315.8 11.8 %first_gradients.1 = bf16[768,2304]{1,0:T(8,128)(2,1)S(1)} custom-call(bf16[768,3072]{1,0:T(8,128)(2,1)S(1)} %bitcast.59, bf16[1024,768]{1,0:T(8,128)(2,1)S(1)} %bitcast.69, bf16[3072,768]{1,0:T(8,128)(2,1)S(1)} %bitcast.66, bf16[3072,768]{1,0:T(8,128)(2,1)S(1)} %bitcast.67), custom_call_target="tpu_custom_call" | custom-call | flops 8999999488 | bytes 20000000 | tf_op jit(solution)/shard_map/first_gradients/pallas_call | solution.py:577
  329.5 3.7 collective-permute-done.4
  334.0 2.6 add_convert_fusion
  336.8 1.5 collective-permute-start.5
  338.8 1.9 copy-done.14
  340.8 1.4 copy-done.16
  342.2 11.7 %input_parts.1 = (f32[2,512,768]{2,1,0:T(8,128)S(1)}, bf16[2,2,512,768]{3,2,1,0:T(8,128)(2,1)S(1)}) custom-call(f32[2,512,768]{2,1,0:T(8,128)S(1)} %bitcast.68, bf16[2,512,768]{2,1,0:T(8,128)(2,1)S(1)} %copy-done.16, bf16[2,1536,768]{2,1,0:T(8,128)(2,1)S(1)} %copy-done.12, bf16[2,1536,768]{2,1,0:T(8,128)(2,1)} %get-tuple-element.55.v_ref, ...), custom_call_target="tpu_custom_call" | custom-call | flops 8999999488 | bytes 20000000 | tf_op jit(solution)/shard_map/input_parts/pallas_call | solution.py:613
  353.8 5.6 %collective-permute-done.5 = bf16[400,1152]{1,0:T(8,128)(2,1)S(1)} collective-permute-done((bf16[400,1152]{1,0:T(8,128)(2,1)S(1)}, bf16[400,1152]{1,0:T(8,128)(2,1)S(1)}, u32[]{:S(2)}, u32[]{:S(2)}) %collective-permute-start.5) | collective-permute-done | bytes 921632 | tf_op jit(solution)/shard_map/ppermute | solution.py:231
  361.5 1.3 collective-permute-start.6
  362.8 1.2 slice_bitcast_fusion
  364.1 1.3 collective-permute-start.10
  365.4 19.7 %collective-permute-done.6 = bf16[208,1152]{1,0:T(8,128)(2,1)} collective-permute-done((bf16[208,1152]{1,0:T(8,128)(2,1)}, bf16[208,1152]{1,0:T(8,128)(2,1)}, u32[]{:S(2)}, u32[]{:S(2)}) %collective-permute-start.6) | collective-permute-done | bytes 479264 | tf_op jit(solution)/shard_map/ppermute | solution.py:231
  387.2 2.4 collective-permute-start.7
  389.6 1.3 slice_bitcast_fusion.1
  390.9 2.5 collective-permute-start.11
  393.3 27.2 %collective-permute-done.7 = bf16[112,1152]{1,0:T(8,128)(2,1)S(1)} collective-permute-done((bf16[112,1152]{1,0:T(8,128)(2,1)S(1)}, bf16[112,1152]{1,0:T(8,128)(2,1)S(1)}, u32[]{:S(2)}, u32[]{:S(2)}) %collective-permute-start.7) | collective-permute-done | bytes 258080 | tf_op jit(solution)/shard_map/ppermute | solution.py:231
  422.7 2.6 collective-permute-start.8
  425.4 1.5 collective-permute-start.12
  427.6 1.9 collective-permute-done.8
  430.4 1.5 collective-permute-start.9
  434.1 6.2 %collective-permute-done.9 = bf16[48,1152]{1,0:T(8,128)(2,1)S(1)} collective-permute-done((bf16[48,1152]{1,0:T(8,128)(2,1)S(1)}, bf16[48,1152]{1,0:T(8,128)(2,1)S(1)}, u32[]{:S(2)}, u32[]{:S(2)}) %collective-permute-start.9) | collective-permute-done | bytes 110624 | tf_op jit(solution)/shard_map/ppermute | solution.py:231
  441.1 5.1 %convert_add_fusion = f32[2,512,768]{2,1,0:T(8,128)} fusion(bf16[2,512,768]{2,1,0:T(8,128)(2,1)} %collective-permute-done.11, f32[2,512,768]{2,1,0:T(8,128)} %copy-done.4, bf16[2,512,768]{2,1,0:T(8,128)(2,1)} %collective-permute-done.10), kind=kLoop, calls=%fused_computation.6 | loop fusion | flops 3145728 | bytes 9437184 | tf_op jit(solution)/shard_map/add | solution.py:765
  446.1 5.5 %adam_slots.1 = (f32[9,48,768]{2,1,0:T(8,128)}, f32[9,48,768]{2,1,0:T(8,128)}, f32[9,48,768]{2,1,0:T(8,128)}, f32[9,48,768]{2,1,0:T(8,128)}, bf16[9,48,768]{2,1,0:T(8,128)(2,1)}) custom-call(s32[9]{0:T(128)S(1)} %get-tuple-element.81.unit_ref, f32[9,48,768]{2,1,0:T(8,128)S(1)} %copy-done, f32[9,48,768]{2,1,0:T(8,128)S(1)} %copy-done.5, ...), custom_call_target="tpu_custom_call" | custom-call | tf_op jit(solution)/shard_map/adam_slots/pallas_call | solution.py:351
  (143 shorter events, 20.7 us)
Async XLA Ops:
  7.2 7.2 %copy-start.27 = (s32[16]{0:T(128)S(1)}, s32[16]{0:T(128)}, u32[]{:S(2)}) copy-start(s32[16]{0:T(128)} %param.16) | copy-start | bytes 196
  7.2 13.4 %copy-start.21 = (bf16[2,512,768]{2,1,0:T(8,128)(2,1)S(1)}, bf16[2,512,768]{2,1,0:T(8,128)(2,1)}, u32[]{:S(2)}) copy-start(bf16[2,512,768]{2,1,0:T(8,128)(2,1)} %param.12) | copy-start | bytes 4718596
  7.2 72.4 %all-gather.3.cloned.1.call-start = ((), (), s32[]{:S(2)}) async-start(), calls=%async_computation.1 | async-start | bytes 3760128 | tf_op jit(solution)/shard_map/all_gather | solution.py:669
  11.4 68.3 %copy-start.22 = (s32[2,8192]{1,0:T(2,128)S(1)}, s32[2,8192]{1,0:T(2,128)}, u32[]{:S(2)}) copy-start(s32[2,8192]{1,0:T(2,128)} %param.14) | copy-start | bytes 196612
  11.4 8.4 %collective-permute-start.1 = (bf16[48,2304]{1,0:T(8,128)(2,1)S(1)}, bf16[48,2304]{1,0:T(8,128)(2,1)S(1)}, u32[]{:S(2)}, u32[]{:S(2)}) collective-permute-start(bf16[48,2304]{1,0:T(8,128)(2,1)S(1)} %pick_units.3), channel_id=1, source_target_pairs={{0,1},{1,0},{2,3},{3,2},{4,5},{5,4},{6,7},{7,6},{8,9},{9,8},{10,11... | collective-permute-start | bytes 663560 | tf_op jit(solution)/shard_map/ppermute | solution.py:231
  20.6 149.7 %all-gather.5.cloned.1.call-start = ((), (), s32[]{:S(2)}) async-start(), calls=%async_computation.2 | async-start | bytes 17965056 | tf_op jit(solution)/shard_map/all_gather | solution.py:672
  20.6 24.4 %collective-permute-start.3 = (bf16[2,512,768]{2,1,0:T(8,128)(2,1)S(1)}, bf16[2,512,768]{2,1,0:T(8,128)(2,1)}, u32[]{:S(2)}, u32[]{:S(2)}) collective-permute-start(bf16[2,512,768]{2,1,0:T(8,128)(2,1)S(1)} %copy-done.21), channel_id=1, source_target_pairs={{2,0},{4,2},{6,4},{8,6},{10,8},{12,10},{14,12},{16,14},{18,16},{20... | collective-permute-start | bytes 4718600 | tf_op jit(solution)/shard_map/ppermute | solution.py:226
  21.9 23.1 %collective-permute-start.2 = (bf16[2,512,768]{2,1,0:T(8,128)(2,1)S(1)}, bf16[2,512,768]{2,1,0:T(8,128)(2,1)}, u32[]{:S(2)}, u32[]{:S(2)}) collective-permute-start(bf16[2,512,768]{2,1,0:T(8,128)(2,1)S(1)} %copy-done.21), channel_id=1, source_target_pairs={{0,2},{2,4},{4,6},{6,8},{8,10},{10,12},{12,14},{14,16},{16,18},{18... | collective-permute-start | bytes 4718600 | tf_op jit(solution)/shard_map/ppermute | solution.py:226
  26.2 17.0 %collective-permute-start = (bf16[9,48,768]{2,1,0:T(8,128)(2,1)S(1)}, bf16[9,48,768]{2,1,0:T(8,128)(2,1)S(1)}, u32[]{:S(2)}, u32[]{:S(2)}) collective-permute-start(bf16[9,48,768]{2,1,0:T(8,128)(2,1)S(1)} %convert_element_type.183.refs_0_), channel_id=1, source_target_pairs={{0,1},{1,0},{2,3},{3,2},{4,5},{5,4},{6,7},{7,6},{8,9},{9,8},{10,11... | collective-permute-start | bytes 1990664 | tf_op jit(solution)/shard_map/ppermute | solution.py:231
  79.6 341.2 %reduce-scatter.2.cloned.1.call-start = ((), (), s32[]{:S(2)}) async-start(), calls=%async_computation.3 | async-start | bytes 16293888 | tf_op jit(solution)/shard_map/reduce_scatter | solution.py:701
  91.3 12.7 %slice-start.2 = ((s8[4718592]{0:T(1024)(128)(4,1)}), s8[524288]{0:T(1024)(128)(4,1)S(1)}, s32[]{:S(2)}) async-start(s8[4718592]{0:T(1024)(128)(4,1)} %bitcast.73), calls=%async_computation.6 | async-start | bytes 1048576
  98.0 6.0 %slice-start.3 = ((s8[4718592]{0:T(1024)(128)(4,1)}), s8[4194304]{0:T(1024)(128)(4,1)S(1)}, s32[]{:S(2)}) async-start(s8[4718592]{0:T(1024)(128)(4,1)} %bitcast.73), calls=%async_computation.7 | async-start | bytes 8388608
  101.2 4.0 copy-start.7
  105.1 9.7 %copy-start.9 = (s32[12]{0:T(128)S(1)}, s32[12]{0:T(128)}, u32[]{:S(2)}) copy-start(s32[12]{0:T(128)} %win_ref.3) | copy-start | bytes 148
  114.8 3.9 copy-start.10
  164.7 1.2 copy-start.17
  245.6 65.5 %slice-start = ((s8[4718592]{0:T(1024)(128)(4,1)}), s8[524288]{0:T(1024)(128)(4,1)S(1)}, s32[]{:S(2)}) async-start(s8[4718592]{0:T(1024)(128)(4,1)} %bitcast.57), calls=%async_computation.4 | async-start | bytes 1048576
  245.8 1.4 copy-start.18
  247.2 1.4 copy-start.19
  248.7 62.5 %slice-start.1 = ((s8[4718592]{0:T(1024)(128)(4,1)}), s8[4194304]{0:T(1024)(128)(4,1)S(1)}, s32[]{:S(2)}) async-start(s8[4718592]{0:T(1024)(128)(4,1)} %bitcast.57), calls=%async_computation.5 | async-start | bytes 8388608
  311.1 16.4 %copy-start.11 = (bf16[2,1536,768]{2,1,0:T(8,128)(2,1)}, bf16[2,1536,768]{2,1,0:T(8,128)(2,1)S(1)}, u32[]{:S(2)}) copy-start(bf16[2,1536,768]{2,1,0:T(8,128)(2,1)S(1)} %get-tuple-element.54.k_ref) | copy-start | bytes 14155780
  311.1 16.4 %copy-start.15 = (bf16[2,512,768]{2,1,0:T(8,128)(2,1)}, bf16[2,512,768]{2,1,0:T(8,128)(2,1)S(1)}, u32[]{:S(2)}) copy-start(bf16[2,512,768]{2,1,0:T(8,128)(2,1)S(1)} %get-tuple-element.53.q_ref) | copy-start | bytes 4718596
  311.2 4.6 %copy-start.13 = (bf16[2,1536,768]{2,1,0:T(8,128)(2,1)S(1)}, bf16[2,1536,768]{2,1,0:T(8,128)(2,1)}, u32[]{:S(2)}) copy-start(bf16[2,1536,768]{2,1,0:T(8,128)(2,1)} %get-tuple-element.55.v_ref) | copy-start | bytes 14155780
  327.5 1.7 copy-start.3
  329.3 3.9 collective-permute-start.4
  334.0 4.4 copy-start.12
  336.6 1.7 copy-start.28
  336.6 2.2 copy-start.8
  336.8 22.7 %collective-permute-start.5 = (bf16[400,1152]{1,0:T(8,128)(2,1)S(1)}, bf16[400,1152]{1,0:T(8,128)(2,1)S(1)}, u32[]{:S(2)}, u32[]{:S(2)}) collective-permute-start(bf16[400,1152]{1,0:T(8,128)(2,1)S(1)} %pad_maximum_fusion.3), channel_id=1, source_target_pairs={{0,1},{1,0},{2,3},{3,2},{4,5},{5,4},{6,7},{7,6},{8,9},{9,8},{10,11... | collective-permute-start | bytes 2764808 | tf_op jit(solution)/shard_map/ppermute | solution.py:231
  338.8 1.9 copy-start.14
  340.8 1.4 copy-start.16
  353.8 6.8 %copy-start.4 = (f32[2,512,768]{2,1,0:T(8,128)}, f32[2,512,768]{2,1,0:T(8,128)S(1)}, u32[]{:S(2)}) copy-start(f32[2,512,768]{2,1,0:T(8,128)S(1)} %get-tuple-element.61) | copy-start | bytes 9437188
  361.5 23.6 %collective-permute-start.6 = (bf16[208,1152]{1,0:T(8,128)(2,1)}, bf16[208,1152]{1,0:T(8,128)(2,1)}, u32[]{:S(2)}, u32[]{:S(2)}) collective-permute-start(bf16[208,1152]{1,0:T(8,128)(2,1)} %pad_maximum_fusion.4), channel_id=1, source_target_pairs={{0,4},{2,6},{4,0},{6,2},{8,12},{10,14},{12,8},{14,10},{16,20},{18,... | collective-permute-start | bytes 1437704 | tf_op jit(solution)/shard_map/ppermute | solution.py:231
  362.8 24.2 %copy-start.20 = (bf16[4,1,48,1152]{3,2,1,0:T(8,128)(2,1)S(1)}, bf16[4,1,48,1152]{3,2,1,0:T(8,128)(2,1)}, u32[]{:S(2)}) copy-start(bf16[4,1,48,1152]{3,2,1,0:T(8,128)(2,1)} %get-tuple-element.96) | copy-start | bytes 1327108
  364.1 70.0 %collective-permute-start.10 = (bf16[2,512,768]{2,1,0:T(8,128)(2,1)}, bf16[2,512,768]{2,1,0:T(8,128)(2,1)}, u32[]{:S(2)}, u32[]{:S(2)}) collective-permute-start(bf16[2,512,768]{2,1,0:T(8,128)(2,1)} %slice_bitcast_fusion), channel_id=1, source_target_pairs={{2,0},{4,2},{6,4},{8,6},{10,8},{12,10},{14,12},{16,14},{18,16},{20... | collective-permute-start | bytes 4718600 | tf_op jit(solution)/shard_map/ppermute | solution.py:226
  387.2 33.4 %collective-permute-start.7 = (bf16[112,1152]{1,0:T(8,128)(2,1)S(1)}, bf16[112,1152]{1,0:T(8,128)(2,1)S(1)}, u32[]{:S(2)}, u32[]{:S(2)}) collective-permute-start(bf16[112,1152]{1,0:T(8,128)(2,1)S(1)} %pad_maximum_fusion.5), channel_id=1, source_target_pairs={{0,8},{2,10},{4,12},{6,14},{8,0},{10,2},{12,4},{14,6},{16,24},{18,... | collective-permute-start | bytes 774152 | tf_op jit(solution)/shard_map/ppermute | solution.py:231
  390.9 43.2 %collective-permute-start.11 = (bf16[2,512,768]{2,1,0:T(8,128)(2,1)}, bf16[2,512,768]{2,1,0:T(8,128)(2,1)}, u32[]{:S(2)}, u32[]{:S(2)}) collective-permute-start(bf16[2,512,768]{2,1,0:T(8,128)(2,1)} %slice_bitcast_fusion.1), channel_id=1, source_target_pairs={{0,2},{2,4},{4,6},{6,8},{8,10},{10,12},{12,14},{14,16},{16,18},{18... | collective-permute-start | bytes 4718600 | tf_op jit(solution)/shard_map/ppermute | solution.py:226
  420.7 12.1 %copy-start.24 = (f32[4,768]{1,0:T(4,128)S(1)}, f32[4,768]{1,0:T(4,128)}, u32[]{:S(2)}) copy-start(f32[4,768]{1,0:T(4,128)} %norm_ref.1) | copy-start | bytes 36868
  420.7 12.1 %copy-start.25 = (f32[4,768]{1,0:T(4,128)S(1)}, f32[4,768]{1,0:T(4,128)}, u32[]{:S(2)}) copy-start(f32[4,768]{1,0:T(4,128)} %param.21) | copy-start | bytes 36868
  420.7 12.1 %copy-start.26 = (f32[4,768]{1,0:T(4,128)S(1)}, f32[4,768]{1,0:T(4,128)}, u32[]{:S(2)}) copy-start(f32[4,768]{1,0:T(4,128)} %param.22) | copy-start | bytes 36868
  420.8 1.2 copy-start.1
  422.0 4.9 %copy-start.2 = (bf16[48,9984]{1,0:T(8,128)(2,1)S(1)}, bf16[48,9984]{1,0:T(8,128)(2,1)}, u32[]{:S(2)}) copy-start(bf16[48,9984]{1,0:T(8,128)(2,1)} %reduce-scatter.2.cloned.1.call-done.col_ref) | copy-start | bytes 2875396
  422.7 6.8 %collective-permute-start.8 = (bf16[64,1152]{1,0:T(8,128)(2,1)S(1)}, bf16[64,1152]{1,0:T(8,128)(2,1)}, u32[]{:S(2)}, u32[]{:S(2)}) collective-permute-start(bf16[64,1152]{1,0:T(8,128)(2,1)S(1)} %pad_maximum_fusion.7), channel_id=1, source_target_pairs={{0,16},{2,18},{4,20},{6,22},{8,24},{10,26},{12,28},{14,30},{16,0},... | collective-permute-start | bytes 442376 | tf_op jit(solution)/shard_map/ppermute | solution.py:231
  425.4 20.7 %collective-permute-start.12 = (bf16[9,48,768]{2,1,0:T(8,128)(2,1)S(1)}, bf16[9,48,768]{2,1,0:T(8,128)(2,1)S(1)}, u32[]{:S(2)}, u32[]{:S(2)}) collective-permute-start(bf16[9,48,768]{2,1,0:T(8,128)(2,1)S(1)} %to_slots.3), channel_id=1, source_target_pairs={{0,1},{1,0},{2,3},{3,2},{4,5},{5,4},{6,7},{7,6},{8,9},{9,8},{10,11... | collective-permute-start | bytes 1990664 | tf_op jit(solution)/shard_map/ppermute | solution.py:231
  430.4 9.8 %collective-permute-start.9 = (bf16[48,1152]{1,0:T(8,128)(2,1)S(1)}, bf16[48,1152]{1,0:T(8,128)(2,1)S(1)}, u32[]{:S(2)}, u32[]{:S(2)}) collective-permute-start(bf16[48,1152]{1,0:T(8,128)(2,1)S(1)} %fusion.5), channel_id=1, source_target_pairs={{0,1},{1,0},{2,3},{3,2},{4,5},{5,4},{6,7},{7,6},{8,9},{9,8},{10,11... | collective-permute-start | bytes 331784 | tf_op jit(solution)/shard_map/ppermute | solution.py:231
  441.0 5.1 %copy-start = (f32[9,48,768]{2,1,0:T(8,128)S(1)}, f32[9,48,768]{2,1,0:T(8,128)}, u32[]{:S(2)}) copy-start(f32[9,48,768]{2,1,0:T(8,128)} %w_ref.1) | copy-start | bytes 3981316
  441.0 5.1 %copy-start.5 = (f32[9,48,768]{2,1,0:T(8,128)S(1)}, f32[9,48,768]{2,1,0:T(8,128)}, u32[]{:S(2)}) copy-start(f32[9,48,768]{2,1,0:T(8,128)} %m_ref.1) | copy-start | bytes 3981316
  441.0 5.1 %copy-start.6 = (f32[9,48,768]{2,1,0:T(8,128)S(1)}, f32[9,48,768]{2,1,0:T(8,128)}, u32[]{:S(2)}) copy-start(f32[9,48,768]{2,1,0:T(8,128)} %v_ref.1) | copy-start | bytes 3981316
  (1 other events, 0.8 us)
Sparse Core Ops, SparseCore 0:
  20.7 58.8 all-gather.2
  81.7 88.4 all-gather.4
  245.8 163.7 reduce-scatter.1
